TPU v7x, 32 devices: a whole 2x2x4 slice. The times are simulated.
32 devices in a mesh: dp: 16 (over z, y, x), mp: 2 (over core).
Axes of the slice: x: 2, y: 2, z: 4, core: 2. Of those that a mesh axis runs over, the one named last changes fastest.
Arguments:
- tokens: float32 [32768, 768], P('dp'), may hold values from -6 to 6
- latents: float32 [1024, 768], P('dp'), may hold values from -6 to 6
- condition: float32 [128, 768], P('dp'), may hold values from -6 to 6
- modulator: float32 [768, 4608], P('dp'), may hold values from -0.21875 to 0.21875
- offsets: float32 [4608], P('dp'), may hold values from -3 to 3
- local_qkv: float32 [768, 3, 768], P('dp', None, 'mp'), may hold values from -0.21875 to 0.21875
- local_out: float32 [768, 768], P('dp', 'mp'), may hold values from -0.875 to 0.875
- global_qkv: float32 [768, 3, 768], P('dp', None, 'mp'), may hold values from -0.21875 to 0.21875
- global_out: float32 [768, 768], P('dp', 'mp'), may hold values from -0.4375 to 0.4375
- latent_gain: float32 [768], P('dp'), may hold values from 0.1 to 1.9
- up_weight: float32 [768, 3072], P('dp', 'mp'), may hold values from -0.21875 to 0.21875
- down_weight: float32 [768, 3072], P('dp', 'mp'), may hold values from -0.109375 to 0.109375
- group_image: int32 [128], replicated, may hold values from 0 to 7, as said below
- latent_keep: int32 [1024], replicated, may hold values 0 or 1
- token_cotangent: float32 [32768, 768], P('dp'), may hold values from -6 to 6
- latent_cotangent: float32 [1024, 768], P('dp'), may hold values from -6 to 6
Outputs:
- token_output: float32 [32768, 768], P('dp')
- latent_output: float32 [1024, 768], P('dp')
- grad_tokens: float32 [32768, 768], P('dp')
- grad_latents: float32 [1024, 768], P('dp')
- grad_condition: float32 [128, 768], P('dp')
- grad_modulator: float32 [768, 4608], P('dp')
- grad_offsets: float32 [4608], P('dp')
- grad_localqkv: float32 [768, 3, 768], P('dp', None, 'mp')
- grad_localout: float32 [768, 768], P('dp', 'mp')
- grad_globalqkv: float32 [768, 3, 768], P('dp', None, 'mp')
- grad_globalout: float32 [768, 768], P('dp', 'mp')
- grad_gain: float32 [768], P('dp')
- grad_upweight: float32 [768, 3072], P('dp', 'mp')
- grad_downweight: float32 [768, 3072], P('dp', 'mp')
Inputs may be any that keep to these rules, and one draw needn't show every extreme that they name: `group_image`: never falling from group to group, starting at 0 and rising by at most one; groups 8 - 1 to 120 always belong to one image.
All inputs are finite; a program needn't handle non-finite values.
Results may differ from a plain program's by a relative error of at most 0.015.
The roundings to bfloat16 on the way count: a program that leaves them out, or rounds other values in their place, can miss the bound.
Values may be sent and summed in bfloat16 or wider, within the bound.
No kernel may reach another device: no remote copies, remote signals or barrier semaphores. Data moves between devices by JAX's collectives and lax.ppermute only.
A program may use at most 256 MiB of HBM per device.

v0:
```python
import jax
import jax.numpy as jnp
from jax import lax
from jax.sharding import PartitionSpec as P

HD = 64


EPSILON = 1e-06
LOWER = jnp.bfloat16
UPPER = jnp.float32


def normalize(values):
    center = values - jnp.mean(values, -1, keepdims=True)
    inverse = lax.rsqrt(jnp.mean(center * center, -1, keepdims=True) + EPSILON)
    return (center * inverse, inverse)


def norm_back(grad_normed, normed, inverse):
    mean_grad = jnp.mean(grad_normed, -1, keepdims=True)
    mean_proj = jnp.mean(grad_normed * normed, -1, keepdims=True)
    return inverse * (grad_normed - mean_grad - normed * mean_proj)


def body(
    tokens,
    latents,
    condition,
    modulator,
    offsets,
    local_qkv,
    local_out,
    global_qkv,
    global_out,
    latent_gain,
    up_weight,
    down_weight,
    group_image,
    latent_keep,
    token_cotangent,
    latent_cotangent,
):
    groups = condition.shape[0]
    features = tokens.shape[1]
    group_len = tokens.shape[0] // groups
    lat_count = latents.shape[0] // groups
    item_count = group_len + lat_count
    scaling = HD ** (-0.5)
    gathered = (
        lax.all_gather(modulator.astype(LOWER), "dp", axis=0, tiled=True),
        lax.all_gather(offsets.astype(LOWER), "dp", axis=0, tiled=True),
        lax.all_gather(local_qkv.astype(LOWER), "dp", axis=0, tiled=True),
        lax.all_gather(local_out.astype(LOWER), "dp", axis=0, tiled=True),
        lax.all_gather(global_qkv.astype(LOWER), "dp", axis=0, tiled=True),
        lax.all_gather(global_out.astype(LOWER), "dp", axis=0, tiled=True),
        lax.all_gather(latent_gain.astype(LOWER), "dp", axis=0, tiled=True),
        lax.all_gather(up_weight.astype(LOWER), "dp", axis=0, tiled=True),
        lax.all_gather(down_weight.astype(LOWER), "dp", axis=0, tiled=True),
    )
    w_mod, b_mod, w_qkv, w_out, w_gqkv, w_gout, gain_low, w_up, w_down = gathered
    local_width = w_out.shape[1]
    head_count = local_width // HD
    scaled = jax.nn.silu(condition).astype(LOWER)
    modulation = jnp.dot(scaled, w_mod, preferred_element_type=UPPER) + b_mod.astype(UPPER)
    shift_one, scale_one, gate_one, shift_two, scale_two, gate_two = [
        modulation[:, None, number * features : (number + 1) * features] for number in range(6)
    ]
    items = jnp.concatenate(
        [tokens.reshape(groups, group_len, features), latents.reshape(groups, lat_count, features)],
        axis=1,
    )
    normed_one, inverse_one = normalize(items)
    input_one = (normed_one * (1.0 + scale_one) + shift_one).astype(LOWER)
    triple = jnp.einsum("gnd,dke->gnke", input_one, w_qkv, preferred_element_type=UPPER).astype(
        LOWER
    )
    queries = triple[:, :, 0].reshape(groups, item_count, head_count, HD)
    key_rows = triple[:, :, 1].reshape(groups, item_count, head_count, HD)
    value_rows = triple[:, :, 2].reshape(groups, item_count, head_count, HD)
    scores = (
        jnp.einsum("gnhe,gmhe->ghnm", queries, key_rows, preferred_element_type=UPPER) * scaling
    )
    peak = jnp.max(scores, -1, keepdims=True)
    log_total = peak + jnp.log(jnp.sum(jnp.exp(scores - peak), -1, keepdims=True))
    weights = jnp.exp(scores - log_total)
    mixed_heads = (
        jnp.einsum(
            "ghnm,gmhe->gnhe", weights.astype(LOWER), value_rows, preferred_element_type=UPPER
        )
        .astype(LOWER)
        .reshape(groups, item_count, local_width)
    )
    attended = lax.psum(
        jnp.einsum("gnc,dc->gnd", mixed_heads, w_out, preferred_element_type=UPPER).astype(
            jnp.bfloat16
        ),
        "mp",
    ).astype(jnp.float32)
    after_local = items + gate_one * attended
    lat_one = after_local[:, group_len:].reshape(groups * lat_count, features)
    lat_normed, lat_inverse = normalize(lat_one)
    lat_input = (lat_normed * gain_low.astype(UPPER)).astype(LOWER)
    lat_triple = jnp.einsum("nd,dke->nke", lat_input, w_gqkv, preferred_element_type=UPPER).astype(
        LOWER
    )
    all_keys, all_values = (
        lax.all_gather(lat_triple[:, 1], "dp", axis=0, tiled=True),
        lax.all_gather(lat_triple[:, 2], "dp", axis=0, tiled=True),
    )
    lat_total = all_keys.shape[0]
    own_count = groups * lat_count
    lat_queries = lat_triple[:, 0].reshape(-1, head_count, HD)
    key_heads = all_keys.reshape(lat_total, head_count, HD)
    value_heads = all_values.reshape(lat_total, head_count, HD)
    first_group = lax.axis_index("dp") * groups
    own_images = jnp.repeat(lax.dynamic_slice_in_dim(group_image, first_group, groups), lat_count)
    all_images = jnp.repeat(group_image, lat_count)
    own_rows = first_group * lat_count + jnp.arange(own_count)
    allowed = (own_images[:, None] == all_images[None, :]) & (
        (latent_keep[None, :] == 1) | (own_rows[:, None] == jnp.arange(lat_total)[None, :])
    )
    lat_scores = (
        jnp.einsum("nhe,mhe->hnm", lat_queries, key_heads, preferred_element_type=UPPER) * scaling
    )
    lat_scores = jnp.where(allowed[None], lat_scores, -1e30)
    lat_peak = jnp.max(lat_scores, -1, keepdims=True)
    lat_log = lat_peak + jnp.log(jnp.sum(jnp.exp(lat_scores - lat_peak), -1, keepdims=True))
    lat_weights = jnp.exp(lat_scores - lat_log)
    lat_mixed = (
        jnp.einsum(
            "hnm,mhe->nhe", lat_weights.astype(LOWER), value_heads, preferred_element_type=UPPER
        )
        .astype(LOWER)
        .reshape(-1, local_width)
    )
    lat_branch = lax.psum(
        jnp.einsum("nc,dc->nd", lat_mixed, w_gout, preferred_element_type=UPPER).astype(
            jnp.bfloat16
        ),
        "mp",
    ).astype(jnp.float32)
    lat_two = lat_one + lat_branch
    after_latent = jnp.concatenate(
        [after_local[:, :group_len], lat_two.reshape(groups, lat_count, features)], axis=1
    )
    normed_two, inverse_two = normalize(after_latent)
    input_two = (normed_two * (1.0 + scale_two) + shift_two).astype(LOWER)
    upward = jnp.einsum("gnd,df->gnf", input_two, w_up, preferred_element_type=UPPER)
    hidden = jax.nn.gelu(upward).astype(LOWER)
    narrowed = lax.psum(
        jnp.einsum("gnf,df->gnd", hidden, w_down, preferred_element_type=UPPER).astype(
            jnp.bfloat16
        ),
        "mp",
    ).astype(jnp.float32)
    result = after_latent + gate_two * narrowed
    grad_result = jnp.concatenate(
        [
            token_cotangent.reshape(groups, group_len, features),
            latent_cotangent.reshape(groups, lat_count, features),
        ],
        axis=1,
    )
    grad_gate_two = jnp.sum(grad_result * narrowed, 1)
    grad_narrow = (gate_two * grad_result).astype(LOWER)
    grad_hidden = jnp.einsum("gnd,df->gnf", grad_narrow, w_down, preferred_element_type=UPPER)
    grad_upward = jax.vjp(jax.nn.gelu, upward)[1](grad_hidden)[0].astype(LOWER)
    down_grad = jnp.einsum("gnd,gnf->df", grad_narrow, hidden, preferred_element_type=UPPER)
    up_grad = jnp.einsum("gnd,gnf->df", input_two, grad_upward, preferred_element_type=UPPER)
    grad_input_two = lax.psum(
        jnp.einsum("gnf,df->gnd", grad_upward, w_up, preferred_element_type=UPPER).astype(
            jnp.bfloat16
        ),
        "mp",
    ).astype(jnp.float32)
    grad_shift_two = jnp.sum(grad_input_two, 1)
    grad_scale_two = jnp.sum(grad_input_two * normed_two, 1)
    grad_after_latent = grad_result + norm_back(
        grad_input_two * (1.0 + scale_two), normed_two, inverse_two
    )
    grad_lat_two = grad_after_latent[:, group_len:].reshape(-1, features)
    grad_branch = grad_lat_two.astype(LOWER)
    grad_lat_mixed = (
        jnp.einsum("nd,dc->nc", grad_branch, w_gout, preferred_element_type=UPPER)
        .astype(LOWER)
        .reshape(-1, head_count, HD)
    )
    gout_grad = jnp.einsum("nd,nc->dc", grad_branch, lat_mixed, preferred_element_type=UPPER)
    grad_lat_weights = jnp.einsum(
        "nhe,mhe->hnm", grad_lat_mixed, value_heads, preferred_element_type=UPPER
    )
    lat_delta = jnp.sum(grad_lat_weights * lat_weights, -1, keepdims=True)
    grad_lat_scores = (lat_weights * (grad_lat_weights - lat_delta)).astype(LOWER)
    grad_lat_queries = (
        jnp.einsum("hnm,mhe->nhe", grad_lat_scores, key_heads, preferred_element_type=UPPER)
        * scaling
    ).astype(LOWER)
    key_terms = (
        jnp.einsum("hnm,nhe->mhe", grad_lat_scores, lat_queries, preferred_element_type=UPPER)
        * scaling
    )
    value_terms = jnp.einsum(
        "hnm,nhe->mhe", lat_weights.astype(LOWER), grad_lat_mixed, preferred_element_type=UPPER
    )
    grad_keys, grad_values = (
        lax.psum_scatter(
            key_terms.reshape(lat_total, local_width), "dp", scatter_dimension=0, tiled=True
        ),
        lax.psum_scatter(
            value_terms.reshape(lat_total, local_width), "dp", scatter_dimension=0, tiled=True
        ),
    )
    grad_lat_triple = jnp.stack(
        [
            grad_lat_queries.reshape(-1, local_width),
            grad_keys.astype(LOWER),
            grad_values.astype(LOWER),
        ],
        axis=1,
    )
    gqkv_grad = jnp.einsum("nd,nke->dke", lat_input, grad_lat_triple, preferred_element_type=UPPER)
    grad_lat_input = lax.psum(
        jnp.einsum("nke,dke->nd", grad_lat_triple, w_gqkv, preferred_element_type=UPPER).astype(
            jnp.bfloat16
        ),
        "mp",
    ).astype(jnp.float32)
    gain_grad = jnp.sum(grad_lat_input * lat_normed, 0)
    grad_lat_one = grad_lat_two + norm_back(
        grad_lat_input * gain_low.astype(UPPER), lat_normed, lat_inverse
    )
    grad_after_local = jnp.concatenate(
        [grad_after_latent[:, :group_len], grad_lat_one.reshape(groups, lat_count, features)],
        axis=1,
    )
    grad_gate_one = jnp.sum(grad_after_local * attended, 1)
    grad_attended = (gate_one * grad_after_local).astype(LOWER)
    out_grad = jnp.einsum("gnd,gnc->dc", grad_attended, mixed_heads, preferred_element_type=UPPER)
    grad_mixed = (
        jnp.einsum("gnd,dc->gnc", grad_attended, w_out, preferred_element_type=UPPER)
        .astype(LOWER)
        .reshape(groups, item_count, head_count, HD)
    )
    again_scores = (
        jnp.einsum("gnhe,gmhe->ghnm", queries, key_rows, preferred_element_type=UPPER) * scaling
    )
    again_weights = jnp.exp(again_scores - log_total)
    grad_weights = jnp.einsum(
        "gnhe,gmhe->ghnm", grad_mixed, value_rows, preferred_element_type=UPPER
    )
    row_delta = jnp.sum(grad_weights * again_weights, -1, keepdims=True)
    grad_scores = (again_weights * (grad_weights - row_delta)).astype(LOWER)
    grad_queries = (
        jnp.einsum("ghnm,gmhe->gnhe", grad_scores, key_rows, preferred_element_type=UPPER) * scaling
    ).astype(LOWER)
    grad_key_rows = (
        jnp.einsum("ghnm,gnhe->gmhe", grad_scores, queries, preferred_element_type=UPPER) * scaling
    ).astype(LOWER)
    grad_value_rows = jnp.einsum(
        "ghnm,gnhe->gmhe", again_weights.astype(LOWER), grad_mixed, preferred_element_type=UPPER
    ).astype(LOWER)
    grad_triple = jnp.stack(
        [
            grad_queries.reshape(groups, item_count, local_width),
            grad_key_rows.reshape(groups, item_count, local_width),
            grad_value_rows.reshape(groups, item_count, local_width),
        ],
        axis=2,
    )
    qkv_grad = jnp.einsum("gnd,gnke->dke", input_one, grad_triple, preferred_element_type=UPPER)
    grad_input_one = lax.psum(
        jnp.einsum("gnke,dke->gnd", grad_triple, w_qkv, preferred_element_type=UPPER).astype(
            jnp.bfloat16
        ),
        "mp",
    ).astype(jnp.float32)
    grad_shift_one = jnp.sum(grad_input_one, 1)
    grad_scale_one = jnp.sum(grad_input_one * normed_one, 1)
    grad_items = grad_after_local + norm_back(
        grad_input_one * (1.0 + scale_one), normed_one, inverse_one
    )
    grad_modulation = jnp.concatenate(
        [
            grad_shift_one,
            grad_scale_one,
            grad_gate_one,
            grad_shift_two,
            grad_scale_two,
            grad_gate_two,
        ],
        axis=-1,
    ).astype(LOWER)
    mod_grad = jnp.dot(scaled.T, grad_modulation, preferred_element_type=UPPER)
    bias_grad = jnp.sum(grad_modulation.astype(UPPER), 0)
    grad_scaled = jnp.dot(grad_modulation, w_mod.T, preferred_element_type=UPPER)
    grad_condition = jax.vjp(jax.nn.silu, condition)[1](grad_scaled)[0]
    reduced = (
        lax.psum_scatter(mod_grad, "dp", scatter_dimension=0, tiled=True),
        lax.psum_scatter(bias_grad, "dp", scatter_dimension=0, tiled=True),
        lax.psum_scatter(qkv_grad, "dp", scatter_dimension=0, tiled=True),
        lax.psum_scatter(out_grad, "dp", scatter_dimension=0, tiled=True),
        lax.psum_scatter(gqkv_grad, "dp", scatter_dimension=0, tiled=True),
        lax.psum_scatter(gout_grad, "dp", scatter_dimension=0, tiled=True),
        lax.psum_scatter(gain_grad, "dp", scatter_dimension=0, tiled=True),
        lax.psum_scatter(up_grad, "dp", scatter_dimension=0, tiled=True),
        lax.psum_scatter(down_grad, "dp", scatter_dimension=0, tiled=True),
    )
    return (
        result[:, :group_len].reshape(-1, features),
        result[:, group_len:].reshape(-1, features),
        grad_items[:, :group_len].reshape(-1, features),
        grad_items[:, group_len:].reshape(-1, features),
        grad_condition,
    ) + tuple(reduced)


def solution(mesh):
    placed = (
        P("dp", None),
        P("dp", None),
        P("dp", None),
        P("dp", None),
        P("dp"),
        P("dp", None, "mp"),
        P("dp", "mp"),
        P("dp", None, "mp"),
        P("dp", "mp"),
        P("dp"),
        P("dp", "mp"),
        P("dp", "mp"),
        P(),
        P(),
        P("dp", None),
        P("dp", None),
    )
    return jax.shard_map(
        body,
        mesh=mesh,
        in_specs=placed,
        out_specs=(
            P("dp", None),
            P("dp", None),
            P("dp", None),
            P("dp", None),
            P("dp", None),
            P("dp", None),
            P("dp"),
            P("dp", None, "mp"),
            P("dp", "mp"),
            P("dp", None, "mp"),
            P("dp", "mp"),
            P("dp"),
            P("dp", "mp"),
            P("dp", "mp"),
        ),
        check_vma=False,
    )
```

profile of v0, /device:TPU:0, one launch (start us, length us, event | category | flops | bytes accessed | tf_op | source)
XLA Modules:
  0.0 2081.4 jit_solution(3559365334400927944)
XLA Ops:
  15.4 80.1 %all-reduce.5 = (bf16[4608]{0:T(1024)(128)(2,1)S(1)}, bf16[768]{0:T(1024)(128)(2,1)S(1)}) all-reduce(bf16[4608]{0:T(1024)(128)(2,1)S(1)} %dynamic-update-slice, bf16[768]{0:T(1024)(128)(2,1)S(1)} %dynamic-update-slice.1), channel_id=1, replica_groups=mesh['dp'=16,'mp'=2] {'dp'}, use_global_device_ids=true, to_apply=%add | all-reduce | flops 5376 | bytes 21504
  96.5 3.9 fusion.89
  101.6 41.6 %all_gather.36 = bf16[768,384]{1,0:T(8,128)(2,1)S(1)} all-gather(bf16[48,384]{1,0:T(8,128)(2,1)S(1)} %convert_element_type.184), channel_id=1, replica_groups=mesh['dp'=16,'mp'=2] {'dp'}, dimensions={0}, use_global_device_ids=true | all-gather | bytes 626688 | tf_op jit(solution)/shard_map/all_gather | solution.py:54
  143.2 4.2 convolution_add_fusion
  148.1 34.9 %all-gather.10.cloned.1.call-done = bf16[768,3,384]{2,0,1:T(8,128)(2,1)} async-done(((bf16[48,3,384]{2,0,1:T(8,128)(2,1)}), bf16[768,3,384]{2,0,1:T(8,128)(2,1)}) %all-gather.10.cloned.1.call-update) | async-done | bytes 1769488 | tf_op jit(solution)/shard_map/all_gather | solution.py:53
  183.0 7.7 convolution_convert_fusion
  193.2 2.8 copy.107
  196.0 4.3 copy.106
  200.3 4.1 copy.105
  204.5 11.9 multiply_reduce_fusion.1
  216.4 10.4 exponential_reduce_fusion
  226.8 10.2 convolution_convert_fusion.3
  238.5 4.3 convolution_convert_fusion.1
  244.2 44.6 %all_gather.41 = bf16[768,384]{1,0:T(8,128)(2,1)} all-gather(bf16[48,384]{1,0:T(8,128)(2,1)S(1)} %convert_element_type.195), channel_id=1, replica_groups=mesh['dp'=16,'mp'=2] {'dp'}, dimensions={0}, use_global_device_ids=true | all-gather | bytes 626688 | tf_op jit(solution)/shard_map/all_gather | solution.py:56
  288.9 4.4 fusion.14
  293.3 2.8 copy-done.2
  297.5 31.1 %all-gather.12.cloned.1.call-done = bf16[768,3,384]{2,0,1:T(8,128)(2,1)} async-done(((bf16[48,3,384]{2,0,1:T(8,128)(2,1)}), bf16[768,3,384]{2,0,1:T(8,128)(2,1)}) %all-gather.12.cloned.1.call-update) | async-done | bytes 1769488 | tf_op jit(solution)/shard_map/all_gather | solution.py:55
  330.8 43.4 %all-gather.1 = bf16[1024,1,384]{2,0,1:T(8,128)(2,1)S(1)} all-gather(bf16[64,1,384]{2,0,1:T(8,128)(2,1)S(1)} %get-tuple-element.42), channel_id=3, replica_groups=mesh['dp'=16,'mp'=2] {'dp'}, dimensions={0}, use_global_device_ids=true | all-gather | bytes 835584 | tf_op jit(solution)/shard_map/all_gather | solution.py:108
  374.5 39.9 %all-gather = bf16[1024,1,384]{2,0,1:T(8,128)(2,1)S(1)} all-gather(bf16[64,1,384]{2,0,1:T(8,128)(2,1)S(1)} %get-tuple-element.44), channel_id=2, replica_groups=mesh['dp'=16,'mp'=2] {'dp'}, dimensions={0}, use_global_device_ids=true | all-gather | bytes 835584 | tf_op jit(solution)/shard_map/all_gather | solution.py:109
  421.6 6.0 slice.86
  427.6 6.6 all-reduce.15.cloned.1.call-done
  435.4 3.5 fusion.92
  440.6 60.3 %all-gather.14.cloned.1.call-done = bf16[768,1536]{1,0:T(8,128)(2,1)} async-done(((bf16[48,1536]{1,0:T(8,128)(2,1)}), bf16[768,1536]{1,0:T(8,128)(2,1)}) %all-gather.14.cloned.1.call-update) | async-done | bytes 2359312 | tf_op jit(solution)/shard_map/all_gather | solution.py:58
  500.9 11.4 fusion.34
  512.3 53.1 %all-gather.16.cloned.1.call-done = bf16[768,1536]{1,0:T(8,128)(2,1)} async-done(((bf16[48,1536]{1,0:T(8,128)(2,1)}), bf16[768,1536]{1,0:T(8,128)(2,1)}) %all-gather.16.cloned.1.call-update) | async-done | bytes 2359312 | tf_op jit(solution)/shard_map/all_gather | solution.py:59
  565.5 16.4 fusion.6
  584.6 6.6 fusion.36
  591.3 22.3 %all-reduce.17.cloned.1.call-done = bf16[8,264,768]{2,1,0:T(8,128)(2,1)} async-done(((bf16[8,264,768]{2,1,0:T(8,128)(2,1)}), bf16[8,264,768]{2,1,0:T(8,128)(2,1)}) %all-reduce.17.cloned.1.call-update) | async-done | bytes 3244048 | tf_op jit(solution)/shard_map/psum | solution.py:171
  613.6 7.1 fusion.22
  620.8 6.2 fusion.20
  634.5 3.1 copy.117
  642.8 120.8 %reduce-scatter.12.cloned.1.call-done = f32[64,384]{1,0:T(8,128)} async-done(((f32[1024,384]{1,0:T(8,128)}), f32[64,384]{1,0:T(8,128)}) %reduce-scatter.12.cloned.1.call-update) | async-done | bytes 98320 | tf_op jit(solution)/shard_map/reduce_scatter | solution.py:210
  764.4 127.7 %reduce-scatter.10.cloned.1.call-done = f32[64,384]{1,0:T(8,128)} async-done(((f32[1024,384]{1,0:T(8,128)}), f32[64,384]{1,0:T(8,128)}) %reduce-scatter.10.cloned.1.call-update) | async-done | bytes 98320 | tf_op jit(solution)/shard_map/reduce_scatter | solution.py:207
  895.9 12.8 fusion.39
  908.7 6.1 slice.96
  917.7 4.7 convolution_convert_fusion.4
  925.0 12.8 convolution_convert_fusion.2
  937.9 13.6 multiply_reduce_fusion
  951.5 13.5 multiply_convert_fusion
  965.0 7.0 multiply_convert_fusion.4
  971.9 5.6 multiply_convert_fusion.5
  977.5 4.2 copy.125
  981.7 4.1 copy.123
  988.6 9.2 bitcast_convert_fusion
  1001.1 7.4 convolution_bitcast_fusion.3
  1008.7 13.1 convolution_bitcast_fusion
  1022.1 14.7 convolution_bitcast_fusion.1
  1036.9 3.4 fusion.71
  1040.5 11.7 convolution_bitcast_fusion.2
  1053.5 3.1 reduce.2
  1057.5 6.3 fusion.27
  1063.9 9.5 fusion.15
  1073.6 3.4 fusion.17
  1077.0 7.1 fusion.86
  1085.6 6.2 slice.98
  1091.7 3.3 slice.94
  1095.1 75.3 %all-reduce.4 = (f32[4608]{0:T(1024)S(1)}, f32[768]{0:T(1024)S(1)}) all-reduce(f32[4608]{0:T(1024)S(1)} %convert_reduce_fusion, f32[768]{0:T(1024)S(1)} %copy-done.52), channel_id=7, replica_groups=mesh['dp'=16,'mp'=2] {'dp'}, use_global_device_ids=true, to_apply=%region_34.35.clone | all-reduce | flops 5376 | bytes 43008
  1174.9 5.6 fusion.73
  1180.4 107.3 %reduce-scatter.18.cloned.1.call-done = f32[48,384]{1,0:T(8,128)} async-done(((f32[768,384]{1,0:T(8,128)}), f32[48,384]{1,0:T(8,128)}) %reduce-scatter.18.cloned.1.call-update) | async-done | bytes 73744 | tf_op jit(solution)/shard_map/reduce_scatter | solution.py:302
  1287.8 141.5 %reduce-scatter.26.cloned.1.call-done = f32[48,1536]{1,0:T(8,128)} async-done(((f32[768,1536]{1,0:T(8,128)}), f32[48,1536]{1,0:T(8,128)}) %reduce-scatter.26.cloned.1.call-update) | async-done | bytes 294928 | tf_op jit(solution)/shard_map/reduce_scatter | solution.py:307
  1429.3 142.3 %reduce-scatter.24.cloned.1.call-done = f32[48,1536]{1,0:T(8,128)} async-done(((f32[768,1536]{1,0:T(8,128)}), f32[48,1536]{1,0:T(8,128)}) %reduce-scatter.24.cloned.1.call-update) | async-done | bytes 294928 | tf_op jit(solution)/shard_map/reduce_scatter | solution.py:306
  1571.6 138.0 %reduce-scatter.20.cloned.1.call-done = f32[48,3,384]{2,0,1:T(8,128)} async-done(((f32[768,3,384]{2,0,1:T(8,128)}), f32[48,3,384]{2,0,1:T(8,128)}) %reduce-scatter.20.cloned.1.call-update) | async-done | bytes 221200 | tf_op jit(solution)/shard_map/reduce_scatter | solution.py:303
  1709.6 138.2 %reduce-scatter.16.cloned.1.call-done = f32[48,3,384]{2,0,1:T(8,128)} async-done(((f32[768,3,384]{2,0,1:T(8,128)}), f32[48,3,384]{2,0,1:T(8,128)}) %reduce-scatter.16.cloned.1.call-update) | async-done | bytes 221200 | tf_op jit(solution)/shard_map/reduce_scatter | solution.py:301
  1847.8 226.8 %reduce-scatter.14.cloned.1.call-done = f32[48,4608]{1,0:T(8,128)} async-done(((f32[768,4608]{1,0:T(8,128)}), f32[48,4608]{1,0:T(8,128)}) %reduce-scatter.14.cloned.1.call-update) | async-done | bytes 884752 | tf_op jit(solution)/shard_map/reduce_scatter | solution.py:299
  (263 shorter events, 67.6 us)
Async XLA Ops:
  7.2 93.3 %copy-start.15 = (f32[64,768]{1,0:T(8,128)S(1)}, f32[64,768]{1,0:T(8,128)}, u32[]{:S(2)}) copy-start(f32[64,768]{1,0:T(8,128)} %param.17) | copy-start | bytes 589828
  7.2 136.0 %all-gather.8.cloned.1.call-start = ((), (), s32[]{:S(2)}) async-start(), calls=%async_computation.9 | async-start | bytes 7520256 | tf_op jit(solution)/shard_map/all_gather | solution.py:51
  9.3 173.7 %all-gather.10.cloned.1.call-start = ((), (), s32[]{:S(2)}) async-start(), calls=%async_computation.10 | async-start | bytes 1880064 | tf_op jit(solution)/shard_map/all_gather | solution.py:53
  10.9 277.9 %all-reduce.13.cloned.1.call-start = ((), (), s32[]{:S(2)}) async-start(), calls=%async_computation.11 | async-start | bytes 6488064 | tf_op jit(solution)/shard_map/psum | solution.py:94
  96.5 46.6 %copy-start.27 = (f32[8,768]{1,0:T(8,128)S(1)}, f32[8,768]{1,0:T(8,128)}, u32[]{:S(2)}) copy-start(f32[8,768]{1,0:T(8,128)} %param.18) | copy-start | bytes 73732
  100.5 82.5 %copy-start.34 = (f32[8,264]{1,0:T(8,128)}, f32[8,264]{1,0:T(8,128)S(1)}, u32[]{:S(2)}) copy-start(f32[8,264]{1,0:T(8,128)S(1)} %broadcast_multiply_fusion.5) | copy-start | bytes 25348
  101.5 89.1 %copy-start.36 = (f32[8,264]{1,0:T(8,128)}, f32[8,264]{1,0:T(8,128)S(1)}, u32[]{:S(2)}) copy-start(f32[8,264]{1,0:T(8,128)S(1)} %add_rsqrt_fusion.1) | copy-start | bytes 25348
  143.2 93.9 %copy-start.18 = (bf16[768,384]{1,0:T(8,128)(2,1)}, bf16[768,384]{1,0:T(8,128)(2,1)S(1)}, u32[]{:S(2)}) copy-start(bf16[768,384]{1,0:T(8,128)(2,1)S(1)} %all_gather.36) | copy-start | bytes 1769476
  148.1 42.6 %copy-start.30 = (f32[8,768]{1,0:T(8,128)}, f32[8,768]{1,0:T(8,128)S(1)}, u32[]{:S(2)}) copy-start(f32[8,768]{1,0:T(8,128)S(1)} %get-tuple-element.40) | copy-start | bytes 73732
  148.1 42.6 %copy-start.49 = (f32[8,768]{1,0:T(8,128)}, f32[8,768]{1,0:T(8,128)S(1)}, u32[]{:S(2)}) copy-start(f32[8,768]{1,0:T(8,128)S(1)} %get-tuple-element.39) | copy-start | bytes 73732
  148.1 140.8 %copy-start.44 = (f32[8,768]{1,0:T(8,128)}, f32[8,768]{1,0:T(8,128)S(1)}, u32[]{:S(2)}) copy-start(f32[8,768]{1,0:T(8,128)S(1)} %get-tuple-element.41) | copy-start | bytes 73732
  196.0 20.3 copy-start.7
  216.4 10.5 copy-start.8
  242.8 85.8 %all-gather.12.cloned.1.call-start = ((), (), s32[]{:S(2)}) async-start(), calls=%async_computation.12 | async-start | bytes 1880064 | tf_op jit(solution)/shard_map/all_gather | solution.py:55
  243.5 190.7 %all-reduce.15.cloned.1.call-start = ((), (), s32[]{:S(2)}) async-start(), calls=%async_computation.13 | async-start | bytes 196608 | tf_op jit(solution)/shard_map/psum | solution.py:137
  296.3 32.3 %copy-start.53 = (f32[64]{0:T(128)}, f32[64]{0:T(128)S(1)}, u32[]{:S(2)}) copy-start(f32[64]{0:T(128)S(1)} %div.48) | copy-start | bytes 772
  297.5 31.1 %copy-start.55 = (f32[64]{0:T(128)}, f32[64]{0:T(128)S(1)}, u32[]{:S(2)}) copy-start(f32[64]{0:T(128)S(1)} %rsqrt.29) | copy-start | bytes 772
  415.6 12.0 copy-start.41
  416.1 11.6 copy-start.20
  418.1 82.8 %all-gather.14.cloned.1.call-start = ((), (), s32[]{:S(2)}) async-start(), calls=%async_computation.14 | async-start | bytes 2506752 | tf_op jit(solution)/shard_map/all_gather | solution.py:58
  419.9 145.6 %all-gather.16.cloned.1.call-start = ((), (), s32[]{:S(2)}) async-start(), calls=%async_computation.15 | async-start | bytes 2506752 | tf_op jit(solution)/shard_map/all_gather | solution.py:59
  421.6 192.1 %all-reduce.17.cloned.1.call-start = ((), (), s32[]{:S(2)}) async-start(), calls=%async_computation.16 | async-start | bytes 6488064 | tf_op jit(solution)/shard_map/psum | solution.py:171
  565.5 19.1 copy-start.59
  591.3 172.3 %reduce-scatter.12.cloned.1.call-start = ((), (), s32[]{:S(2)}) async-start(), calls=%async_computation.18 | async-start | bytes 1671168 | tf_op jit(solution)/shard_map/reduce_scatter | solution.py:210
  613.6 7.1 copy-start.24
  613.6 7.2 copy-start.32
  613.6 7.2 copy-start.39
  620.8 8.8 copy-start.14
  637.7 254.5 %reduce-scatter.10.cloned.1.call-start = ((), (), s32[]{:S(2)}) async-start(), calls=%async_computation.17 | async-start | bytes 1671168 | tf_op jit(solution)/shard_map/reduce_scatter | solution.py:207
  642.2 272.5 %all-reduce.19.cloned.1.call-start = ((), (), s32[]{:S(2)}) async-start(), calls=%async_computation.19 | async-start | bytes 196608 | tf_op jit(solution)/shard_map/psum | solution.py:223
  895.9 157.6 %all-reduce.21.cloned.1.call-start = ((), (), s32[]{:S(2)}) async-start(), calls=%async_computation.27 | async-start | bytes 12976128 | tf_op jit(solution)/shard_map/psum | solution.py:151
  908.7 9.0 copy-start.19
  908.7 9.0 copy-start.45
  917.7 83.4 %copy-start.22 = (f32[8,8,768]{2,1,0:T(8,128)}, f32[8,8,768]{2,1,0:T(8,128)S(1)}, u32[]{:S(2)}) copy-start(f32[8,8,768]{2,1,0:T(8,128)S(1)} %fusion.62) | copy-start | bytes 589828
  925.0 12.8 copy-start.9
  977.5 8.3 copy-start.13
  997.8 182.6 %reduce-scatter.22.cloned.1.call-start = ((), (), s32[]{:S(2)}) async-start(), calls=%async_computation.24 | async-start | bytes 1253376 | tf_op jit(solution)/shard_map/reduce_scatter | solution.py:304
  1001.0 7.6 copy-start.25
  1001.0 7.6 copy-start.42
  1001.0 286.7 %reduce-scatter.18.cloned.1.call-start = ((), (), s32[]{:S(2)}) async-start(), calls=%async_computation.22 | async-start | bytes 1253376 | tf_op jit(solution)/shard_map/reduce_scatter | solution.py:302
  1008.6 13.5 copy-start.33
  1008.6 13.5 copy-start.40
  1008.6 13.5 copy-start.51
  1008.6 420.7 %reduce-scatter.26.cloned.1.call-start = ((), (), s32[]{:S(2)}) async-start(), calls=%async_computation.26 | async-start | bytes 5013504 | tf_op jit(solution)/shard_map/reduce_scatter | solution.py:307
  1021.8 549.7 %reduce-scatter.24.cloned.1.call-start = ((), (), s32[]{:S(2)}) async-start(), calls=%async_computation.25 | async-start | bytes 5013504 | tf_op jit(solution)/shard_map/reduce_scatter | solution.py:306
  1036.9 672.8 %reduce-scatter.20.cloned.1.call-start = ((), (), s32[]{:S(2)}) async-start(), calls=%async_computation.23 | async-start | bytes 3760128 | tf_op jit(solution)/shard_map/reduce_scatter | solution.py:303
  1040.4 12.0 copy-start.5
  1040.4 807.4 %reduce-scatter.16.cloned.1.call-start = ((), (), s32[]{:S(2)}) async-start(), calls=%async_computation.21 | async-start | bytes 3760128 | tf_op jit(solution)/shard_map/reduce_scatter | solution.py:301
  1052.1 1022.5 %reduce-scatter.14.cloned.1.call-start = ((), (), s32[]{:S(2)}) async-start(), calls=%async_computation.20 | async-start | bytes 15040512 | tf_op jit(solution)/shard_map/reduce_scatter | solution.py:299
  1053.5 10.3 copy-start.3
  1056.6 7.2 copy-start.10
  1056.6 7.2 copy-start.16
  1056.6 7.2 copy-start.23
  1056.6 7.2 copy-start.38
  1057.5 16.0 slice-start
  1057.5 16.0 slice-start.4
  1063.8 9.6 copy-start.48
  1063.9 9.6 copy-start.47
  1063.9 9.6 slice-start.1
  1063.9 9.6 slice-start.5
  1063.9 9.6 copy-start.17
  1063.9 9.6 copy-start.26
  1063.9 9.6 copy-start.43
  1084.1 7.6 slice-start.2
  (22 other events, 96.3 us)
Sparse Core Ops, SparseCore 0:
  11.4 111.3 all-gather.7
  126.1 56.8 all-gather.9
  242.9 22.2 all-reduce.12
  268.3 60.2 all-gather.11
  418.3 15.9 all-reduce.14
  437.4 63.4 all-gather.13
  504.3 61.0 all-gather.15
  591.4 22.1 all-reduce.16
  637.8 125.6 reduce-scatter.11
  768.7 123.3 reduce-scatter.9
  896.0 16.7 all-reduce.18
  997.9 31.7 all-reduce.20
  1035.0 124.8 reduce-scatter.21
  1165.1 122.6 reduce-scatter.17
  1293.4 135.8 reduce-scatter.25
  1435.7 135.8 reduce-scatter.23
  1577.1 132.4 reduce-scatter.19
  1715.1 132.6 reduce-scatter.15
  1854.2 220.4 reduce-scatter.13
where the time goes:
time: 2090 us; the launch traced here: 2080 us
  waiting for transfers between devices  1350 us (65%)
  blocking collectives  325 us (16%)
  matrix products  217 us (10%)
  other arithmetic  94.4 us (5%)
  local copies, waits for them, and re-layouts  74.3 us (4%)
    reduce_scatter x1, waiting for transfers between devices, body(): lax.psum_scatter(mod_grad, 'dp', scatter_dimension=0, tiled=True)  227 us
    unnamed x2, blocking collectives  155 us
    reduce_scatter x1, waiting for transfers between devices, body(): lax.psum_scatter(up_grad, 'dp', scatter_dimension=0, tiled=True)  142 us
    reduce_scatter x1, waiting for transfers between devices, body(): lax.psum_scatter(down_grad, 'dp', scatter_dimension=0, tiled=True)  142 us
    reduce_scatter x1, waiting for transfers between devices, body(): lax.psum_scatter(qkv_grad, 'dp', scatter_dimension=0, tiled=True)  138 us
    reduce_scatter x1, waiting for transfers between devices, body(): lax.psum_scatter(gqkv_grad, 'dp', scatter_dimension=0, tiled=True)  138 us
    reduce_scatter x1, waiting for transfers between devices, body(): lax.psum_scatter(key_terms.reshape(lat_total, local_width), 'dp', scatter...  128 us
    reduce_scatter x1, waiting for transfers between devices, body(): lax.psum_scatter(value_terms.reshape(lat_total, local_width), 'dp', scatt...  121 us
  transfers between devices with their start and end apart: 19, of which 14 were waited for; matrix products, arithmetic and copies ran while one was open for 9% of the time, Pallas kernels for 0%

commit v1 on v0

v1 whole, which is shorter than its diff:
```python
import jax
import jax.numpy as jnp
from jax import lax
from jax.sharding import PartitionSpec as P

HD = 64
EPSILON = 1e-06
LOWER = jnp.bfloat16
UPPER = jnp.float32


def normalize(values):
    center = values - jnp.mean(values, -1, keepdims=True)
    inverse = lax.rsqrt(jnp.mean(center * center, -1, keepdims=True) + EPSILON)
    return (center * inverse, inverse)


def norm_back(grad_normed, normed, inverse):
    mean_grad = jnp.mean(grad_normed, -1, keepdims=True)
    mean_proj = jnp.mean(grad_normed * normed, -1, keepdims=True)
    return inverse * (grad_normed - mean_grad - normed * mean_proj)


def dot(left, right, dims):
    return lax.dot_general(left, right, ((dims[0], dims[1]), ((), ())), preferred_element_type=UPPER)


def mm(left, right):
    return dot(left, right, ((1,), (0,)))


def mm_nt(left, right):
    return dot(left, right, ((1,), (1,)))


def mm_tn(left, right):
    return dot(left, right, ((0,), (0,)))


class Moves:
    def __init__(self, dp_size):
        self.dp_size = dp_size
        self.staged = dp_size == 16
        self.dp = lax.axis_index("dp")
        self.mp = lax.axis_index("mp")
        if self.staged:
            self.z = self.dp // 4
            self.y = (self.dp // 2) % 2
            self.x = self.dp % 2

    def swap(self, value):
        return lax.ppermute(value, "mp", [(0, 1), (1, 0)])

    def in_order(self, own, other, axis=0):
        return jnp.where(
            self.mp == 0,
            jnp.concatenate([own, other], axis),
            jnp.concatenate([other, own], axis),
        )

    def flip(self, value, bits):
        return lax.ppermute(value, "dp", [(d, d ^ bits) for d in range(16)])

    def turn(self, value, step):
        return lax.ppermute(value, "dp", [(d, (d + 4 * step) % 16) for d in range(16)])

    def pair(self, own, other, index):
        return jnp.where(
            index == 0, jnp.stack([own, other], 1), jnp.stack([other, own], 1)
        )

    def gather(self, value, direct=False):
        if not self.staged:
            return lax.all_gather(value, "dp", axis=0)
        got = [value] + [self.turn(value, step) for step in (1, 2, 3)]
        line = jnp.zeros((4,) + value.shape, value.dtype)
        for step in range(4):
            line = lax.dynamic_update_index_in_dim(line, got[step], (self.z - step) % 4, 0)
        if direct:
            quad = jnp.zeros((4, 4) + value.shape, value.dtype)
            here = self.y * 2 + self.x
            for bits in range(4):
                part = line if bits == 0 else self.flip(line, bits)
                quad = lax.dynamic_update_index_in_dim(quad, part, here ^ bits, 1)
            return quad.reshape((16,) + value.shape)
        first, second = line[:2], line[2:]
        first_x = self.pair(first, self.flip(first, 1), self.x)
        second_y = self.pair(second, self.flip(second, 2), self.y)
        first_all = self.pair(first_x, self.flip(first_x, 2), self.y)
        other = self.flip(second_y, 1)
        second_all = jnp.where(
            self.x == 0, jnp.stack([second_y, other], 2), jnp.stack([other, second_y], 2)
        )
        return jnp.concatenate([first_all, second_all], 0).reshape((16,) + value.shape)

    def pick(self, value, index, axis):
        return lax.dynamic_index_in_dim(value, index, axis, keepdims=False)

    def scatter_sum(self, value):
        if not self.staged:
            return lax.psum_scatter(
                value.astype(UPPER), "dp", scatter_dimension=0, tiled=False
            )
        kind = value.dtype

        def add(one, two):
            return (one.astype(UPPER) + two.astype(UPPER)).astype(kind)

        cube = value.reshape((4, 2, 2) + value.shape[1:])
        first, second = cube[:2], cube[2:]
        got_first = self.flip(self.pick(first, 1 - self.y, 1), 2)
        got_second = self.flip(self.pick(second, 1 - self.x, 2), 1)
        first = add(self.pick(first, self.y, 1), got_first)
        second = add(self.pick(second, self.x, 2), got_second)
        got_first = self.flip(self.pick(first, 1 - self.x, 1), 1)
        got_second = self.flip(self.pick(second, 1 - self.y, 1), 2)
        line = jnp.concatenate(
            [
                add(self.pick(first, self.x, 1), got_first),
                add(self.pick(second, self.y, 1), got_second),
            ],
            0,
        )
        total = self.pick(line, self.z, 0).astype(UPPER)
        for step in (1, 2, 3):
            part = self.pick(line, (self.z + step) % 4, 0)
            total = total + self.turn(part, step).astype(UPPER)
        return total

    def exchange(self, value):
        return lax.all_to_all(value, "dp", 0, 0, tiled=True)


def attention_forward(items, shift, scale, gate, w_qkv, w_out):
    groups, count, features = items.shape
    heads = features // HD
    normed, inverse = normalize(items)
    inputs = (normed * (1.0 + scale) + shift).astype(LOWER)
    triple = jnp.einsum("gnd,dk->gnk", inputs, w_qkv, preferred_element_type=UPPER).astype(LOWER)
    triple = triple.reshape(groups, count, 2, 3, heads // 2, HD)
    queries, keys, values = [
        triple[:, :, :, kind].reshape(groups, count, heads, HD) for kind in range(3)
    ]
    scores = jnp.einsum("gnhe,gmhe->ghnm", queries, keys, preferred_element_type=UPPER) * HD**-0.5
    peak = jnp.max(scores, -1, keepdims=True)
    log_total = peak + jnp.log(jnp.sum(jnp.exp(scores - peak), -1, keepdims=True))
    weights = jnp.exp(scores - log_total)
    mixed = (
        jnp.einsum("ghnm,gmhe->gnhe", weights.astype(LOWER), values, preferred_element_type=UPPER)
        .astype(LOWER)
        .reshape(groups, count, features)
    )
    attended = jnp.einsum("gnc,dc->gnd", mixed, w_out, preferred_element_type=UPPER)
    after = items + gate * attended
    return after, (normed, inverse, inputs, queries, keys, values, log_total, mixed, attended)


def attention_backward(grad_after, saved, scale, gate, w_qkv, w_out):
    normed, inverse, inputs, queries, keys, values, log_total, mixed, attended = saved
    groups, count, features = normed.shape
    heads = features // HD
    grad_gate = jnp.sum(grad_after * attended, 1)
    grad_attended = (gate * grad_after).astype(LOWER)
    out_grad = jnp.einsum("gnd,gnc->dc", grad_attended, mixed, preferred_element_type=UPPER)
    grad_mixed = (
        jnp.einsum("gnd,dc->gnc", grad_attended, w_out, preferred_element_type=UPPER)
        .astype(LOWER)
        .reshape(groups, count, heads, HD)
    )
    scores = jnp.einsum("gnhe,gmhe->ghnm", queries, keys, preferred_element_type=UPPER) * HD**-0.5
    weights = jnp.exp(scores - log_total)
    grad_weights = jnp.einsum("gnhe,gmhe->ghnm", grad_mixed, values, preferred_element_type=UPPER)
    delta = jnp.sum(grad_weights * weights, -1, keepdims=True)
    grad_scores = (weights * (grad_weights - delta)).astype(LOWER)
    grad_queries = (
        jnp.einsum("ghnm,gmhe->gnhe", grad_scores, keys, preferred_element_type=UPPER) * HD**-0.5
    ).astype(LOWER)
    grad_keys = (
        jnp.einsum("ghnm,gnhe->gmhe", grad_scores, queries, preferred_element_type=UPPER) * HD**-0.5
    ).astype(LOWER)
    grad_values = jnp.einsum(
        "ghnm,gnhe->gmhe", weights.astype(LOWER), grad_mixed, preferred_element_type=UPPER
    ).astype(LOWER)
    grad_triple = jnp.stack(
        [
            part.reshape(groups, count, 2, heads // 2, HD)
            for part in (grad_queries, grad_keys, grad_values)
        ],
        axis=3,
    ).reshape(groups, count, 3 * features)
    qkv_grad = jnp.einsum("gnd,gnk->dk", inputs, grad_triple, preferred_element_type=UPPER)
    grad_inputs = jnp.einsum("gnk,dk->gnd", grad_triple, w_qkv, preferred_element_type=UPPER)
    grad_shift = jnp.sum(grad_inputs, 1)
    grad_scale = jnp.sum(grad_inputs * normed, 1)
    grad_items = grad_after + norm_back(grad_inputs * (1.0 + scale), normed, inverse)
    return grad_items, grad_shift, grad_scale, grad_gate, qkv_grad, out_grad


def feed_forward(rows, grad_result, shift, scale, gate, w_up, w_down):
    normed, inverse = normalize(rows)
    inputs = (normed * (1.0 + scale) + shift).astype(LOWER)
    upward = jnp.einsum("gnd,df->gnf", inputs, w_up, preferred_element_type=UPPER)
    hidden, pull = jax.vjp(jax.nn.gelu, upward)
    hidden = hidden.astype(LOWER)
    narrowed = jnp.einsum("gnf,df->gnd", hidden, w_down, preferred_element_type=UPPER)
    result = rows + gate * narrowed
    grad_gate = jnp.sum(grad_result * narrowed, 1)
    grad_narrow = (gate * grad_result).astype(LOWER)
    grad_hidden = jnp.einsum("gnd,df->gnf", grad_narrow, w_down, preferred_element_type=UPPER)
    grad_upward = pull(grad_hidden)[0].astype(LOWER)
    down_grad = jnp.einsum("gnd,gnf->df", grad_narrow, hidden, preferred_element_type=UPPER)
    up_grad = jnp.einsum("gnd,gnf->df", inputs, grad_upward, preferred_element_type=UPPER)
    grad_inputs = jnp.einsum("gnf,df->gnd", grad_upward, w_up, preferred_element_type=UPPER)
    grad_shift = jnp.sum(grad_inputs, 1)
    grad_scale = jnp.sum(grad_inputs * normed, 1)
    grad_rows = grad_result + norm_back(grad_inputs * (1.0 + scale), normed, inverse)
    return result, grad_rows, grad_shift, grad_scale, grad_gate, up_grad, down_grad


def split_three(value):
    high = lax.reduce_precision(value, 8, 7)
    rest = value - high
    middle = lax.reduce_precision(rest, 8, 7)
    return [part.astype(LOWER) for part in (high, middle, rest - middle)]


def make_body(dp_size):
    def body(
        tokens,
        latents,
        condition,
        modulator,
        offsets,
        local_qkv,
        local_out,
        global_qkv,
        global_out,
        latent_gain,
        up_weight,
        down_weight,
        group_image,
        latent_keep,
        token_cotangent,
        latent_cotangent,
    ):
        move = Moves(dp_size)
        mp = move.mp
        groups = condition.shape[0]
        own = groups // 2
        features = tokens.shape[1]
        group_len = tokens.shape[0] // groups
        lat_count = latents.shape[0] // groups
        shard = modulator.shape[0]
        half = local_out.shape[1]
        units = up_weight.shape[1]
        width = modulator.shape[1]
        heads = half // HD

        def mine(value, axis=0):
            size = value.shape[axis] // 2
            return lax.dynamic_slice_in_dim(value, mp * size, size, axis)

        def others(value, axis=0):
            size = value.shape[axis] // 2
            return lax.dynamic_slice_in_dim(value, (1 - mp) * size, size, axis)

        scaled = jax.nn.silu(condition).astype(LOWER)
        extra = jnp.concatenate([latent_gain, offsets]).astype(LOWER)
        extra = jnp.pad(extra, (0, features - extra.shape[0]))[None]
        vectors = move.gather(jnp.concatenate([scaled, extra], 0), direct=True)
        scaled_all = vectors[:, :groups].reshape(dp_size * groups, features)
        gain = vectors[:, groups, :shard].reshape(features).astype(UPPER)
        bias = vectors[:, groups, shard : shard + width // dp_size].reshape(width).astype(UPPER)
        scaled_mine = lax.dynamic_slice_in_dim(scaled_all, move.dp * shard, shard, 1)

        def modulate(columns, bias_part):
            terms = mm(scaled_mine, mine(columns, 1).astype(LOWER))
            total = move.scatter_sum(terms.reshape(dp_size, groups, -1))
            full = move.in_order(mine(total), move.swap(others(total)), 1)
            return [
                part[:, None] for part in jnp.split(full + bias_part[None], 3, axis=1)
            ]

        middle = width // 2
        shift_one, scale_one, gate_one = modulate(modulator[:, :middle], bias[:middle])

        def whole(shard_rows, direct=False):
            gathered = move.gather(shard_rows, direct)
            return gathered.reshape((features,) + shard_rows.shape[1:])

        qkv_mine = whole(local_qkv.reshape(shard, 3 * half).astype(LOWER))
        w_qkv = jnp.concatenate([qkv_mine, move.swap(qkv_mine)], 1)
        small = whole(
            jnp.concatenate(
                [local_out, global_qkv.reshape(shard, 3 * half), global_out], 1
            ).astype(LOWER)
        )
        out_mine = small[:, :half]
        w_gqkv = small[:, half : 4 * half]
        w_gout = small[:, 4 * half :]
        w_out = jnp.concatenate([out_mine, move.swap(out_mine)], 1)
        wide = whole(jnp.concatenate([up_weight, down_weight], 1).astype(LOWER))
        wide_other = move.swap(wide)
        w_up = jnp.concatenate([wide[:, :units], wide_other[:, :units]], 1)
        w_down = jnp.concatenate([wide[:, units:], wide_other[:, units:]], 1)
        shift_two, scale_two, gate_two = modulate(modulator[:, middle:], bias[middle:])

        own_tokens = mine(tokens).reshape(own, group_len, features)
        own_latents = mine(latents).reshape(own, lat_count, features)
        items = jnp.concatenate([own_tokens, own_latents], axis=1)
        after_local, saved = attention_forward(
            items, shift_one, scale_one, gate_one, w_qkv, w_out
        )
        lat_one = after_local[:, group_len:].reshape(own * lat_count, features)

        lat_normed, lat_inverse = normalize(lat_one)
        lat_input = (lat_normed * gain).astype(LOWER)
        lat_input = move.in_order(lat_input, move.swap(lat_input))
        lat_triple = mm(lat_input, w_gqkv).astype(LOWER)
        chip_count = groups * lat_count
        lat_total = dp_size * chip_count
        key_values = move.gather(lat_triple[:, half:], direct=True).reshape(lat_total, 2 * half)

        def by_head(value):
            return value.reshape(value.shape[0], heads, HD)

        lat_queries = by_head(lat_triple[:, :half])
        key_heads, value_heads = by_head(key_values[:, :half]), by_head(key_values[:, half:])
        images = jnp.repeat(group_image, lat_count)
        first = move.dp * chip_count
        own_images = lax.dynamic_slice_in_dim(images, first, chip_count)
        own_keep = lax.dynamic_slice_in_dim(latent_keep, first, chip_count)
        rows = first + jnp.arange(chip_count)
        same = (own_images[:, None] == images[None, :])
        itself = rows[:, None] == jnp.arange(lat_total)[None, :]
        allowed = same & ((latent_keep[None, :] == 1) | itself)
        allowed_keys = same & ((own_keep[:, None] == 1) | itself)
        lat_scores = (
            jnp.einsum("nhe,mhe->hnm", lat_queries, key_heads, preferred_element_type=UPPER)
            * HD**-0.5
        )
        lat_scores = jnp.where(allowed[None], lat_scores, -1e30)
        lat_peak = jnp.max(lat_scores, -1, keepdims=True)
        lat_log = lat_peak + jnp.log(jnp.sum(jnp.exp(lat_scores - lat_peak), -1, keepdims=True))
        lat_weights = jnp.exp(lat_scores - lat_log)
        lat_mixed = (
            jnp.einsum(
                "hnm,mhe->nhe", lat_weights.astype(LOWER), value_heads, preferred_element_type=UPPER
            )
            .astype(LOWER)
            .reshape(chip_count, half)
        )
        branch = mm_nt(lat_mixed, w_gout)
        branch = mine(branch) + move.swap(others(branch))
        lat_two = lat_one + branch

        token_grad = mine(token_cotangent).reshape(own, group_len, features)
        lat_grad = mine(latent_cotangent).reshape(own, lat_count, features)
        (
            token_result,
            grad_tokens_two,
            shift_a,
            scale_a,
            gate_a,
            up_a,
            down_a,
        ) = feed_forward(
            after_local[:, :group_len], token_grad, shift_two, scale_two, gate_two, w_up, w_down
        )
        (
            lat_result,
            grad_lat_two,
            shift_b,
            scale_b,
            gate_b,
            up_b,
            down_b,
        ) = feed_forward(
            lat_two.reshape(own, lat_count, features),
            lat_grad,
            shift_two,
            scale_two,
            gate_two,
            w_up,
            w_down,
        )
        grad_shift_two, grad_scale_two, grad_gate_two = (
            shift_a + shift_b,
            scale_a + scale_b,
            gate_a + gate_b,
        )

        def reduce(value_mine, value_other):
            both = (value_mine + move.swap(value_other.astype(LOWER)).astype(UPPER)).astype(LOWER)
            return move.scatter_sum(both.reshape(dp_size, shard, -1))

        up_grad, down_grad = (up_a + up_b), (down_a + down_b)
        wide_grad = reduce(
            jnp.concatenate([up_grad[:, :units], down_grad[:, :units]], 1),
            jnp.concatenate([up_grad[:, units:], down_grad[:, units:]], 1),
        )
        token_output = move.in_order(token_result, move.swap(token_result))
        latent_output = move.in_order(lat_result, move.swap(lat_result))

        grad_lat_two = grad_lat_two.reshape(own * lat_count, features)
        grad_branch = grad_lat_two.astype(LOWER)
        grad_branch = move.in_order(grad_branch, move.swap(grad_branch))
        grad_mixed_rows = mm(grad_branch, w_gout).astype(LOWER)
        grad_mixed = by_head(grad_mixed_rows)
        gout_grad = mm_tn(grad_branch, lat_mixed)
        grad_weights = jnp.einsum(
            "nhe,mhe->hnm", grad_mixed, value_heads, preferred_element_type=UPPER
        )
        delta = jnp.sum(grad_weights * lat_weights, -1, keepdims=True)
        grad_scores = (lat_weights * (grad_weights - delta)).astype(LOWER)
        grad_queries = (
            jnp.einsum("hnm,mhe->nhe", grad_scores, key_heads, preferred_element_type=UPPER)
            * HD**-0.5
        ).astype(LOWER)
        stats = split_three(lat_log[..., 0].T) + split_three(delta[..., 0].T)
        stats = jnp.pad(jnp.concatenate(stats, 1), ((0, 0), (0, 128 - 6 * heads)))
        sent = jnp.concatenate([lat_triple[:, :half], grad_mixed_rows, stats], 1)
        came = move.gather(sent, direct=True).reshape(lat_total, -1)
        all_queries, all_grads = by_head(came[:, :half]), by_head(came[:, half : 2 * half])
        parts = came[:, 2 * half :].astype(UPPER)

        def rejoin(at):
            return sum(
                parts[:, (at + number) * heads : (at + number + 1) * heads] for number in range(3)
            ).T[:, None, :]

        all_log, all_delta = rejoin(0), rejoin(3)
        own_keys, own_values = by_head(lat_triple[:, half : 2 * half]), by_head(
            lat_triple[:, 2 * half :]
        )
        back_scores = (
            jnp.einsum("mhe,nhe->hmn", own_keys, all_queries, preferred_element_type=UPPER)
            * HD**-0.5
        )
        back_weights = jnp.exp(jnp.where(allowed_keys[None], back_scores - all_log, -1e30))
        back_grads = jnp.einsum(
            "mhe,nhe->hmn", own_values, all_grads, preferred_element_type=UPPER
        )
        back_scores_grad = (back_weights * (back_grads - all_delta)).astype(LOWER)
        grad_keys = (
            jnp.einsum("hmn,nhe->mhe", back_scores_grad, all_queries, preferred_element_type=UPPER)
            * HD**-0.5
        ).astype(LOWER)
        grad_values = jnp.einsum(
            "hmn,nhe->mhe", back_weights.astype(LOWER), all_grads, preferred_element_type=UPPER
        ).astype(LOWER)
        grad_lat_triple = jnp.concatenate(
            [part.reshape(chip_count, half) for part in (grad_queries, grad_keys, grad_values)], 1
        )
        gqkv_grad = mm_tn(lat_input, grad_lat_triple)
        grad_lat_input = mm_nt(grad_lat_triple, w_gqkv)
        grad_lat_input = mine(grad_lat_input) + move.swap(others(grad_lat_input))
        gain_part = jnp.sum(grad_lat_input * lat_normed, 0)
        grad_lat_one = grad_lat_two + norm_back(grad_lat_input * gain, lat_normed, lat_inverse)

        grad_after = jnp.concatenate(
            [grad_tokens_two, grad_lat_one.reshape(own, lat_count, features)], axis=1
        )
        grad_items, grad_shift_one, grad_scale_one, grad_gate_one, qkv_grad, out_grad = (
            attention_backward(grad_after, saved, scale_one, gate_one, w_qkv, w_out)
        )
        out_both = out_grad[:, :half] + move.swap(out_grad[:, half:].astype(LOWER)).astype(UPPER)
        small_grad = move.scatter_sum(
            jnp.concatenate([out_both, gqkv_grad, gout_grad], 1)
            .astype(LOWER)
            .reshape(dp_size, shard, -1)
        )
        qkv_sum = reduce(qkv_grad[:, : 3 * half], qkv_grad[:, 3 * half :])
        grad_tokens = grad_items[:, :group_len]
        grad_tokens = move.in_order(grad_tokens, move.swap(grad_tokens))
        grad_latents = grad_items[:, group_len:]
        grad_latents = move.in_order(grad_latents, move.swap(grad_latents))

        grad_modulation = jnp.concatenate(
            [
                grad_shift_one,
                grad_scale_one,
                grad_gate_one,
                grad_shift_two,
                grad_scale_two,
                grad_gate_two,
            ],
            axis=-1,
        ).astype(LOWER)
        gain_row = jnp.pad(
            jnp.concatenate(split_three(gain_part)), (0, width - 3 * features)
        )[None]
        rows_sent = jnp.concatenate([grad_modulation, gain_row], 0)
        rows_all = move.gather(rows_sent, direct=True)
        rows_other = move.swap(rows_all)
        gain_all = (rows_all[:, own].astype(UPPER) + rows_other[:, own].astype(UPPER)).sum(0)
        gain_all = gain_all[: 3 * features].reshape(3, features).sum(0)
        gain_grad = lax.dynamic_slice_in_dim(gain_all, move.dp * shard, shard)
        mod_all = move.in_order(rows_all[:, :own], rows_other[:, :own], 1).reshape(-1, width)
        mod_grad = mm_tn(scaled_mine, mod_all)
        bias_all = jnp.sum(mod_all.astype(UPPER), 0)
        piece = width // dp_size
        bias_grad = lax.dynamic_slice_in_dim(bias_all, move.dp * piece, piece)
        grad_scaled = mm_nt(mod_all, modulator.astype(LOWER)).reshape(dp_size, groups, shard)
        grad_scaled = move.exchange(grad_scaled).transpose(1, 0, 2).reshape(groups, features)
        grad_condition = jax.vjp(jax.nn.silu, condition)[1](grad_scaled)[0]

        return (
            token_output.reshape(-1, features),
            latent_output.reshape(-1, features),
            grad_tokens.reshape(-1, features),
            grad_latents.reshape(-1, features),
            grad_condition,
            mod_grad,
            bias_grad,
            qkv_sum.reshape(shard, 3, half),
            small_grad[:, :half],
            small_grad[:, half : 4 * half].reshape(shard, 3, half),
            small_grad[:, 4 * half :],
            gain_grad,
            wide_grad[:, :units],
            wide_grad[:, units:],
        )

    return body


def solution(mesh):
    rows, heads = P("dp", None), P("dp", None, "mp")
    columns, vector = P("dp", "mp"), P("dp")
    return jax.shard_map(
        make_body(mesh.shape["dp"]),
        mesh=mesh,
        in_specs=(
            rows,
            rows,
            rows,
            rows,
            vector,
            heads,
            columns,
            heads,
            columns,
            vector,
            columns,
            columns,
            P(),
            P(),
            rows,
            rows,
        ),
        out_specs=(
            rows,
            rows,
            rows,
            rows,
            rows,
            rows,
            vector,
            heads,
            columns,
            heads,
            columns,
            vector,
            columns,
            columns,
        ),
        check_vma=False,
    )
```

time: 2090 us -> 811 us (0.39)
  waiting for transfers between devices: 1350 us -> 200 us
  blocking collectives: 325 us -> 0 us
  starting transfers between devices: 1.18 us -> 121 us
  local copies, waits for them, and re-layouts: 74.3 us -> 153 us
  other arithmetic: 94.4 us -> 124 us
    reduce_scatter x9 -> x0, waiting for transfers between devices: 1140 us -> none  [the longest x1 227 us: body(): lax.psum_scatter(mod_grad, 'dp', scatter_dimension=0, tiled=True)]
    ppermute x0 -> x97, waiting for transfers between devices: none -> 198 us  [the longest x44 162 us: flip(): return lax.ppermute(value, 'dp', [(d, d ^ bits) for d in range(16)])]
    all_gather x5 -> x0, waiting for transfers between devices: 179 us -> none  [the longest x1 60.3 us: body(): lax.all_gather(up_weight.astype(LOWER), 'dp', axis=0, tiled=True)]
    all_gather x4 -> x0, blocking collectives: 169 us -> none  [the longest x1 44.6 us: body(): lax.all_gather(global_out.astype(LOWER), 'dp', axis=0, tiled=True)]
    unnamed x2 -> x0, blocking collectives: 155 us -> none
    ppermute x0 -> x97, starting transfers between devices: none -> 117 us  [the longest x36 67.4 us: turn(): lax.ppermute(value, 'dp', [(d, (d + 4 * step) % 16) for d in range(16)])]
    dynamic_update_slice x0 -> x42, local copies, waits for them, and re-layouts: none -> 36.7 us  [the longest x25 22.4 us: gather(): lax.dynamic_update_index_in_dim(line, got[step], (self.z - step) % 4, 0)]
    psum x5 -> x0, waiting for transfers between devices: 28.9 us -> none  [the longest x1 22.3 us: body(): lax.psum(jnp.einsum('gnf,df->gnd', grad_upward, w_up, preferred_element_t...]
  transfers between devices with their start and end apart: 19 -> 98, of which waited for: 14 -> 45; matrix products, arithmetic and copies ran while one was open for 9% -> 47% of each run, Pallas kernels for 0% -> 0%
where the time goes in v1:
time: 811 us; the launch traced here: 799 us
  waiting for transfers between devices  200 us (25%)
  matrix products  198 us (24%)
  local copies, waits for them, and re-layouts  153 us (19%)
  other arithmetic  124 us (15%)
  starting transfers between devices  121 us (15%)
    ppermute x44, waiting for transfers between devices, flip(): return lax.ppermute(value, 'dp', [(d, d ^ bits) for d in range(16)])  162 us
    ppermute x36, starting transfers between devices, turn(): lax.ppermute(value, 'dp', [(d, (d + 4 * step) % 16) for d in range(16)])  67.4 us
    ppermute x44, starting transfers between devices, flip(): return lax.ppermute(value, 'dp', [(d, d ^ bits) for d in range(16)])  47.3 us
    ppermute x36, waiting for transfers between devices, turn(): lax.ppermute(value, 'dp', [(d, (d + 4 * step) % 16) for d in range(16)])  33 us
    dynamic_update_slice x25, local copies, waits for them, and re-layouts, gather(): lax.dynamic_update_index_in_dim(line, got[step], (self.z - step) % 4, 0)  22.4 us
    dot_general x10, matrix products, dot(): lax.dot_general(left, right, ((dims[0], dims[1]), ((), ())), preferred_el...  18.1 us
    dot_general x2, matrix products, feed_forward(): jnp.einsum('gnd,df->gnf', grad_narrow, w_down, preferred_element_type=UPPER)  17.9 us
    dot_general x2, matrix products, feed_forward(): jnp.einsum('gnd,gnf->df', grad_narrow, hidden, preferred_element_type=UPPER)  16.3 us
  transfers between devices with their start and end apart: 98, of which 45 were waited for; matrix products, arithmetic and copies ran while one was open for 47% of the time, Pallas kernels for 0%

profile of v1, /device:TPU:0, one launch (start us, length us, event | category | flops | bytes accessed | tf_op | source)
XLA Modules:
  0.0 799.4 jit_solution(12410481319295345354)
XLA Ops:
  3.6 4.0 collective-permute-start.1
  60.4 3.1 collective-permute-start.24
  95.9 8.6 %collective-permute-start.38 = (bf16[48,3072]{1,0:T(8,128)(2,1)}, bf16[48,3072]{1,0:T(8,128)(2,1)S(1)}, u32[]{:S(2)}, u32[]{:S(2)}) collective-permute-start(bf16[48,3072]{1,0:T(8,128)(2,1)} %pad_maximum_fusion.14), channel_id=1, source_target_pairs={{0,8},{2,10},{4,12},{6,14},{8,16},{10,18},{12,20},{14,22},{16,24},... | collective-permute-start | bytes 884744 | tf_op jit(solution)/shard_map/ppermute | solution.py:65
  120.1 4.5 collective-permute-done.9
  125.1 3.8 collective-permute-done.7
  129.4 3.8 collective-permute-done.33
  133.8 4.0 collective-permute-done.31
  138.3 3.8 collective-permute-start.10
  165.7 14.0 %collective-permute-done.20 = bf16[2,2,48,1152]{3,2,1,0:T(8,128)(2,1)S(1)} collective-permute-done((bf16[2,2,48,1152]{3,2,1,0:T(8,128)(2,1)S(1)}, bf16[2,2,48,1152]{3,2,1,0:T(8,128)(2,1)S(1)}, u32[]{:S(2)}, u32[]{:S(2)}) %collective-permute-start.20) | collective-permute-done | bytes 442400 | tf_op jit(solution)/shard_map/ppermute | solution.py:62
  184.8 14.4 %collective-permute-done.28 = bf16[2,2,48,1920]{3,2,1,0:T(8,128)(2,1)S(1)} collective-permute-done((bf16[2,2,48,1920]{3,2,1,0:T(8,128)(2,1)S(1)}, bf16[2,2,48,1920]{3,2,1,0:T(8,128)(2,1)S(1)}, u32[]{:S(2)}, u32[]{:S(2)}) %collective-permute-start.28) | collective-permute-done | bytes 737312 | tf_op jit(solution)/shard_map/ppermute | solution.py:62
  200.7 18.6 %collective-permute-done.44 = bf16[2,2,48,3072]{3,2,1,0:T(8,128)(2,1)S(1)} collective-permute-done((bf16[2,2,48,3072]{3,2,1,0:T(8,128)(2,1)S(1)}, bf16[2,2,48,3072]{3,2,1,0:T(8,128)(2,1)S(1)}, u32[]{:S(2)}, u32[]{:S(2)}) %collective-permute-start.44) | collective-permute-done | bytes 1179680 | tf_op jit(solution)/shard_map/ppermute | solution.py:62
  222.2 4.8 fusion.177
  228.3 5.9 convolution_convert_fusion
  234.2 8.3 %copy.812 = bf16[4,264,2304]{1,2,0:T(8,128)(2,1)} copy(bf16[4,264,2304]{2,1,0:T(8,128)(2,1)} %convolution_convert_fusion) | data formatting | bytes 9732096 | tf_op jit(solution)/shard_map/convert_element_type | solution.py:139
  242.5 4.1 fusion.175
  246.6 9.0 %multiply_reduce_fusion.1 = (f32[4,12,264]{2,1,0:T(8,128)S(1)}, f32[4,12,264,264]{2,3,1,0:T(8,128)}) fusion(bf16[4,264,12,64]{1,3,2,0:T(8,128)(2,1)S(1)} %bitcast.550, bf16[4,264,12,64]{1,3,2,0:T(8,128)(2,1)S(1)} %bitcast.554), kind=kOutput, calls=%fused_computation.6 | convolution fusion | flops 434890368 | bytes 16676352 | tf_op jit(solution)/shard_map/gnhe,gmhe->ghnm/dot_general | solution.py:144
  255.7 10.3 %exponential_reduce_fusion = f32[4,12,264]{2,1,0:T(8,128)S(1)} fusion(f32[4,12,264,264]{2,3,1,0:T(8,128)} %get-tuple-element.294, f32[4,12,264]{2,1,0:T(8,128)S(1)} %get-tuple-element.293), kind=kLoop, calls=%fused_computation.3 | loop fusion | flops 10023552 | bytes 13483008 | tf_op jit(solution)/shard_map/reduce_sum | solution.py:146
  266.1 10.4 %convolution_convert_fusion.4 = bf16[4,12,64,264]{3,2,1,0:T(8,128)(2,1)S(1)} fusion(bf16[4,264,12,64]{1,3,2,0:T(8,128)(2,1)S(1)} %bitcast.552, f32[4,12,264,264]{2,3,1,0:T(8,128)} %get-tuple-element.294, f32[4,12,264]{2,1,0:T(8,128)S(1)} %log_add_fusion), kind=kOutput, calls=%fused_computation.73 | convolution fusion | flops 439059456 | bytes 16676352 | tf_op jit(solution)/shard_map/ghnm,gmhe->gnhe/dot_general | solution.py:149
  276.5 5.9 multiply_add_fusion.1
  305.3 5.3 collective-permute-done.51
  311.6 10.2 %collective-permute-done.52 = bf16[4,64,768]{2,1,0:T(8,128)(2,1)S(1)} collective-permute-done((bf16[4,64,768]{2,1,0:T(8,128)(2,1)}, bf16[4,64,768]{2,1,0:T(8,128)(2,1)S(1)}, u32[]{:S(2)}, u32[]{:S(2)}) %collective-permute-start.52) | collective-permute-done | bytes 393248 | tf_op jit(solution)/shard_map/ppermute | solution.py:62
  338.7 8.3 %fusion.169 = f32[4,256,3072]{2,1,0:T(8,128)} fusion(f32[4,768]{1,0:T(4,128)S(1)} %get-tuple-element.270, f32[4,768]{1,0:T(4,128)S(1)} %get-tuple-element.271, f32[4,256]{1,0:T(4,128)S(1)} %add_rsqrt_fusion.1, f32[4,256]{1,0:T(4,128)S(1)} %broadcast_multiply_fusion.5, f32[4,264,768]{2,1,0:T(8,128)S(1)} %get-tuple-element.295, ...), kind=kOutput, calls=%fused_computation.520 | convolution fusion | flops 4845207552 | bytes 20480000 | tf_op jit(solution)/shard_map/gnd,df->gnf/dot_general | solution.py:202
  347.0 11.9 %fusion.170 = f32[4,256,768]{2,1,0:T(8,128)S(1)} fusion(bf16[768,1536]{1,0:T(8,128)(2,1)S(1)} %get-tuple-element.186, bf16[768,1536]{1,0:T(8,128)(2,1)S(1)} %copy-done.33, f32[4,256,3072]{2,1,0:T(8,128)} %fusion.169), kind=kOutput, calls=%fused_computation.521 | convolution fusion | flops 4869586944 | bytes 20447232 | tf_op jit(solution)/shard_map/gnf,df->gnd/dot_general | solution.py:205
  361.8 16.9 %fusion.6 = bf16[4,256,3072]{2,1,0:T(8,128)(2,1)} fusion(f32[4,256,3072]{2,1,0:T(8,128)} %fusion.169, f32[4,256,768]{2,1,0:T(8,128)S(1)} %bitcast.562, f32[4,768]{1,0:T(4,128)S(1)} %get-tuple-element.269, bf16[768,1536]{1,0:T(8,128)(2,1)} %copy-done.36, bf16[768,1536]{1,0:T(8,128)(2,1)S(1)} %copy-done.33), kind=kOutput, calls=%fused_computation.13 | convolution fusion | flops 4905762816 | bytes 26750976 | tf_op jit(solution)/shard_map/gnd,df->gnf/dot_general | solution.py:209
  378.7 11.2 %fusion.41 = f32[768,3072,1]{1,0,2:T(8,128)} fusion(f32[4,256,768]{2,1,0:T(8,128)S(1)} %bitcast.563, f32[4,768]{1,0:T(4,128)S(1)} %get-tuple-element.269, f32[4,256,3072]{2,1,0:T(8,128)} %fusion.169), kind=kOutput, calls=%fused_computation.174 | convolution fusion | flops 4861722624 | bytes 25178112 | tf_op jit(solution)/shard_map/gnd,gnf->df/dot_general | solution.py:211
  390.0 7.9 multiply_reduce_fusion.7
  397.8 5.7 fusion.168
  413.0 5.1 bitcast_add_fusion
  425.8 3.3 multiply_add_fusion.2
  434.6 3.3 multiply_reduce_fusion.12
  438.3 3.5 collective-permute-start.58
  441.8 3.3 fusion.28
  445.2 3.4 collective-permute-done.57
  450.2 3.4 collective-permute-done.59
  461.3 5.9 collective-permute-done.60
  467.2 12.3 %collective-permute-done.61 = bf16[4,64,896]{2,1,0:T(8,128)(2,1)S(1)} collective-permute-done((bf16[4,64,896]{2,1,0:T(8,128)(2,1)S(1)}, bf16[4,64,896]{2,1,0:T(8,128)(2,1)S(1)}, u32[]{:S(2)}, u32[]{:S(2)}) %collective-permute-start.61) | collective-permute-done | bytes 458784 | tf_op jit(solution)/shard_map/ppermute | solution.py:62
  484.1 4.0 fusion.44
  498.0 3.1 fusion.29
  503.6 2.9 convolution_convert_fusion.1
  512.3 12.7 %convolution_convert_fusion.3 = bf16[4,12,64,264]{3,2,1,0:T(8,128)(2,1)} fusion(bf16[4,264,12,64]{1,3,2,0:T(8,128)(2,1)} %bitcast.556, f32[4,12,264,264]{2,3,1,0:T(8,128)} %get-tuple-element.294, f32[4,12,264]{2,1,0:T(8,128)S(1)} %copy-done.24), kind=kOutput, calls=%fused_computation.72 | convolution fusion | flops 439059456 | bytes 16676352 | tf_op jit(solution)/shard_map/ghnm,gnhe->gmhe/dot_general | solution.py:181
  525.0 13.3 %multiply_reduce_fusion = (f32[4,12,264]{2,1,0:T(8,128)S(1)}, f32[4,12,264,264]{2,3,1,0:T(8,128)}) fusion(f32[4,12,264,264]{2,3,1,0:T(8,128)} %get-tuple-element.294, f32[4,12,264]{2,1,0:T(8,128)S(1)} %copy-done.24, bf16[4,264,12,64]{1,3,2,0:T(8,128)(2,1)} %bitcast.557, bf16[4,264,12,64]{1,3,2,0:T(8,128)(2,1)S(1)} %bitcast.553), kind=kOutput, calls=%fused_computation.1 | convolution fusion | flops 441581184 | bytes 30108672 | tf_op jit(solution)/shard_map/gnhe,gmhe->ghnm/dot_general | solution.py:172
  538.3 14.1 %multiply_convert_fusion = bf16[4,12,264,264]{2,3,1,0:T(8,128)(2,1)S(1)} fusion(f32[4,12,264,264]{2,3,1,0:T(8,128)} %get-tuple-element.304, f32[4,12,264,264]{2,3,1,0:T(8,128)} %get-tuple-element.294, f32[4,12,264]{2,1,0:T(8,128)S(1)} %get-tuple-element.303, f32[4,12,264]{2,1,0:T(8,128)S(1)} %copy-done.24), kind=kLoop, calls=%fused_computation | loop fusion | flops 16727040 | bytes 33555456 | tf_op jit(solution)/shard_map/convert_element_type | solution.py:174
  552.4 7.0 multiply_convert_fusion.2
  559.4 4.3 multiply_convert_fusion.3
  565.8 8.9 %convolution_bitcast_fusion = f32[768,2304]{1,0:T(8,128)} fusion(bf16[4,264,2304]{1,2,0:T(8,128)(2,1)S(1)} %bitcast.574, f32[4,768]{1,0:T(4,128)S(1)} %copy-done.92, f32[4,768]{1,0:T(4,128)S(1)} %copy-done.88, f32[4,264]{1,0:T(4,128)S(1)} %copy-done.90, f32[4,264]{1,0:T(4,128)S(1)} %copy-done.76, f32[4,8,768]{2,1,0:T(8,128)S(1)} %copy-done.28, ...), kind=kOutput, calls=%fused_computation.24 | convolution fusion | flops 3741990912 | bytes 15220992 | tf_op jit(solution)/shard_map/gnd,gnk->dk/dot_general | solution.py:191
  574.7 7.1 multiply_reduce_fusion.3
  594.9 3.4 slice.493
  613.7 3.0 collective-permute-done.69
  617.8 4.7 collective-permute-done.70
  624.5 4.4 collective-permute-done.71
  648.1 3.5 all-to-all-start
  652.7 4.0 fusion.25
  669.5 5.9 collective-permute-done.83
  687.8 4.9 collective-permute-done.87
  696.3 8.4 %collective-permute-done.74 = bf16[2,2,48,1152]{3,2,0,1:T(8,128)(2,1)S(1)} collective-permute-done((bf16[2,2,48,1152]{3,2,0,1:T(8,128)(2,1)S(1)}, bf16[2,2,48,1152]{3,2,0,1:T(8,128)(2,1)S(1)}, u32[]{:S(2)}, u32[]{:S(2)}) %collective-permute-start.74) | collective-permute-done | bytes 442400 | tf_op jit(solution)/shard_map/ppermute | solution.py:62
  708.6 7.4 maximum_select_fusion
  716.7 8.9 %fusion.8 = bf16[768,3072]{1,0:T(8,128)(2,1)} fusion(f32[768,1536]{1,0:T(8,128)} %slice.405, f32[768,1536]{1,0:T(8,128)} %slice.404, bf16[768,3072]{1,0:T(8,128)(2,1)} %collective-permute-done.89), kind=kLoop, calls=%fused_computation.17 | loop fusion | flops 9437184 | bytes 18874368 | tf_op jit(solution)/shard_map/convert_element_type | solution.py:394
  730.8 4.4 collective-permute-start.78
  740.3 3.0 collective-permute-done.79
  744.0 11.0 %collective-permute-done.90 = bf16[2,2,48,3072]{3,2,0,1:T(8,128)(2,1)S(1)} collective-permute-done((bf16[2,2,48,3072]{3,2,0,1:T(8,128)(2,1)S(1)}, bf16[2,2,48,3072]{3,2,0,1:T(8,128)(2,1)S(1)}, u32[]{:S(2)}, u32[]{:S(2)}) %collective-permute-start.90) | collective-permute-done | bytes 1179680 | tf_op jit(solution)/shard_map/ppermute | solution.py:62
  757.0 11.4 %collective-permute-done.92 = bf16[2,2,48,3072]{3,2,0,1:T(8,128)(2,1)S(1)} collective-permute-done((bf16[2,2,48,3072]{3,2,0,1:T(8,128)(2,1)S(1)}, bf16[2,2,48,3072]{3,2,0,1:T(8,128)(2,1)S(1)}, u32[]{:S(2)}, u32[]{:S(2)}) %collective-permute-start.92) | collective-permute-done | bytes 1179680 | tf_op jit(solution)/shard_map/ppermute | solution.py:62
  769.7 6.2 collective-permute-done.91
  783.3 5.1 maximum_select_fusion.1
  788.9 9.0 %collective-permute-done.95 = bf16[48,3072]{1,0:T(8,128)(2,1)S(1)} collective-permute-done((bf16[48,3072]{1,0:T(8,128)(2,1)S(1)}, bf16[48,3072]{1,0:T(8,128)(2,1)S(1)}, u32[]{:S(2)}, u32[]{:S(2)}) %collective-permute-start.95) | collective-permute-done | bytes 294944 | tf_op jit(solution)/shard_map/ppermute | solution.py:65
  (718 shorter events, 347.7 us)
Async XLA Ops:
  3.6 43.8 %collective-permute-start.1 = (bf16[9,768]{1,0:T(8,128)(2,1)}, bf16[9,768]{1,0:T(8,128)(2,1)}, u32[]{:S(2)}, u32[]{:S(2)}) collective-permute-start(bf16[9,768]{1,0:T(8,128)(2,1)} %get-tuple-element.281), channel_id=1, source_target_pairs={{0,16},{2,18},{4,20},{6,22},{8,24},{10,26},{12,28},{14,30},{16,0},... | collective-permute-start | bytes 41480 | tf_op jit(solution)/shard_map/ppermute | solution.py:65
  7.6 40.6 %collective-permute-start = (bf16[9,768]{1,0:T(8,128)(2,1)}, bf16[9,768]{1,0:T(8,128)(2,1)}, u32[]{:S(2)}, u32[]{:S(2)}) collective-permute-start(bf16[9,768]{1,0:T(8,128)(2,1)} %get-tuple-element.281), channel_id=1, source_target_pairs={{0,8},{2,10},{4,12},{6,14},{8,16},{10,18},{12,20},{14,22},{16,24},... | collective-permute-start | bytes 41480 | tf_op jit(solution)/shard_map/ppermute | solution.py:65
  9.2 39.8 %collective-permute-start.2 = (bf16[9,768]{1,0:T(8,128)(2,1)}, bf16[9,768]{1,0:T(8,128)(2,1)}, u32[]{:S(2)}, u32[]{:S(2)}) collective-permute-start(bf16[9,768]{1,0:T(8,128)(2,1)} %get-tuple-element.281), channel_id=1, source_target_pairs={{0,24},{2,26},{4,28},{6,30},{8,0},{10,2},{12,4},{14,6},{16,8},{18,... | collective-permute-start | bytes 41480 | tf_op jit(solution)/shard_map/ppermute | solution.py:65
  13.1 78.9 %collective-permute-start.16 = (bf16[48,1152]{1,0:T(8,128)(2,1)}, bf16[48,1152]{1,0:T(8,128)(2,1)}, u32[]{:S(2)}, u32[]{:S(2)}) collective-permute-start(bf16[48,1152]{1,0:T(8,128)(2,1)} %bitcast.257), channel_id=1, source_target_pairs={{0,24},{2,26},{4,28},{6,30},{8,0},{10,2},{12,4},{14,6},{16,8},{18,... | collective-permute-start | bytes 331784 | tf_op jit(solution)/shard_map/ppermute | solution.py:65
  13.1 75.3 %collective-permute-start.15 = (bf16[48,1152]{1,0:T(8,128)(2,1)}, bf16[48,1152]{1,0:T(8,128)(2,1)}, u32[]{:S(2)}, u32[]{:S(2)}) collective-permute-start(bf16[48,1152]{1,0:T(8,128)(2,1)} %bitcast.257), channel_id=1, source_target_pairs={{0,16},{2,18},{4,20},{6,22},{8,24},{10,26},{12,28},{14,30},{16,0},... | collective-permute-start | bytes 331784 | tf_op jit(solution)/shard_map/ppermute | solution.py:65
  53.2 11.9 %collective-permute-start.3 = (bf16[4,9,768]{2,0,1:T(4,128)(2,1)S(1)}, bf16[4,9,768]{2,0,1:T(4,128)(2,1)S(1)}, u32[]{:S(2)}, u32[]{:S(2)}) collective-permute-start(bf16[4,9,768]{2,0,1:T(4,128)(2,1)S(1)} %dynamic_update_slice.146), channel_id=1, source_target_pairs={{0,2},{2,0},{4,6},{6,4},{8,10},{10,8},{12,14},{14,12},{16,18},{18,... | collective-permute-start | bytes 165896 | tf_op jit(solution)/shard_map/ppermute | solution.py:62
  58.7 26.2 %collective-permute-start.14 = (bf16[48,1152]{1,0:T(8,128)(2,1)}, bf16[48,1152]{1,0:T(8,128)(2,1)}, u32[]{:S(2)}, u32[]{:S(2)}) collective-permute-start(bf16[48,1152]{1,0:T(8,128)(2,1)} %bitcast.257), channel_id=1, source_target_pairs={{0,8},{2,10},{4,12},{6,14},{8,16},{10,18},{12,20},{14,22},{16,24},... | collective-permute-start | bytes 331784 | tf_op jit(solution)/shard_map/ppermute | solution.py:65
  60.4 47.8 %collective-permute-start.24 = (bf16[48,1920]{1,0:T(8,128)(2,1)}, bf16[48,1920]{1,0:T(8,128)(2,1)}, u32[]{:S(2)}, u32[]{:S(2)}) collective-permute-start(bf16[48,1920]{1,0:T(8,128)(2,1)} %pad_maximum_fusion.16), channel_id=1, source_target_pairs={{0,24},{2,26},{4,28},{6,30},{8,0},{10,2},{12,4},{14,6},{16,8},{18,... | collective-permute-start | bytes 552968 | tf_op jit(solution)/shard_map/ppermute | solution.py:65
  65.1 40.0 %collective-permute-start.23 = (bf16[48,1920]{1,0:T(8,128)(2,1)}, bf16[48,1920]{1,0:T(8,128)(2,1)}, u32[]{:S(2)}, u32[]{:S(2)}) collective-permute-start(bf16[48,1920]{1,0:T(8,128)(2,1)} %pad_maximum_fusion.16), channel_id=1, source_target_pairs={{0,16},{2,18},{4,20},{6,22},{8,24},{10,26},{12,28},{14,30},{16,0},... | collective-permute-start | bytes 552968 | tf_op jit(solution)/shard_map/ppermute | solution.py:65
  84.9 10.9 %collective-permute-start.22 = (bf16[48,1920]{1,0:T(8,128)(2,1)}, bf16[48,1920]{1,0:T(8,128)(2,1)S(1)}, u32[]{:S(2)}, u32[]{:S(2)}) collective-permute-start(bf16[48,1920]{1,0:T(8,128)(2,1)} %pad_maximum_fusion.16), channel_id=1, source_target_pairs={{0,8},{2,10},{4,12},{6,14},{8,16},{10,18},{12,20},{14,22},{16,24},... | collective-permute-start | bytes 552968 | tf_op jit(solution)/shard_map/ppermute | solution.py:65
  88.4 55.1 %collective-permute-start.40 = (bf16[48,3072]{1,0:T(8,128)(2,1)}, bf16[48,3072]{1,0:T(8,128)(2,1)S(1)}, u32[]{:S(2)}, u32[]{:S(2)}) collective-permute-start(bf16[48,3072]{1,0:T(8,128)(2,1)} %pad_maximum_fusion.14), channel_id=1, source_target_pairs={{0,24},{2,26},{4,28},{6,30},{8,0},{10,2},{12,4},{14,6},{16,8},{18,... | collective-permute-start | bytes 884744 | tf_op jit(solution)/shard_map/ppermute | solution.py:65
  91.9 50.9 %collective-permute-start.39 = (bf16[48,3072]{1,0:T(8,128)(2,1)}, bf16[48,3072]{1,0:T(8,128)(2,1)S(1)}, u32[]{:S(2)}, u32[]{:S(2)}) collective-permute-start(bf16[48,3072]{1,0:T(8,128)(2,1)} %pad_maximum_fusion.14), channel_id=1, source_target_pairs={{0,16},{2,18},{4,20},{6,22},{8,24},{10,26},{12,28},{14,30},{16,0},... | collective-permute-start | bytes 884744 | tf_op jit(solution)/shard_map/ppermute | solution.py:65
  95.9 42.4 %collective-permute-start.38 = (bf16[48,3072]{1,0:T(8,128)(2,1)}, bf16[48,3072]{1,0:T(8,128)(2,1)S(1)}, u32[]{:S(2)}, u32[]{:S(2)}) collective-permute-start(bf16[48,3072]{1,0:T(8,128)(2,1)} %pad_maximum_fusion.14), channel_id=1, source_target_pairs={{0,8},{2,10},{4,12},{6,14},{8,16},{10,18},{12,20},{14,22},{16,24},... | collective-permute-start | bytes 884744 | tf_op jit(solution)/shard_map/ppermute | solution.py:65
  117.8 39.7 %collective-permute-start.19 = (bf16[2,48,1152]{2,1,0:T(8,128)(2,1)S(1)}, bf16[2,48,1152]{2,1,0:T(8,128)(2,1)S(1)}, u32[]{:S(2)}, u32[]{:S(2)}) collective-permute-start(bf16[2,48,1152]{2,1,0:T(8,128)(2,1)S(1)} %get-tuple-element.250), channel_id=1, source_target_pairs={{0,4},{2,6},{4,0},{6,2},{8,12},{10,14},{12,8},{14,10},{16,20},{18,... | collective-permute-start | bytes 663560 | tf_op jit(solution)/shard_map/ppermute | solution.py:62
  137.8 20.6 %collective-permute-start.17 = (bf16[2,48,1152]{2,1,0:T(8,128)(2,1)S(1)}, bf16[2,48,1152]{2,1,0:T(8,128)(2,1)S(1)}, u32[]{:S(2)}, u32[]{:S(2)}) collective-permute-start(bf16[2,48,1152]{2,1,0:T(8,128)(2,1)S(1)} %get-tuple-element.251), channel_id=1, source_target_pairs={{0,2},{2,0},{4,6},{6,4},{8,10},{10,8},{12,14},{14,12},{16,18},{18,... | collective-permute-start | bytes 663560 | tf_op jit(solution)/shard_map/ppermute | solution.py:62
  138.3 9.8 %collective-permute-start.10 = (f32[8,1152]{1,0:T(8,128)S(1)}, f32[8,1152]{1,0:T(8,128)S(1)}, u32[]{:S(2)}, u32[]{:S(2)}) collective-permute-start(f32[8,1152]{1,0:T(8,128)S(1)} %get-tuple-element.261), channel_id=1, source_target_pairs={{0,8},{2,10},{4,12},{6,14},{8,16},{10,18},{12,20},{14,22},{16,24},... | collective-permute-start | bytes 110600 | tf_op jit(solution)/shard_map/ppermute | solution.py:65
  154.0 9.7 %collective-permute-start.27 = (bf16[2,48,1920]{2,1,0:T(8,128)(2,1)S(1)}, bf16[2,48,1920]{2,1,0:T(8,128)(2,1)S(1)}, u32[]{:S(2)}, u32[]{:S(2)}) collective-permute-start(bf16[2,48,1920]{2,1,0:T(8,128)(2,1)S(1)} %get-tuple-element.231), channel_id=1, source_target_pairs={{0,4},{2,6},{4,0},{6,2},{8,12},{10,14},{12,8},{14,10},{16,20},{18,... | collective-permute-start | bytes 1105928 | tf_op jit(solution)/shard_map/ppermute | solution.py:62
  156.0 27.0 %collective-permute-start.43 = (bf16[2,48,3072]{2,1,0:T(8,128)(2,1)S(1)}, bf16[2,48,3072]{2,1,0:T(8,128)(2,1)S(1)}, u32[]{:S(2)}, u32[]{:S(2)}) collective-permute-start(bf16[2,48,3072]{2,1,0:T(8,128)(2,1)S(1)} %get-tuple-element.214), channel_id=1, source_target_pairs={{0,4},{2,6},{4,0},{6,2},{8,12},{10,14},{12,8},{14,10},{16,20},{18,... | collective-permute-start | bytes 1769480 | tf_op jit(solution)/shard_map/ppermute | solution.py:62
  157.5 24.1 %collective-permute-start.41 = (bf16[2,48,3072]{2,1,0:T(8,128)(2,1)S(1)}, bf16[2,48,3072]{2,1,0:T(8,128)(2,1)S(1)}, u32[]{:S(2)}, u32[]{:S(2)}) collective-permute-start(bf16[2,48,3072]{2,1,0:T(8,128)(2,1)S(1)} %get-tuple-element.215), channel_id=1, source_target_pairs={{0,2},{2,0},{4,6},{6,4},{8,10},{10,8},{12,14},{14,12},{16,18},{18,... | collective-permute-start | bytes 1769480 | tf_op jit(solution)/shard_map/ppermute | solution.py:62
  160.8 20.6 %collective-permute-start.18 = (bf16[2,2,48,1152]{3,2,0,1:T(8,128)(2,1)S(1)}, bf16[2,2,48,1152]{3,2,0,1:T(8,128)(2,1)S(1)}, u32[]{:S(2)}, u32[]{:S(2)}) collective-permute-start(bf16[2,2,48,1152]{3,2,0,1:T(8,128)(2,1)S(1)} %maximum_select_fusion.16), channel_id=1, source_target_pairs={{0,4},{2,6},{4,0},{6,2},{8,12},{10,14},{12,8},{14,10},{16,20},{18,... | collective-permute-start | bytes 1327112 | tf_op jit(solution)/shard_map/ppermute | solution.py:62
  162.4 17.3 %collective-permute-start.20 = (bf16[2,2,48,1152]{3,2,1,0:T(8,128)(2,1)S(1)}, bf16[2,2,48,1152]{3,2,1,0:T(8,128)(2,1)S(1)}, u32[]{:S(2)}, u32[]{:S(2)}) collective-permute-start(bf16[2,2,48,1152]{3,2,1,0:T(8,128)(2,1)S(1)} %maximum_select_fusion.17), channel_id=1, source_target_pairs={{0,2},{2,0},{4,6},{6,4},{8,10},{10,8},{12,14},{14,12},{16,18},{18,... | collective-permute-start | bytes 1327112 | tf_op jit(solution)/shard_map/ppermute | solution.py:62
  163.6 35.8 %collective-permute-start.26 = (bf16[2,2,48,1920]{3,2,0,1:T(8,128)(2,1)S(1)}, bf16[2,2,48,1920]{3,2,0,1:T(8,128)(2,1)S(1)}, u32[]{:S(2)}, u32[]{:S(2)}) collective-permute-start(bf16[2,2,48,1920]{3,2,0,1:T(8,128)(2,1)S(1)} %maximum_select_fusion.13), channel_id=1, source_target_pairs={{0,4},{2,6},{4,0},{6,2},{8,12},{10,14},{12,8},{14,10},{16,20},{18,... | collective-permute-start | bytes 2211848 | tf_op jit(solution)/shard_map/ppermute | solution.py:62
  179.7 19.4 %collective-permute-start.28 = (bf16[2,2,48,1920]{3,2,1,0:T(8,128)(2,1)S(1)}, bf16[2,2,48,1920]{3,2,1,0:T(8,128)(2,1)S(1)}, u32[]{:S(2)}, u32[]{:S(2)}) collective-permute-start(bf16[2,2,48,1920]{3,2,1,0:T(8,128)(2,1)S(1)} %maximum_select_fusion.14), channel_id=1, source_target_pairs={{0,2},{2,0},{4,6},{6,4},{8,10},{10,8},{12,14},{14,12},{16,18},{18,... | collective-permute-start | bytes 2211848 | tf_op jit(solution)/shard_map/ppermute | solution.py:62
  181.6 45.4 %collective-permute-start.21 = (bf16[768,1152]{1,0:T(8,128)(2,1)S(1)}, bf16[768,1152]{1,0:T(8,128)(2,1)S(1)}, u32[]{:S(2)}, u32[]{:S(2)}) collective-permute-start(bf16[768,1152]{1,0:T(8,128)(2,1)S(1)} %bitcast.600), channel_id=1, source_target_pairs={{0,1},{1,0},{2,3},{3,2},{4,5},{5,4},{6,7},{7,6},{8,9},{9,8},{10,11... | collective-permute-start | bytes 5308424 | tf_op jit(solution)/shard_map/ppermute | solution.py:52
  181.9 37.8 %collective-permute-start.42 = (bf16[2,2,48,3072]{3,2,0,1:T(8,128)(2,1)S(1)}, bf16[2,2,48,3072]{3,2,0,1:T(8,128)(2,1)S(1)}, u32[]{:S(2)}, u32[]{:S(2)}) collective-permute-start(bf16[2,2,48,3072]{3,2,0,1:T(8,128)(2,1)S(1)} %maximum_select_fusion.7), channel_id=1, source_target_pairs={{0,4},{2,6},{4,0},{6,2},{8,12},{10,14},{12,8},{14,10},{16,20},{18,... | collective-permute-start | bytes 3538952 | tf_op jit(solution)/shard_map/ppermute | solution.py:62
  183.2 36.2 %collective-permute-start.44 = (bf16[2,2,48,3072]{3,2,1,0:T(8,128)(2,1)S(1)}, bf16[2,2,48,3072]{3,2,1,0:T(8,128)(2,1)S(1)}, u32[]{:S(2)}, u32[]{:S(2)}) collective-permute-start(bf16[2,2,48,3072]{3,2,1,0:T(8,128)(2,1)S(1)} %maximum_select_fusion.8), channel_id=1, source_target_pairs={{0,2},{2,0},{4,6},{6,4},{8,10},{10,8},{12,14},{14,12},{16,18},{18,... | collective-permute-start | bytes 3538952 | tf_op jit(solution)/shard_map/ppermute | solution.py:62
  200.7 75.8 %collective-permute-start.29 = (bf16[768,384]{1,0:T(8,128)(2,1)}, bf16[768,384]{1,0:T(8,128)(2,1)}, u32[]{:S(2)}, u32[]{:S(2)}) collective-permute-start(bf16[768,384]{1,0:T(8,128)(2,1)} %slice.356), channel_id=1, source_target_pairs={{0,1},{1,0},{2,3},{3,2},{4,5},{5,4},{6,7},{7,6},{8,9},{9,8},{10,11... | collective-permute-start | bytes 1769480 | tf_op jit(solution)/shard_map/ppermute | solution.py:52
  222.2 113.4 %collective-permute-start.45 = (bf16[768,3072]{1,0:T(8,128)(2,1)}, bf16[768,3072]{1,0:T(8,128)(2,1)}, u32[]{:S(2)}, u32[]{:S(2)}) collective-permute-start(bf16[768,3072]{1,0:T(8,128)(2,1)} %bitcast.92), channel_id=1, source_target_pairs={{0,1},{1,0},{2,3},{3,2},{4,5},{5,4},{6,7},{7,6},{8,9},{9,8},{10,11... | collective-permute-start | bytes 14155784 | tf_op jit(solution)/shard_map/ppermute | solution.py:52
  286.2 9.8 %collective-permute-start.49 = (bf16[64,768]{1,0:T(8,128)(2,1)S(1)}, bf16[64,768]{1,0:T(8,128)(2,1)S(1)}, u32[]{:S(2)}, u32[]{:S(2)}) collective-permute-start(bf16[64,768]{1,0:T(8,128)(2,1)S(1)} %slice.370), channel_id=1, source_target_pairs={{0,16},{2,18},{4,20},{6,22},{8,24},{10,26},{12,28},{14,30},{16,0},... | collective-permute-start | bytes 294920 | tf_op jit(solution)/shard_map/ppermute | solution.py:65
  298.3 12.4 %collective-permute-start.51 = (bf16[4,64,768]{2,1,0:T(8,128)(2,1)}, bf16[4,64,768]{2,1,0:T(8,128)(2,1)}, u32[]{:S(2)}, u32[]{:S(2)}) collective-permute-start(bf16[4,64,768]{2,1,0:T(8,128)(2,1)} %bitcast_dynamic-update-slice_fusion.24), channel_id=1, source_target_pairs={{0,2},{2,0},{4,6},{6,4},{8,10},{10,8},{12,14},{14,12},{16,18},{18,... | collective-permute-start | bytes 1179656 | tf_op jit(solution)/shard_map/ppermute | solution.py:62
  302.2 19.7 %collective-permute-start.53 = (bf16[4,64,768]{2,1,0:T(8,128)(2,1)}, bf16[4,64,768]{2,1,0:T(8,128)(2,1)S(1)}, u32[]{:S(2)}, u32[]{:S(2)}) collective-permute-start(bf16[4,64,768]{2,1,0:T(8,128)(2,1)} %bitcast_dynamic-update-slice_fusion.24), channel_id=1, source_target_pairs={{0,6},{2,4},{4,2},{6,0},{8,14},{10,12},{12,10},{14,8},{16,22},{18,... | collective-permute-start | bytes 1179656 | tf_op jit(solution)/shard_map/ppermute | solution.py:62
  303.1 18.7 %collective-permute-start.52 = (bf16[4,64,768]{2,1,0:T(8,128)(2,1)}, bf16[4,64,768]{2,1,0:T(8,128)(2,1)S(1)}, u32[]{:S(2)}, u32[]{:S(2)}) collective-permute-start(bf16[4,64,768]{2,1,0:T(8,128)(2,1)} %bitcast_dynamic-update-slice_fusion.24), channel_id=1, source_target_pairs={{0,4},{2,6},{4,0},{6,2},{8,12},{10,14},{12,8},{14,10},{16,20},{18,... | collective-permute-start | bytes 1179656 | tf_op jit(solution)/shard_map/ppermute | solution.py:62
  425.4 31.6 %collective-permute-start.55 = (f32[4,8,768]{2,1,0:T(8,128)}, f32[4,8,768]{2,1,0:T(8,128)}, u32[]{:S(2)}, u32[]{:S(2)}) collective-permute-start(f32[4,8,768]{2,1,0:T(8,128)} %get-tuple-element.257), channel_id=1, source_target_pairs={{0,1},{1,0},{2,3},{3,2},{4,5},{5,4},{6,7},{7,6},{8,9},{9,8},{10,11... | collective-permute-start | bytes 294920 | tf_op jit(solution)/shard_map/ppermute | solution.py:52
  429.1 279.5 %collective-permute-start.46 = (f32[4,256,768]{2,1,0:T(8,128)}, f32[4,256,768]{2,1,0:T(8,128)}, u32[]{:S(2)}, u32[]{:S(2)}) collective-permute-start(f32[4,256,768]{2,1,0:T(8,128)} %get-tuple-element.190), channel_id=1, source_target_pairs={{0,1},{1,0},{2,3},{3,2},{4,5},{5,4},{6,7},{7,6},{8,9},{9,8},{10,11... | collective-permute-start | bytes 9437192 | tf_op jit(solution)/shard_map/ppermute | solution.py:52
  432.1 284.6 %collective-permute-start.89 = (bf16[768,3072]{1,0:T(8,128)(2,1)}, bf16[768,3072]{1,0:T(8,128)(2,1)}, u32[]{:S(2)}, u32[]{:S(2)}) collective-permute-start(bf16[768,3072]{1,0:T(8,128)(2,1)} %pad_maximum_fusion.2), channel_id=1, source_target_pairs={{0,1},{1,0},{2,3},{3,2},{4,5},{5,4},{6,7},{7,6},{8,9},{9,8},{10,11... | collective-permute-start | bytes 14155784 | tf_op jit(solution)/shard_map/ppermute | solution.py:52
  438.3 11.8 %collective-permute-start.58 = (bf16[64,896]{1,0:T(8,128)(2,1)S(1)}, bf16[64,896]{1,0:T(8,128)(2,1)S(1)}, u32[]{:S(2)}, u32[]{:S(2)}) collective-permute-start(bf16[64,896]{1,0:T(8,128)(2,1)S(1)} %fusion.88), channel_id=1, source_target_pairs={{0,16},{2,18},{4,20},{6,22},{8,24},{10,26},{12,28},{14,30},{16,0},... | collective-permute-start | bytes 344072 | tf_op jit(solution)/shard_map/ppermute | solution.py:65
  453.6 13.5 %collective-permute-start.60 = (bf16[4,64,896]{2,1,0:T(8,128)(2,1)S(1)}, bf16[4,64,896]{2,1,0:T(8,128)(2,1)S(1)}, u32[]{:S(2)}, u32[]{:S(2)}) collective-permute-start(bf16[4,64,896]{2,1,0:T(8,128)(2,1)S(1)} %bitcast_dynamic-update-slice_fusion.17), channel_id=1, source_target_pairs={{0,2},{2,0},{4,6},{6,4},{8,10},{10,8},{12,14},{14,12},{16,18},{18,... | collective-permute-start | bytes 1376264 | tf_op jit(solution)/shard_map/ppermute | solution.py:62
  458.8 20.8 %collective-permute-start.62 = (bf16[4,64,896]{2,1,0:T(8,128)(2,1)S(1)}, bf16[4,64,896]{2,1,0:T(8,128)(2,1)S(1)}, u32[]{:S(2)}, u32[]{:S(2)}) collective-permute-start(bf16[4,64,896]{2,1,0:T(8,128)(2,1)S(1)} %bitcast_dynamic-update-slice_fusion.17), channel_id=1, source_target_pairs={{0,6},{2,4},{4,2},{6,0},{8,14},{10,12},{12,10},{14,8},{16,22},{18,... | collective-permute-start | bytes 1376264 | tf_op jit(solution)/shard_map/ppermute | solution.py:62
  460.0 19.5 %collective-permute-start.61 = (bf16[4,64,896]{2,1,0:T(8,128)(2,1)S(1)}, bf16[4,64,896]{2,1,0:T(8,128)(2,1)S(1)}, u32[]{:S(2)}, u32[]{:S(2)}) collective-permute-start(bf16[4,64,896]{2,1,0:T(8,128)(2,1)S(1)} %bitcast_dynamic-update-slice_fusion.17), channel_id=1, source_target_pairs={{0,4},{2,6},{4,0},{6,2},{8,12},{10,14},{12,8},{14,10},{16,20},{18,... | collective-permute-start | bytes 1376264 | tf_op jit(solution)/shard_map/ppermute | solution.py:62
  585.2 14.6 %collective-permute-start.67 = (bf16[5,4608]{1,0:T(8,128)(2,1)}, bf16[5,4608]{1,0:T(8,128)(2,1)}, u32[]{:S(2)}, u32[]{:S(2)}) collective-permute-start(bf16[5,4608]{1,0:T(8,128)(2,1)} %get-tuple-element.267), channel_id=1, source_target_pairs={{0,16},{2,18},{4,20},{6,22},{8,24},{10,26},{12,28},{14,30},{16,0},... | collective-permute-start | bytes 138248 | tf_op jit(solution)/shard_map/ppermute | solution.py:65
  586.8 14.0 %collective-permute-start.66 = (bf16[5,4608]{1,0:T(8,128)(2,1)}, bf16[5,4608]{1,0:T(8,128)(2,1)}, u32[]{:S(2)}, u32[]{:S(2)}) collective-permute-start(bf16[5,4608]{1,0:T(8,128)(2,1)} %get-tuple-element.267), channel_id=1, source_target_pairs={{0,8},{2,10},{4,12},{6,14},{8,16},{10,18},{12,20},{14,22},{16,24},... | collective-permute-start | bytes 138248 | tf_op jit(solution)/shard_map/ppermute | solution.py:65
  588.7 14.3 %collective-permute-start.68 = (bf16[5,4608]{1,0:T(8,128)(2,1)}, bf16[5,4608]{1,0:T(8,128)(2,1)}, u32[]{:S(2)}, u32[]{:S(2)}) collective-permute-start(bf16[5,4608]{1,0:T(8,128)(2,1)} %get-tuple-element.267), channel_id=1, source_target_pairs={{0,24},{2,26},{4,28},{6,30},{8,0},{10,2},{12,4},{14,6},{16,8},{18,... | collective-permute-start | bytes 138248 | tf_op jit(solution)/shard_map/ppermute | solution.py:65
  599.8 31.6 %collective-permute-start.81 = (bf16[768,384]{0,1:T(8,128)(2,1)}, bf16[768,384]{0,1:T(8,128)(2,1)}, u32[]{:S(2)}, u32[]{:S(2)}) collective-permute-start(bf16[768,384]{0,1:T(8,128)(2,1)} %slice.494), channel_id=1, source_target_pairs={{0,1},{1,0},{2,3},{3,2},{4,5},{5,4},{6,7},{7,6},{8,9},{9,8},{10,11... | collective-permute-start | bytes 1769480 | tf_op jit(solution)/shard_map/ppermute | solution.py:52
  600.8 11.2 %collective-permute-start.65 = (f32[4,8,768]{2,1,0:T(8,128)S(1)}, f32[4,8,768]{2,1,0:T(8,128)}, u32[]{:S(2)}, u32[]{:S(2)}) collective-permute-start(f32[4,8,768]{2,1,0:T(8,128)S(1)} %slice.387), channel_id=1, source_target_pairs={{0,1},{1,0},{2,3},{3,2},{4,5},{5,4},{6,7},{7,6},{8,9},{9,8},{10,11... | collective-permute-start | bytes 294920 | tf_op jit(solution)/shard_map/ppermute | solution.py:52
  612.0 70.0 %collective-permute-start.73 = (bf16[768,1152]{1,0:T(8,128)(2,1)}, bf16[768,1152]{1,0:T(8,128)(2,1)}, u32[]{:S(2)}, u32[]{:S(2)}) collective-permute-start(bf16[768,1152]{1,0:T(8,128)(2,1)} %slice.493), channel_id=1, source_target_pairs={{0,1},{1,0},{2,3},{3,2},{4,5},{5,4},{6,7},{7,6},{8,9},{9,8},{10,11... | collective-permute-start | bytes 5308424 | tf_op jit(solution)/shard_map/ppermute | solution.py:52
  631.4 11.1 %collective-permute-start.72 = (bf16[16,5,4608]{2,0,1:T(8,128)(2,1)}, bf16[16,5,4608]{2,0,1:T(8,128)(2,1)}, u32[]{:S(2)}, u32[]{:S(2)}) collective-permute-start(bf16[16,5,4608]{2,0,1:T(8,128)(2,1)} %copy.856), channel_id=1, source_target_pairs={{0,1},{1,0},{2,3},{3,2},{4,5},{5,4},{6,7},{7,6},{8,9},{9,8},{10,11... | collective-permute-start | bytes 2211848 | tf_op jit(solution)/shard_map/ppermute | solution.py:52
  641.6 22.6 %collective-permute-start.82 = (bf16[2,2,48,1920]{3,2,0,1:T(8,128)(2,1)}, bf16[2,2,48,1920]{3,2,0,1:T(8,128)(2,1)}, u32[]{:S(2)}, u32[]{:S(2)}) collective-permute-start(bf16[2,2,48,1920]{3,2,0,1:T(8,128)(2,1)} %bitcast.537), channel_id=1, source_target_pairs={{0,4},{2,6},{4,0},{6,2},{8,12},{10,14},{12,8},{14,10},{16,20},{18,... | collective-permute-start | bytes 2211848 | tf_op jit(solution)/shard_map/ppermute | solution.py:62
  642.5 24.8 %collective-permute-start.84 = (bf16[2,2,48,1920]{3,2,0,1:T(8,128)(2,1)}, bf16[2,2,48,1920]{3,2,0,1:T(8,128)(2,1)}, u32[]{:S(2)}, u32[]{:S(2)}) collective-permute-start(bf16[2,2,48,1920]{3,2,0,1:T(8,128)(2,1)} %bitcast.536), channel_id=1, source_target_pairs={{0,2},{2,0},{4,6},{6,4},{8,10},{10,8},{12,14},{14,12},{16,18},{18,... | collective-permute-start | bytes 2211848 | tf_op jit(solution)/shard_map/ppermute | solution.py:62
  648.1 14.0 %all-to-all-start = ((f32[16,1,384]{2,1,0:T(1,128)}), f32[16,1,384]{2,1,0:T(1,128)S(1)}, u32[]{:S(2)}, u32[]{:S(2)}) async-start(f32[16,1,384]{2,1,0:T(1,128)} %reshape.994), calls=%async_computation | async-start | bytes 49152 | tf_op jit(solution)/shard_map/all_to_all | solution.py:131
  665.7 9.7 %collective-permute-start.83 = (bf16[2,48,1920]{2,1,0:T(8,128)(2,1)S(1)}, bf16[2,48,1920]{2,1,0:T(8,128)(2,1)S(1)}, u32[]{:S(2)}, u32[]{:S(2)}) collective-permute-start(bf16[2,48,1920]{2,1,0:T(8,128)(2,1)S(1)} %dynamic-slice_bitcast_fusion.3), channel_id=1, source_target_pairs={{0,2},{2,0},{4,6},{6,4},{8,10},{10,8},{12,14},{14,12},{16,18},{18,... | collective-permute-start | bytes 1105928 | tf_op jit(solution)/shard_map/ppermute | solution.py:62
  678.4 9.5 %collective-permute-start.86 = (bf16[48,1920]{1,0:T(8,128)(2,1)S(1)}, bf16[48,1920]{1,0:T(8,128)(2,1)S(1)}, u32[]{:S(2)}, u32[]{:S(2)}) collective-permute-start(bf16[48,1920]{1,0:T(8,128)(2,1)S(1)} %get-tuple-element.224), channel_id=1, source_target_pairs={{0,8},{2,10},{4,12},{6,14},{8,16},{10,18},{12,20},{14,22},{16,24},... | collective-permute-start | bytes 552968 | tf_op jit(solution)/shard_map/ppermute | solution.py:65
  679.6 13.2 %collective-permute-start.87 = (bf16[48,1920]{1,0:T(8,128)(2,1)S(1)}, bf16[48,1920]{1,0:T(8,128)(2,1)S(1)}, u32[]{:S(2)}, u32[]{:S(2)}) collective-permute-start(bf16[48,1920]{1,0:T(8,128)(2,1)S(1)} %get-tuple-element.225), channel_id=1, source_target_pairs={{0,16},{2,18},{4,20},{6,22},{8,24},{10,26},{12,28},{14,30},{16,0},... | collective-permute-start | bytes 552968 | tf_op jit(solution)/shard_map/ppermute | solution.py:65
  682.0 12.2 %collective-permute-start.88 = (bf16[48,1920]{1,0:T(8,128)(2,1)S(1)}, bf16[48,1920]{1,0:T(8,128)(2,1)S(1)}, u32[]{:S(2)}, u32[]{:S(2)}) collective-permute-start(bf16[48,1920]{1,0:T(8,128)(2,1)S(1)} %get-tuple-element.226), channel_id=1, source_target_pairs={{0,24},{2,26},{4,28},{6,30},{8,0},{10,2},{12,4},{14,6},{16,8},{18,... | collective-permute-start | bytes 552968 | tf_op jit(solution)/shard_map/ppermute | solution.py:65
  687.8 95.5 %collective-permute-start.64 = (f32[4,256,768]{2,1,0:T(8,128)S(1)}, f32[4,256,768]{2,1,0:T(8,128)}, u32[]{:S(2)}, u32[]{:S(2)}) collective-permute-start(f32[4,256,768]{2,1,0:T(8,128)S(1)} %slice.386), channel_id=1, source_target_pairs={{0,1},{1,0},{2,3},{3,2},{4,5},{5,4},{6,7},{7,6},{8,9},{9,8},{10,11... | collective-permute-start | bytes 9437192 | tf_op jit(solution)/shard_map/ppermute | solution.py:52
  692.7 12.0 %collective-permute-start.74 = (bf16[2,2,48,1152]{3,2,0,1:T(8,128)(2,1)S(1)}, bf16[2,2,48,1152]{3,2,0,1:T(8,128)(2,1)S(1)}, u32[]{:S(2)}, u32[]{:S(2)}) collective-permute-start(bf16[2,2,48,1152]{3,2,0,1:T(8,128)(2,1)S(1)} %bitcast.630), channel_id=1, source_target_pairs={{0,4},{2,6},{4,0},{6,2},{8,12},{10,14},{12,8},{14,10},{16,20},{18,... | collective-permute-start | bytes 1327112 | tf_op jit(solution)/shard_map/ppermute | solution.py:62
  694.2 11.7 %collective-permute-start.76 = (bf16[2,2,48,1152]{3,2,0,1:T(8,128)(2,1)S(1)}, bf16[2,2,48,1152]{3,2,0,1:T(8,128)(2,1)S(1)}, u32[]{:S(2)}, u32[]{:S(2)}) collective-permute-start(bf16[2,2,48,1152]{3,2,0,1:T(8,128)(2,1)S(1)} %bitcast.629), channel_id=1, source_target_pairs={{0,2},{2,0},{4,6},{6,4},{8,10},{10,8},{12,14},{14,12},{16,18},{18,... | collective-permute-start | bytes 1327112 | tf_op jit(solution)/shard_map/ppermute | solution.py:62
  704.9 11.1 %collective-permute-start.75 = (bf16[2,48,1152]{2,1,0:T(8,128)(2,1)S(1)}, bf16[2,48,1152]{2,1,0:T(8,128)(2,1)S(1)}, u32[]{:S(2)}, u32[]{:S(2)}) collective-permute-start(bf16[2,48,1152]{2,1,0:T(8,128)(2,1)S(1)} %dynamic-slice_bitcast_fusion.5), channel_id=1, source_target_pairs={{0,2},{2,0},{4,6},{6,4},{8,10},{10,8},{12,14},{14,12},{16,18},{18,... | collective-permute-start | bytes 663560 | tf_op jit(solution)/shard_map/ppermute | solution.py:62
  707.5 22.1 %collective-permute-start.77 = (bf16[2,48,1152]{2,1,0:T(8,128)(2,1)}, bf16[2,48,1152]{2,1,0:T(8,128)(2,1)}, u32[]{:S(2)}, u32[]{:S(2)}) collective-permute-start(bf16[2,48,1152]{2,1,0:T(8,128)(2,1)} %dynamic-slice_bitcast_fusion.4), channel_id=1, source_target_pairs={{0,4},{2,6},{4,0},{6,2},{8,12},{10,14},{12,8},{14,10},{16,20},{18,... | collective-permute-start | bytes 663560 | tf_op jit(solution)/shard_map/ppermute | solution.py:62
  728.6 26.4 %collective-permute-start.90 = (bf16[2,2,48,3072]{3,2,0,1:T(8,128)(2,1)S(1)}, bf16[2,2,48,3072]{3,2,0,1:T(8,128)(2,1)S(1)}, u32[]{:S(2)}, u32[]{:S(2)}) collective-permute-start(bf16[2,2,48,3072]{3,2,0,1:T(8,128)(2,1)S(1)} %bitcast.609), channel_id=1, source_target_pairs={{0,4},{2,6},{4,0},{6,2},{8,12},{10,14},{12,8},{14,10},{16,20},{18,... | collective-permute-start | bytes 3538952 | tf_op jit(solution)/shard_map/ppermute | solution.py:62
  739.5 28.9 %collective-permute-start.92 = (bf16[2,2,48,3072]{3,2,0,1:T(8,128)(2,1)S(1)}, bf16[2,2,48,3072]{3,2,0,1:T(8,128)(2,1)S(1)}, u32[]{:S(2)}, u32[]{:S(2)}) collective-permute-start(bf16[2,2,48,3072]{3,2,0,1:T(8,128)(2,1)S(1)} %bitcast.610), channel_id=1, source_target_pairs={{0,2},{2,0},{4,6},{6,4},{8,10},{10,8},{12,14},{14,12},{16,18},{18,... | collective-permute-start | bytes 3538952 | tf_op jit(solution)/shard_map/ppermute | solution.py:62
  755.5 20.4 %collective-permute-start.91 = (bf16[2,48,3072]{2,1,0:T(8,128)(2,1)S(1)}, bf16[2,48,3072]{2,1,0:T(8,128)(2,1)S(1)}, u32[]{:S(2)}, u32[]{:S(2)}) collective-permute-start(bf16[2,48,3072]{2,1,0:T(8,128)(2,1)S(1)} %dynamic-slice_bitcast_fusion.1), channel_id=1, source_target_pairs={{0,2},{2,0},{4,6},{6,4},{8,10},{10,8},{12,14},{14,12},{16,18},{18,... | collective-permute-start | bytes 1769480 | tf_op jit(solution)/shard_map/ppermute | solution.py:62
  768.9 9.9 %collective-permute-start.93 = (bf16[2,48,3072]{2,1,0:T(8,128)(2,1)S(1)}, bf16[2,48,3072]{2,1,0:T(8,128)(2,1)S(1)}, u32[]{:S(2)}, u32[]{:S(2)}) collective-permute-start(bf16[2,48,3072]{2,1,0:T(8,128)(2,1)S(1)} %dynamic-slice_bitcast_fusion), channel_id=1, source_target_pairs={{0,4},{2,6},{4,0},{6,2},{8,12},{10,14},{12,8},{14,10},{16,20},{18,... | collective-permute-start | bytes 1769480 | tf_op jit(solution)/shard_map/ppermute | solution.py:62
  780.9 17.0 %collective-permute-start.95 = (bf16[48,3072]{1,0:T(8,128)(2,1)S(1)}, bf16[48,3072]{1,0:T(8,128)(2,1)S(1)}, u32[]{:S(2)}, u32[]{:S(2)}) collective-permute-start(bf16[48,3072]{1,0:T(8,128)(2,1)S(1)} %get-tuple-element.208), channel_id=1, source_target_pairs={{0,16},{2,18},{4,20},{6,22},{8,24},{10,26},{12,28},{14,30},{16,0},... | collective-permute-start | bytes 884744 | tf_op jit(solution)/shard_map/ppermute | solution.py:65
  782.0 15.8 %collective-permute-start.96 = (bf16[48,3072]{1,0:T(8,128)(2,1)S(1)}, bf16[48,3072]{1,0:T(8,128)(2,1)S(1)}, u32[]{:S(2)}, u32[]{:S(2)}) collective-permute-start(bf16[48,3072]{1,0:T(8,128)(2,1)S(1)} %get-tuple-element.209), channel_id=1, source_target_pairs={{0,24},{2,26},{4,28},{6,30},{8,0},{10,2},{12,4},{14,6},{16,8},{18,... | collective-permute-start | bytes 884744 | tf_op jit(solution)/shard_map/ppermute | solution.py:65
  (145 other events, 1950.7 us)

commit v2 on v0

v2 whole, which is shorter than its diff:
```python
import jax
import jax.numpy as jnp
from jax import lax
from jax.experimental import pallas as pl
from jax.experimental.pallas import tpu as pltpu
from jax.sharding import PartitionSpec as P

HD = 64
EPSILON = 1e-06
SCALING = HD**-0.5
LOWER = jnp.bfloat16
UPPER = jnp.float32
NEVER = -1e30
SLOT = 16
VMEM_LIMIT = 56 * 1024 * 1024


def dot(left, right, dims):
    return lax.dot_general(left, right, ((dims[0], dims[1]), ((), ())), preferred_element_type=UPPER)


def mm(left, right):
    return dot(left, right, ((1,), (0,)))


def mm_nt(left, right):
    return dot(left, right, ((1,), (1,)))


def mm_tn(left, right):
    return dot(left, right, ((0,), (0,)))


def normalize(values):
    center = values - jnp.mean(values, -1, keepdims=True)
    inverse = lax.rsqrt(jnp.mean(center * center, -1, keepdims=True) + EPSILON)
    return (center * inverse, inverse)


def norm_back(grad_normed, normed, inverse):
    mean_grad = jnp.mean(grad_normed, -1, keepdims=True)
    mean_proj = jnp.mean(grad_normed * normed, -1, keepdims=True)
    return inverse * (grad_normed - mean_grad - normed * mean_proj)


class Moves:
    def __init__(self, dp_size):
        self.dp_size = dp_size
        self.staged = dp_size == 16
        self.dp = lax.axis_index("dp")
        self.mp = lax.axis_index("mp")
        if self.staged:
            self.blocks = (4, 4)
            z, here = self.dp // 4, self.dp % 4
            came = [((z - k) % 4) * 4 + (here ^ b) for b in range(4) for k in range(4)]
            goes = [((z + k) % 4) * 4 + (here ^ b) for b in range(4) for k in range(4)]
        else:
            self.blocks = (1, 1)
            came = goes = [self.dp * 0]
        self.came_at, self.goes_at, self.chips_at = 2, 2 + len(came), 2
        table = [self.mp, self.dp] + came + goes
        if not self.staged:
            self.chips_at = len(table)
            table += [self.dp * 0 + chip for chip in range(dp_size)]
        self.info = jnp.stack(table).astype(jnp.int32)

    def swap(self, value):
        return lax.ppermute(value, "mp", [(0, 1), (1, 0)])

    def in_order(self, own, other, axis=0):
        return jnp.where(
            self.mp == 0,
            jnp.concatenate([own, other], axis),
            jnp.concatenate([other, own], axis),
        )

    def flip(self, value, bits):
        return lax.ppermute(value, "dp", [(d, d ^ bits) for d in range(16)])

    def turn(self, value, step):
        return lax.ppermute(value, "dp", [(d, (d + 4 * step) % 16) for d in range(16)])

    def line(self, value):
        if not self.staged:
            return value
        return jnp.stack([value] + [self.turn(value, step) for step in (1, 2, 3)])

    def spread(self, line, chips=False):
        if not self.staged:
            value = lax.all_gather(line, "dp", axis=0, tiled=not chips)
            return [value if chips else value[None]]
        return [line] + [self.flip(line, bits) for bits in (1, 2, 3)]

    def meet(self, parts):
        if not self.staged:
            return parts
        return [parts[0]] + [self.flip(parts[bits], bits) for bits in (1, 2, 3)]

    def fold(self, terms):
        if not self.staged:
            return terms
        size = terms[0].shape[0] // 4
        sums = [
            sum(term[step * size : (step + 1) * size].astype(UPPER) for term in terms)
            for step in range(4)
        ]
        return sums[:1] + [part.astype(terms[0].dtype) for part in sums[1:]]

    def finish(self, sums):
        if not self.staged:
            return lax.psum_scatter(
                sums[0].astype(UPPER), "dp", scatter_dimension=0, tiled=True
            )
        total = sums[0]
        for step in (1, 2, 3):
            total = total + self.turn(sums[step], step).astype(UPPER)
        return total

    def square_to_line(self, value):
        if not self.staged:
            return value
        rows, columns = value.shape
        groups = [[4 * z + here for here in range(4)] for z in range(4)]
        value = lax.all_to_all(
            value.reshape(4, rows // 4, columns), "dp", 0, 0, axis_index_groups=groups, tiled=True
        )
        total = sum(value[number].astype(UPPER) for number in range(4)).astype(value.dtype)
        return total.reshape(4, rows // 16, columns)

    def line_to_own(self, value):
        if not self.staged:
            return lax.psum_scatter(value.astype(UPPER), "dp", scatter_dimension=0, tiled=True)
        groups = [[4 * z + here for z in range(4)] for here in range(4)]
        value = lax.all_to_all(value, "dp", 0, 0, axis_index_groups=groups, tiled=True)
        return sum(value[number].astype(UPPER) for number in range(4))

    def sum_cores(self, parts, other):
        came = self.swap(other)
        size = parts[0].shape[0]
        return [
            (part.astype(UPPER) + came[b * size : (b + 1) * size].astype(UPPER)).astype(LOWER)
            for b, part in enumerate(parts)
        ]


def wait_for(value, *others):
    return lax.optimization_barrier((value, *others))[0]


ANY = pl.BlockSpec(memory_space=pl.ANY)


def whole(shape):
    return pl.BlockSpec(shape, lambda *_: (0,) * len(shape))


def call(kernel, info, inputs, outputs, scratch=(), grid=(1,), flops=0, moved=0, name=None, after=(), aliased=()):
    skipped = list(aliased) + list(after)

    def inner(info_ref, *refs):
        kernel(info_ref, *refs[len(skipped) :])

    inputs = [(array, ANY) for array in skipped] + inputs
    return pl.pallas_call(
        inner,
        input_output_aliases={1 + number: number for number in range(len(aliased))},
        out_shape=[jax.ShapeDtypeStruct(shape, kind) for shape, kind, _ in outputs],
        grid_spec=pltpu.PrefetchScalarGridSpec(
            num_scalar_prefetch=1,
            grid=grid,
            in_specs=[spec for _, spec in inputs],
            out_specs=[spec for _, _, spec in outputs],
            scratch_shapes=list(scratch),
        ),
        compiler_params=pltpu.CompilerParams(
            dimension_semantics=("arbitrary",) * len(grid), vmem_limit_bytes=VMEM_LIMIT
        ),
        cost_estimate=pl.CostEstimate(flops=flops, bytes_accessed=moved, transcendentals=0),
        name=name,
    )(info, *[array for array, _ in inputs])


def bring(info, at, pieces, parts, sems, take=None):
    copies = []
    for b, piece in enumerate(pieces):
        count, rows, _ = piece.shape
        rows = take or rows
        for k in range(count):
            number = b * count + k
            start = pl.multiple_of(info[at + number] * rows, 16)
            for p, (target, column, source, columns) in enumerate(parts):
                copy = pltpu.make_async_copy(
                    piece.at[k, pl.ds(0, rows), pl.ds(source, columns)],
                    target.at[pl.ds(start, rows), pl.ds(column, columns)],
                    sems.at[number * len(parts) + p],
                )
                copy.start()
                copies.append(copy)
    return copies


def place(info, at, full, targets, column, columns, single=False):
    if single:
        (target,) = targets
    nb, nk = (4, 4) if at > 3 else (1, 1)
    rows = full.shape[0] // (nb * nk)
    for b in range(nb):
        for k in range(nk):
            start = pl.multiple_of(info[at + b * nk + k] * rows, 16)
            value = full[pl.ds(start, rows), :]
            if single:
                target[(b * nk + k) * rows : (b * nk + k + 1) * rows, column : column + columns] = value
            else:
                targets[b][k * rows : (k + 1) * rows, column : column + columns] = value


def place_square(staged, full, target, column, columns):
    if not staged:
        target[:, column : column + columns] = full[...]
        return
    rows = full.shape[0] // 16
    for here in range(4):
        for z in range(4):
            target[(here * 4 + z) * rows : (here * 4 + z + 1) * rows, column : column + columns] = full[
                (z * 4 + here) * rows : (z * 4 + here + 1) * rows, :
            ]


def grouped_rows(tokens, latents):
    pad = jnp.zeros((SLOT - latents.shape[0], latents.shape[1]), UPPER)
    return jnp.concatenate([tokens, latents, pad], 0)


def attention_forward(move, first, count, tokens, latents, mod, own_w, other_w, sizes):
    group_len, lat_count, features, half = sizes
    groups = tokens.shape[0] // group_len
    length = group_len + SLOT
    real = group_len + lat_count
    heads = half // HD
    np_ = len(own_w)

    def kernel(info, tok, lat, mod_ref, *refs):
        own, other = refs[:np_], refs[np_ : 2 * np_]
        after, lat_one, triple_ref, stats, mixed_ref, att_ref = refs[2 * np_ : 2 * np_ + 6]
        w_own, w_other, w_out, sems = refs[2 * np_ + 6 :]

        @pl.when(pl.program_id(0) == 0)
        def _():
            number = sems.shape[0] // 2
            copies = bring(
                info, move.came_at, own,
                [(w_own, 0, 0, 3 * half), (w_out, 0, 3 * half, half)], sems.at[pl.ds(0, number)],
            ) + bring(
                info, move.came_at, other,
                [(w_other, 0, 0, 3 * half), (w_out, half, 3 * half, half)],
                sems.at[pl.ds(number, number)],
            )
            for copy in copies:
                copy.wait()

        rows = grouped_rows(tok[...], lat[...])
        shift, scale, gate = [mod_ref[0, :, i * features : (i + 1) * features] for i in range(3)]
        normed, _ = normalize(rows)
        inputs = (normed * (1.0 + scale) + shift).astype(LOWER)
        for side, weight in ((0, w_own), (1, w_other)):
            triple = mm(inputs, weight[...]).astype(LOWER)
            triple_ref[:, side * 3 * half : (side + 1) * 3 * half] = triple
            pair = []
            for head in range(heads):
                query, key, value = [
                    triple[:, kind * half + head * HD : kind * half + (head + 1) * HD]
                    for kind in range(3)
                ]
                scores = mm_nt(key, query) * SCALING
                scores = jnp.concatenate(
                    [scores[:real], jnp.full((length - real, length), NEVER, UPPER)], 0
                )
                peak = jnp.max(scores, 0, keepdims=True)
                weights = jnp.exp(scores - peak)
                total = jnp.sum(weights, 0, keepdims=True)
                stats[0, side * heads + head : side * heads + head + 1, :] = peak + jnp.log(total)
                weights = (weights * (1.0 / total)).astype(LOWER)
                pair.append(mm_tn(weights, value).astype(LOWER))
                if len(pair) == 2:
                    at = side * half + (head - 1) * HD
                    mixed_ref[:, at : at + 2 * HD] = jnp.concatenate(pair, 1)
                    pair = []
        attended = mm_nt(mixed_ref[...], w_out[...])
        att_ref[...] = attended.astype(LOWER)
        result = rows + gate * attended
        after[...] = result[:group_len]
        lat_one[...] = result[group_len:real]

    at = lambda g, info: (info[0] * groups // 2 + first + g, 0)
    sems = 2 * np_ * own_w[0].shape[0]
    return call(
        kernel,
        move.info,
        [
            (tokens, pl.BlockSpec((group_len, features), at)),
            (latents, pl.BlockSpec((lat_count, features), at)),
            (mod, pl.BlockSpec((1, 1, 3 * features), lambda g, info: (first + g, 0, 0))),
        ]
        + [(piece, ANY) for piece in own_w + other_w],
        [
            ((count * group_len, features), UPPER, pl.BlockSpec((group_len, features), lambda g, info: (g, 0))),
            ((count * lat_count, features), UPPER, pl.BlockSpec((lat_count, features), lambda g, info: (g, 0))),
            ((count * length, 6 * half), LOWER, pl.BlockSpec((length, 6 * half), lambda g, info: (g, 0))),
            ((count, 2 * heads, length), UPPER, pl.BlockSpec((1, 2 * heads, length), lambda g, info: (g, 0, 0))),
            ((count * length, features), LOWER, pl.BlockSpec((length, features), lambda g, info: (g, 0))),
            ((count * length, features), LOWER, pl.BlockSpec((length, features), lambda g, info: (g, 0))),
        ],
        [
            pltpu.VMEM((features, 3 * half), LOWER),
            pltpu.VMEM((features, 3 * half), LOWER),
            pltpu.VMEM((features, 2 * half), LOWER),
            pltpu.SemaphoreType.DMA((2 * sems,)),
        ],
        grid=(count,),
        flops=count * length * features * features * 8 * 2,
        moved=count * 4_000_000,
        name="attention_forward",
    )


def attention_entry(
    move, lat_own, lat_came, lat_one, grad_two, gain, mod, grad_tok, attended, sizes, after=()
):
    group_len, lat_count, features, half = sizes
    count = lat_one.shape[0] // lat_count
    length = group_len + SLOT

    def kernel(info, own, came, lat, two, gain_ref, mod_ref, gtok, att, grad_lat, grad_att, vec):
        normed, inverse = normalize(lat[...])
        into = two[...] + norm_back((own[...] + came[...]) * gain_ref[...], normed, inverse)
        grad_lat[...] = into
        rows = grouped_rows(gtok[...], into)
        vec[0] = jnp.sum(rows * att[...].astype(UPPER), 0, keepdims=True)
        grad_att[...] = (mod_ref[0, :, 2 * features :] * rows).astype(LOWER)

    row = lambda size, columns: pl.BlockSpec((size, columns), lambda g, info: (g, 0))
    return call(
        kernel,
        move.info,
        [(value, row(lat_count, features)) for value in (lat_own, lat_came, lat_one, grad_two)]
        + [
            (gain, whole(gain.shape)),
            (mod, pl.BlockSpec((1, 1, 3 * features), lambda g, info: (g, 0, 0))),
            (grad_tok, row(group_len, features)),
            (attended, row(length, features)),
        ],
        [
            ((count * lat_count, features), UPPER, row(lat_count, features)),
            ((count * length, features), LOWER, row(length, features)),
            ((count, 1, features), UPPER, pl.BlockSpec((1, 1, features), lambda g, info: (g, 0, 0))),
        ],
        grid=(count,),
        flops=count * length * features * 10,
        moved=count * 2_500_000,
        name="attention_entry",
        after=after,
    )


def attention_backward(
    move, first, count, tokens, latents, mod, grad_tok, grad_lat, grad_att, saved, own_w, other_w, sizes, before=(), after=()
):
    group_len, lat_count, features, half = sizes
    groups = tokens.shape[0] // group_len
    mine = groups // 2
    length = group_len + SLOT
    real = group_len + lat_count
    heads = half // HD
    np_ = len(own_w)
    triple_all, stats_all = saved

    def kernel(info, tok, lat, mod_ref, gtok, glat, gatt, triple, stats, *refs):
        own, other = refs[:np_], refs[np_ : 2 * np_]
        out_tok, out_lat, in_ref, tri_ref, vec_ref, full = refs[2 * np_ : 2 * np_ + 6]
        w_in, w_out, sems = refs[2 * np_ + 6 :]

        @pl.when(pl.program_id(0) == 0)
        def _():
            number = sems.shape[0] // 2
            copies = []
            for side, pieces in ((0, own), (1, other)):
                parts = [(w_in, side * 3 * half, 0, 3 * half), (w_out, side * half, 3 * half, half)]
                copies += bring(info, move.came_at, pieces, parts, sems.at[pl.ds(side * number, number)])
            for copy in copies:
                copy.wait()

        rows = grouped_rows(tok[...], lat[...])
        shift, scale = [mod_ref[0, :, i * features : (i + 1) * features] for i in range(2)]
        normed, inverse = normalize(rows)
        in_ref[...] = (normed * (1.0 + scale) + shift).astype(LOWER)
        grad_mixed_all = mm(gatt[...], w_out[...]).astype(LOWER)
        for side in range(2):
            pairs = ([], [], [])
            for head in range(heads):
                base = side * 3 * half + head * HD
                query, key, value = [
                    triple[:, base + kind * half : base + kind * half + HD] for kind in range(3)
                ]
                at = side * half + head * HD
                grad_mixed = grad_mixed_all[:, at : at + HD]
                scores = mm_nt(key, query) * SCALING
                scores = jnp.concatenate(
                    [scores[:real], jnp.full((length - real, length), NEVER, UPPER)], 0
                )
                weights = jnp.exp(scores - stats[0, side * heads + head : side * heads + head + 1, :])
                grad_weights = mm_nt(value, grad_mixed)
                delta = jnp.sum(grad_weights * weights, 0, keepdims=True)
                grad_scores = (weights * (grad_weights - delta)).astype(LOWER)
                pairs[0].append((mm_tn(grad_scores, key) * SCALING).astype(LOWER))
                pairs[1].append((mm(grad_scores, query) * SCALING).astype(LOWER))
                pairs[2].append(mm(weights.astype(LOWER), grad_mixed).astype(LOWER))
                if head % 2:
                    for kind in range(3):
                        at = base + kind * half - HD
                        tri_ref[:, at : at + 2 * HD] = jnp.concatenate(pairs[kind][-2:], 1)
        grad_inputs = mm_nt(tri_ref[...], w_in[...])
        vec_ref[0, 0:1, :] = jnp.sum(grad_inputs, 0, keepdims=True)
        vec_ref[0, 1:2, :] = jnp.sum(grad_inputs * normed, 0, keepdims=True)
        result = grouped_rows(gtok[...], glat[...]) + norm_back(
            grad_inputs * (1.0 + scale), normed, inverse
        )
        out_tok[...] = result[:group_len]
        full[...] = result[:group_len]
        out_lat[...] = result[group_len:real]

    at = lambda g, info: (info[0] * mine + first + g, 0)
    row = lambda size, columns: pl.BlockSpec((size, columns), lambda g, info: (first + g, 0))
    vector = lambda n, size: pl.BlockSpec((1, n, size), lambda g, info: (first + g, 0, 0))
    return call(
        kernel,
        move.info,
        [
            (tokens, pl.BlockSpec((group_len, features), at)),
            (latents, pl.BlockSpec((lat_count, features), at)),
            (mod, vector(1, 3 * features)),
            (grad_tok, row(group_len, features)),
            (grad_lat, row(lat_count, features)),
            (grad_att, row(length, features)),
            (triple_all, row(length, 6 * half)),
            (stats_all, vector(2 * heads, length)),
        ]
        + [(piece, ANY) for piece in own_w + other_w],
        [
            ((mine * group_len, features), UPPER, row(group_len, features)),
            ((mine * lat_count, features), UPPER, row(lat_count, features)),
            ((mine * length, features), LOWER, row(length, features)),
            ((mine * length, 6 * half), LOWER, row(length, 6 * half)),
            ((mine, 2, features), UPPER, vector(2, features)),
            (tokens.shape, UPPER, pl.BlockSpec((group_len, features), at)),
        ],
        [
            pltpu.VMEM((features, 6 * half), LOWER),
            pltpu.VMEM((features, 2 * half), LOWER),
            pltpu.SemaphoreType.DMA((4 * np_ * own_w[0].shape[0],)),
        ],
        grid=(count,),
        flops=count * length * features * features * 20,
        moved=count * 5_000_000,
        name="attention_backward",
        aliased=before,
        after=after,
    )


def attention_gradients(move, side, inputs, triples, grad_att, mixed, half, came=(), after=()):
    total, features = inputs.shape
    nb, nk = move.blocks
    columns = 4 * half

    def kernel(info, in_ref, tri_ref, att_ref, mix_ref, *refs):
        first = mm(jnp.transpose(in_ref[...]), tri_ref[...])
        second = mm(jnp.transpose(att_ref[...]), mix_ref[...])
        if side == 1:
            refs[0][:, : 3 * half] = first.astype(LOWER)
            refs[0][:, 3 * half :] = second.astype(LOWER)
        else:
            other, grads, square = refs[0], refs[1:-1], refs[-1]
            square[:, : 3 * half] = (first + other[:, : 3 * half].astype(UPPER)).astype(LOWER)
            square[:, 3 * half :] = (second + other[:, 3 * half :].astype(UPPER)).astype(LOWER)
            place(info, move.goes_at, square, grads, 0, columns)

    rows = [features // nb] * nb if side == 0 else [features]
    return call(
        kernel,
        move.info,
        [
            (inputs, whole(inputs.shape)),
            (triples, pl.BlockSpec((total, 3 * half), lambda i, info: (0, side))),
            (grad_att, whole(grad_att.shape)),
            (mixed, pl.BlockSpec((total, half), lambda i, info: (0, side))),
        ]
        + [(part, whole(part.shape)) for part in came],
        [((size, columns), LOWER, whole((size, columns))) for size in rows],
        [pltpu.VMEM((features, columns), LOWER)] if side == 0 else [],
        flops=total * features * columns * 2,
        moved=total * (features + columns) * 2,
        name="attention_gradients",
        after=after,
    )


ROOT = 0.7978845608028654
CUBE = 0.044715


def feed_forward(rows, grad_result, shift, scale, gate, w_up, w_down, hidden_ref, upward_ref, step=768):
    normed, inverse = normalize(rows)
    inputs = (normed * (1.0 + scale) + shift).astype(LOWER)
    grad_narrow = (gate * grad_result).astype(LOWER)
    narrowed = grad_inputs = 0.0
    for start in range(0, w_up.shape[1], step):
        units = slice(start, start + step)
        upward = mm(inputs, w_up[:, units])
        square = upward * upward
        bend = jnp.tanh(upward * (ROOT + (ROOT * CUBE) * square))
        half_up = 0.5 * upward
        hidden = (half_up * (1.0 + bend)).astype(LOWER)
        slope = 0.5 * (1.0 + bend) + half_up * (1.0 - bend * bend) * (
            ROOT + (3.0 * ROOT * CUBE) * square
        )
        grad_upward = (mm(grad_narrow, w_down[:, units]) * slope).astype(LOWER)
        hidden_ref[:, units] = hidden
        upward_ref[:, units] = grad_upward
        narrowed = narrowed + mm_nt(hidden, w_down[:, units])
        grad_inputs = grad_inputs + mm_nt(grad_upward, w_up[:, units])
    result = rows + gate * narrowed
    grad_rows = grad_result + norm_back(grad_inputs * (1.0 + scale), normed, inverse)
    return result, grad_rows, inputs, grad_narrow, (
        grad_inputs,
        grad_inputs * normed,
        grad_result * narrowed,
    )


def bring_wide(wide, w_up, w_down, sems):
    units = w_up.shape[1] // 2
    count, rows, _ = wide.shape
    copies = []
    for entry in range(count):
        at = pl.ds(entry // 2 * rows, rows)
        for which, target in enumerate((w_up, w_down)):
            copies.append(
                pltpu.make_async_copy(
                    wide.at[entry, :, pl.ds(which * units, units)],
                    target.at[at, pl.ds(entry % 2 * units, units)],
                    sems.at[2 * entry + which],
                )
            )
    for copy in copies:
        copy.start()
    for copy in copies:
        copy.wait()


def token_feed_forward(move, first, count, rows, cotangent, mod, wide_w, sizes, before=(), after=()):
    group_len, lat_count, features, half = sizes
    groups = cotangent.shape[0] // group_len
    units = wide_w.shape[2] // 2

    def kernel(info, row_ref, cot, mod_ref, *refs):
        wide = refs[0]
        result, grad, inputs_ref, narrow_ref, hidden_ref, upward_ref, vec, full = refs[1:9]
        w_up, w_down, sems = refs[9:]

        @pl.when(pl.program_id(0) == 0)
        def _():
            bring_wide(wide, w_up, w_down, sems)

        shift, scale, gate = [mod_ref[0, :, i * features : (i + 1) * features] for i in range(3)]
        out, grad_rows, inputs, narrow, terms = feed_forward(
            row_ref[...], cot[...], shift, scale, gate, w_up, w_down, hidden_ref, upward_ref
        )
        result[...] = out
        full[...] = out
        grad[...] = grad_rows
        inputs_ref[...] = jnp.transpose(inputs)
        narrow_ref[...] = jnp.transpose(narrow)
        for number, term in enumerate(terms):
            vec[0, number : number + 1, :] = jnp.sum(term, 0, keepdims=True)

    at = pl.BlockSpec((group_len, features), lambda g, info: (info[0] * groups // 2 + first + g, 0))
    turned = pl.BlockSpec((features, group_len), lambda g, info: (0, first + g))
    row = lambda columns: pl.BlockSpec((group_len, columns), lambda g, info: (first + g, 0))
    total = rows.shape[0]
    return call(
        kernel,
        move.info,
        [
            (rows, row(features)),
            (
                cotangent,
                at,
            ),
            (mod, pl.BlockSpec((1, 1, 3 * features), lambda g, info: (first + g, 0, 0))),
        ]
        + [(wide_w, ANY)],
        [
            ((total, features), UPPER, row(features)),
            ((total, features), UPPER, row(features)),
            ((features, total), LOWER, turned),
            ((features, total), LOWER, turned),
            ((total, 2 * units), LOWER, row(2 * units)),
            ((total, 2 * units), LOWER, row(2 * units)),
            ((groups // 2, 3, features), UPPER, pl.BlockSpec((1, 3, features), lambda g, info: (first + g, 0, 0))),
            (cotangent.shape, UPPER, at),
        ],
        [
            pltpu.VMEM((features, 2 * units), LOWER),
            pltpu.VMEM((features, 2 * units), LOWER),
            pltpu.SemaphoreType.DMA((2 * wide_w.shape[0],)),
        ],
        grid=(count,),
        flops=count * group_len * features * units * 16,
        moved=count * 8_000_000,
        name="token_feed_forward",
        aliased=before,
        after=after,
    )


def latent_feed_forward(move, lat_one, branch, came, cotangent, mod, wide_w, sizes, after=()):
    group_len, lat_count, features, half = sizes
    rows_n = lat_one.shape[0]
    count = rows_n // lat_count
    units = wide_w.shape[2] // 2

    def kernel(info, one, own, other, cot, mod_ref, *refs):
        wide = refs[0]
        result, grad, inputs_ref, narrow_ref, hidden_ref, upward_ref, vec = refs[1:8]
        w_up, w_down, sems = refs[8:]
        bring_wide(wide, w_up, w_down, sems)
        vectors = [
            jnp.concatenate(
                [
                    jnp.broadcast_to(mod_ref[g, :, i * features : (i + 1) * features], (lat_count, features))
                    for g in range(count)
                ],
                0,
            )
            for i in range(3)
        ]
        rows = one[...] + own[...] + other[...]
        out, grad_rows, inputs, narrow, terms = feed_forward(
            rows, cot[...], *vectors, w_up, w_down, hidden_ref, upward_ref
        )
        result[...] = out
        grad[...] = grad_rows
        inputs_ref[...] = inputs
        narrow_ref[...] = narrow
        for number, term in enumerate(terms):
            for g in range(count):
                vec[g, number : number + 1, :] = jnp.sum(
                    term[g * lat_count : (g + 1) * lat_count], 0, keepdims=True
                )

    rows_f = (rows_n, features)
    return call(
        kernel,
        move.info,
        [
            (lat_one, whole(rows_f)),
            (branch, whole(rows_f)),
            (came, whole(rows_f)),
            (cotangent, pl.BlockSpec(rows_f, lambda i, info: (info[0], 0))),
            (mod, whole(mod.shape)),
        ]
        + [(wide_w, ANY)],
        [
            (rows_f, UPPER, whole(rows_f)),
            (rows_f, UPPER, whole(rows_f)),
            (rows_f, LOWER, whole(rows_f)),
            (rows_f, LOWER, whole(rows_f)),
            ((rows_n, 2 * units), LOWER, whole((rows_n, 2 * units))),
            ((rows_n, 2 * units), LOWER, whole((rows_n, 2 * units))),
            ((count, 3, features), UPPER, whole((count, 3, features))),
        ],
        [
            pltpu.VMEM((features, 2 * units), LOWER),
            pltpu.VMEM((features, 2 * units), LOWER),
            pltpu.SemaphoreType.DMA((2 * wide_w.shape[0],)),
        ],
        flops=rows_n * features * units * 64,
        moved=12_000_000,
        name="latent_feed_forward",
        after=after,
    )


def wide_gradients(move, side, lefts, rights, lat_lefts, lat_rights, came=(), before=(), after=(), tile=768):
    features, total = lefts[0].shape
    units = rights[0].shape[1] // 2
    tiles = units // tile
    nb, nk = move.blocks
    extra = len(came)

    def kernel(info, *refs):
        outs = refs[8 + extra :]
        step = pl.program_id(1)
        for which in range(2):
            left, right, lat_left, lat_right = [refs[2 * number + which] for number in range(4)]

            @pl.when(pl.program_id(0) == which)
            def _():
                acc = mm_tn(lat_left[...], lat_right[...]) + mm(left[...], right[...])
                if side == 1:
                    outs[0][...] = acc.astype(LOWER)
                else:
                    outs[-1][...] = (acc + refs[8][...].astype(UPPER)).astype(LOWER)

        if side == 0:
            place_square(move.staged, outs[-1], outs[0], 0, tile)

    def columns(rows, which):
        def at(w, s, info):
            core = info[0] if side == 0 else 1 - info[0]
            held = (tiles - 1) if which == 0 else 0
            return (0, core * tiles + jnp.where(w == which, s, held))

        return pl.BlockSpec((rows, tile), at)

    here = lambda w, s, info: (0, w * tiles + s)
    offset = 0 if side == 1 else before[0].shape[1] // tile - 2 * tiles
    out_at = lambda w, s, info: (0, offset + w * tiles + s)
    shapes = [part.shape for part in before] if side == 0 else [(features, 2 * units)]
    return call(
        kernel,
        move.info,
        [(part, whole(part.shape)) for part in lefts]
        + [(part, columns(part.shape[0], which)) for which, part in enumerate(rights)]
        + [(part, whole(part.shape)) for part in lat_lefts]
        + [(part, columns(part.shape[0], which)) for which, part in enumerate(lat_rights)]
        + [(part, pl.BlockSpec((features, tile), here)) for part in came],
        [(shape, LOWER, pl.BlockSpec((shape[0], tile), out_at)) for shape in shapes],
        [pltpu.VMEM((features, tile), LOWER)] if side == 0 else [],
        grid=(2, tiles),
        flops=total * features * units * 4,
        moved=total * units * 4 + features * units * 4,
        name="wide_gradients",
        aliased=before,
        after=after,
    )


def modulation_terms(move, vectors, modulator, bias, middle):
    shard, width = modulator.shape
    size = middle // 2
    nb = len(vectors)
    count = vectors[0].shape[0]
    rows = vectors[0].shape[1]
    chips = count * rows // SLOT
    features = vectors[0].shape[2]

    def kernel(info, *refs):
        pieces = refs[:nb]
        mods, biases = refs[nb : nb + 2], refs[nb + 2 : nb + 4]
        outs = refs[nb + 4 :]
        terms, picked, gain = outs[:nb], outs[nb : 2 * nb], outs[2 * nb]
        shape = (features, shard)
        select = lax.broadcasted_iota(jnp.int32, shape, 0) == (
            lax.broadcasted_iota(jnp.int32, shape, 1) + info[1] * shard
        )
        select = jnp.where(select, 1.0, 0.0).astype(LOWER)
        gains = jnp.zeros((1, features), UPPER)
        for b in range(nb):
            value = pieces[b][...].reshape(chips * SLOT, features)
            gains = gains + jnp.sum(
                value.astype(UPPER).reshape(chips, SLOT, features)[:, 8:9, :], 0
            )
            mine = mm(value, select)
            picked[b][...] = jnp.concatenate(
                [
                    jnp.where(
                        info[0] == 0,
                        mine[k * SLOT : k * SLOT + 4],
                        mine[k * SLOT + 4 : k * SLOT + 8],
                    )
                    for k in range(chips)
                ],
                0,
            )
            for part in range(2):
                product = mm(mine.astype(LOWER), mods[part][...].astype(LOWER)) + biases[part][...]
                product = product.reshape(chips, SLOT, size)
                for k in range(chips):
                    where = (chips - k) % chips if nb > 1 else k
                    terms[b][where, :, part * size : (part + 1) * size] = product[k, :8]
        gain[...] = gains

    columns = lambda rows_, part: pl.BlockSpec((rows_, size), lambda i, info: (0, 2 * part + info[0]))
    return call(
        kernel,
        move.info,
        [(piece, whole(piece.shape)) for piece in vectors]
        + [(modulator, columns(shard, 0)), (modulator, columns(shard, 1))]
        + [(bias, columns(1, 0)), (bias, columns(1, 1))],
        [((chips, 8, 2 * size), UPPER, whole((chips, 8, 2 * size)))] * nb
        + [((chips * 4, shard), UPPER, whole((chips * 4, shard)))] * nb
        + [((1, features), UPPER, whole((1, features)))],
        flops=10_000_000,
        moved=3_000_000,
        name="modulation_terms",
    )


def modulation_gradients(move, picked, grads, modulator, dp_size, after=()):
    shard, width = modulator.shape
    features = width // 6
    nb = len(grads)
    chips = dp_size // nb
    own = 4

    def kernel(info, *refs):
        picks, parts = refs[:nb], refs[nb : 2 * nb]
        mod_ref, out, terms = refs[2 * nb :]
        products = [jnp.zeros((chips * own, shard), UPPER) for _ in range(nb)]
        for i in range(6):
            at = slice(i * features, (i + 1) * features)
            weight = mod_ref[:, at].astype(LOWER)
            total = jnp.zeros((shard, features), UPPER)
            sums = jnp.zeros((1, features), UPPER)
            for b in range(nb):
                value = parts[b][:, i // 2 * 8 : i // 2 * 8 + 8, :].astype(UPPER)
                value = jnp.concatenate(
                    [value[k, i % 2 * own : (i % 2 + 1) * own] for k in range(chips)], 0
                )
                sums = sums + jnp.sum(value, 0, keepdims=True)
                value = value.astype(LOWER)
                total = total + mm_tn(picks[b][...].astype(LOWER), value)
                products[b] = products[b] + mm_nt(value, weight)
            out[:shard, at] = total
            extra = jnp.zeros((1, features), UPPER)
            if i == 0:
                for b in range(nb):
                    for k in range(chips):
                        extra = extra + jnp.sum(parts[b][k, 24:32, :].astype(UPPER), 0, keepdims=True)
            out[shard:, at] = jnp.concatenate(
                [sums, extra, jnp.zeros((6, features), UPPER)], 0
            )
        for b in range(nb):
            for k in range(chips):
                terms[info[move.chips_at + b * chips + k]] = products[b][k * own : (k + 1) * own]

    return call(
        kernel,
        move.info,
        [(piece, whole(piece.shape)) for piece in picked]
        + [(piece, whole(piece.shape)) for piece in grads]
        + [(modulator, whole(modulator.shape))],
        [
            ((shard + 8, width), UPPER, whole((shard + 8, width))),
            ((dp_size, own, shard), UPPER, whole((dp_size, own, shard))),
        ],
        flops=10_000_000,
        moved=3_000_000,
        name="modulation_gradients",
        after=after,
    )


def latent_project(move, own, other, gain, weights, half):
    rows_n, features = own.shape
    np_ = len(weights)

    def kernel(info, own_ref, other_ref, gain_ref, *refs):
        pieces = refs[:np_]
        triple, lat_in, weight, rows, sems = refs[np_:]
        copies = bring(info, move.came_at, pieces, [(weight, 0, 0, 4 * half)], sems)
        here = pl.multiple_of(info[0] * rows_n, rows_n)
        there = pl.multiple_of((1 - info[0]) * rows_n, rows_n)
        rows[pl.ds(here, rows_n), :] = own_ref[...]
        rows[pl.ds(there, rows_n), :] = other_ref[...]
        normed, _ = normalize(rows[...])
        inputs = (normed * gain_ref[...]).astype(LOWER)
        lat_in[...] = inputs
        for copy in copies:
            copy.wait()
        triple[...] = mm(inputs, weight[:, : 3 * half]).astype(LOWER)

    total = 2 * rows_n
    shapes = [(total, 3 * half), (total, features), (features, 4 * half)]
    return call(
        kernel,
        move.info,
        [(own, whole(own.shape)), (other, whole(own.shape)), (gain, whole(gain.shape))]
        + [(piece, ANY) for piece in weights],
        [(shape, LOWER, whole(shape)) for shape in shapes],
        [
            pltpu.VMEM((total, features), UPPER),
            pltpu.SemaphoreType.DMA((np_ * weights[0].shape[0],)),
        ],
        flops=500_000_000,
        moved=6_000_000,
        name="latent_project",
    )


def allowed_pairs(info, own_image, image, keep, own_keep=None):
    count, total = own_image.shape[0], image.shape[1]
    shape = (count, total)
    itself = lax.broadcasted_iota(jnp.int32, shape, 1) == (
        lax.broadcasted_iota(jnp.int32, shape, 0) + info[1] * count
    )
    kept = (keep if own_keep is None else own_keep) == 1
    return (own_image == image) & (kept | itself)


def split_rows(info, full, own, other):
    rows = own.shape[0]
    own[...] = full[pl.ds(pl.multiple_of(info[0] * rows, rows), rows), :]
    other[...] = full[pl.ds(pl.multiple_of((1 - info[0]) * rows, rows), rows), :]


def latent_forward(move, query, key_values, weights, masks, half, features, after=()):
    count = query.shape[0]
    np_ = len(key_values)
    total = np_ * key_values[0].shape[0] * count
    heads = half // HD

    def kernel(info, query_ref, weight, own_image, image, keep, *refs):
        pieces = refs[:np_]
        mixed, stats, own, other, all_kv, full, sems = refs[np_:]
        copies = bring(info, move.chips_at, pieces, [(all_kv, 0, half, 2 * half)], sems)
        allowed = allowed_pairs(info, own_image[...], image[...], keep[...])
        for copy in copies:
            copy.wait()
        lane = lax.broadcasted_iota(jnp.int32, (count, 128), 1)
        logs = jnp.zeros((count, 128), UPPER)
        outs = []
        for head in range(heads):
            at = slice(head * HD, (head + 1) * HD)
            scores = mm_nt(query_ref[:, at], all_kv[:, at]) * SCALING
            scores = jnp.where(allowed, scores, NEVER)
            peak = jnp.max(scores, 1, keepdims=True)
            weights_ = jnp.exp(scores - peak)
            sums = jnp.sum(weights_, 1, keepdims=True)
            logs = jnp.where(lane == head, peak + jnp.log(sums), logs)
            weights_ = (weights_ * (1.0 / sums)).astype(LOWER)
            outs.append(mm(weights_, all_kv[:, half + head * HD : half + (head + 1) * HD]).astype(LOWER))
        stats[...] = logs
        mixed[...] = jnp.concatenate(outs, 1)
        full[...] = mm_nt(mixed[...], weight[:, 3 * half :])
        split_rows(info, full, own, other)

    part = (count // 2, features)
    return call(
        kernel,
        move.info,
        [(query, whole(query.shape)), (weights, whole(weights.shape))]
        + [(mask, whole(mask.shape)) for mask in masks[:3]]
        + [(piece, ANY) for piece in key_values],
        [
            ((count, half), LOWER, whole((count, half))),
            ((count, 128), UPPER, whole((count, 128))),
            (part, UPPER, whole(part)),
            (part, UPPER, whole(part)),
        ],
        [
            pltpu.VMEM((total, 2 * half), LOWER),
            pltpu.VMEM((count, features), UPPER),
            pltpu.SemaphoreType.DMA((np_ * key_values[0].shape[0],)),
        ],
        flops=1_000_000_000,
        moved=6_000_000,
        name="latent_forward",
        after=after,
    )


def latent_backward(move, query, key_values, weights, masks, mixed, stats, grad_own, grad_other, half, features):
    count = query.shape[0]
    np_ = len(key_values)
    total = np_ * key_values[0].shape[0] * count
    heads = half // HD

    def kernel(info, query_ref, weight, own_image, image, keep, mixed_ref, stats_ref, own, other, *refs):
        pieces = refs[:np_]
        sent, grad_query, out_grad, all_kv, full, sems = refs[np_:]
        copies = bring(info, move.chips_at, pieces, [(all_kv, 0, half, 2 * half)], sems)
        allowed = allowed_pairs(info, own_image[...], image[...], keep[...])
        rows_n = own.shape[0]
        full[pl.ds(pl.multiple_of(info[0] * rows_n, rows_n), rows_n), :] = own[...]
        full[pl.ds(pl.multiple_of((1 - info[0]) * rows_n, rows_n), rows_n), :] = other[...]
        branch = full[...].astype(LOWER)
        grad_mixed = mm(branch, weight[:, 3 * half :]).astype(LOWER)
        out_grad[...] = mm_tn(branch, mixed_ref[...])
        sent[:, :half] = grad_mixed
        for copy in copies:
            copy.wait()
        lane = lax.broadcasted_iota(jnp.int32, (count, 128), 1)
        extra = jnp.zeros((count, 128), UPPER)
        outs = []
        for head in range(heads):
            at = slice(head * HD, (head + 1) * HD)
            scores = mm_nt(query_ref[:, at], all_kv[:, at]) * SCALING
            log_total = stats_ref[:, head : head + 1]
            weights_ = jnp.exp(jnp.where(allowed, scores - log_total, NEVER))
            grad_weights = mm_nt(grad_mixed[:, at], all_kv[:, half + head * HD : half + (head + 1) * HD])
            delta = jnp.sum(grad_weights * weights_, 1, keepdims=True)
            grad_scores = (weights_ * (grad_weights - delta)).astype(LOWER)
            outs.append((mm(grad_scores, all_kv[:, at]) * SCALING).astype(LOWER))
            for start, column in ((0, log_total), (3, delta)):
                high = column.astype(LOWER).astype(UPPER)
                middle = (column - high).astype(LOWER).astype(UPPER)
                low = column - high - middle
                for number, part in enumerate((high, middle, low)):
                    extra = jnp.where(lane == (start + number) * heads + head, part, extra)
        sent[:, half:] = extra.astype(LOWER)
        grad_query[...] = jnp.concatenate(outs, 1)

    return call(
        kernel,
        move.info,
        [(query, whole(query.shape)), (weights, whole(weights.shape))]
        + [(mask, whole(mask.shape)) for mask in masks[:3]]
        + [(value, whole(value.shape)) for value in (mixed, stats, grad_own, grad_other)]
        + [(piece, ANY) for piece in key_values],
        [
            ((count, half + 128), LOWER, whole((count, half + 128))),
            ((count, half), LOWER, whole((count, half))),
            ((features, half), UPPER, whole((features, half))),
        ],
        [
            pltpu.VMEM((total, 2 * half), LOWER),
            pltpu.VMEM((count, features), UPPER),
            pltpu.SemaphoreType.DMA((np_ * key_values[0].shape[0],)),
        ],
        flops=1_500_000_000,
        moved=6_000_000,
        name="latent_backward",
    )


def latent_sources(move, key_value, gathered, came, weights, masks, grad_query, lat_in, out_grad, lat_own, lat_other, gain, half, features, room, after=()):
    count = key_value.shape[0]
    np_ = len(came)
    total = np_ * came[0].shape[0] * count
    heads = half // HD
    nb, nk = move.blocks

    def kernel(info, kv, weight, own_image, image, own_keep, grad_query_ref, lat_in_ref, out_grad_ref, lat_o, lat_t, gain_ref, *refs):
        pieces, gathered_refs = refs[:np_], refs[np_ : 2 * np_]
        refs = refs[np_:]
        own, other, gain_rows = refs[np_ : np_ + 3]
        grads = refs[np_ + 3 : np_ + 4]
        all_q, full, rows, square, sems = refs[np_ + 4 :]
        number = sems.shape[0] // 2
        copies = bring(
            info, move.chips_at, pieces, [(all_q, half, 0, half + 128)], sems.at[pl.ds(0, number)]
        ) + bring(
            info, move.chips_at, gathered_refs, [(all_q, 0, 0, half)], sems.at[pl.ds(number, number)]
        )
        allowed = allowed_pairs(info, own_image[...], image[...], None, own_keep[...])
        for copy in copies:
            copy.wait()
        turned = jnp.transpose(all_q[:, 2 * half :].astype(UPPER))
        keys, values = [], []
        for head in range(heads):
            at = slice(head * HD, (head + 1) * HD)
            other_at = slice(half + head * HD, half + (head + 1) * HD)
            last_at = slice(2 * half + head * HD, 2 * half + (head + 1) * HD)
            log_total, delta = [
                sum(turned[(s + i) * heads + head : (s + i) * heads + head + 1] for i in range(3))
                for s in (0, 3)
            ]
            scores = mm_nt(kv[:, other_at], all_q[:, at]) * SCALING
            weights_ = jnp.exp(jnp.where(allowed, scores - log_total, NEVER))
            grad_weights = mm_nt(kv[:, last_at], all_q[:, other_at])
            grad_scores = (weights_ * (grad_weights - delta)).astype(LOWER)
            keys.append((mm(grad_scores, all_q[:, at]) * SCALING).astype(LOWER))
            values.append(mm(weights_.astype(LOWER), all_q[:, other_at]).astype(LOWER))
        triple = jnp.concatenate([grad_query_ref[...]] + keys + values, 1)
        full[...] = mm_nt(triple, weight[:, : 3 * half])
        split_rows(info, full, own, other)
        rows_n = lat_o.shape[0]
        rows[pl.ds(pl.multiple_of(info[0] * rows_n, rows_n), rows_n), :] = lat_o[...]
        rows[pl.ds(pl.multiple_of((1 - info[0]) * rows_n, rows_n), rows_n), :] = lat_t[...]
        normed, _ = normalize(rows[...])
        square[:, : 3 * half] = mm_tn(lat_in_ref[...], triple).astype(LOWER)
        square[:, 3 * half : 4 * half] = out_grad_ref[...].astype(LOWER)
        total_gain = jnp.sum(full[...] * normed, 0, keepdims=True)
        for number in range(3):
            part = total_gain.astype(LOWER).astype(UPPER)
            gain_rows[number : number + 1, :] = part
            total_gain = total_gain - part
        gain_rows[3:, :] = jnp.zeros((5, features), UPPER)
        place_square(move.staged, square, grads[0], 0, 4 * half)

    part = (count // 2, features)
    columns = 4 * half
    return call(
        kernel,
        move.info,
        [(key_value, whole(key_value.shape)), (weights, whole(weights.shape))]
        + [(mask, whole(mask.shape)) for mask in (masks[0], masks[1], masks[3])]
        + [
            (value, whole(value.shape))
            for value in (grad_query, lat_in, out_grad, lat_own, lat_other, gain)
        ]
        + [(piece, ANY) for piece in came + gathered],
        [(part, UPPER, whole(part))] * 2
        + [((8, features), UPPER, whole((8, features)))]
        + [((features, columns + room), LOWER, whole((features, columns)))],
        [
            pltpu.VMEM((total, 2 * half + 128), LOWER),
            pltpu.VMEM((count, features), UPPER),
            pltpu.VMEM((count, features), UPPER),
            pltpu.VMEM((features, columns), LOWER),
            pltpu.SemaphoreType.DMA((2 * np_ * came[0].shape[0],)),
        ],
        flops=2_000_000_000,
        moved=8_000_000,
        name="latent_sources",
        after=after,
    )


def fill(move, full, other, after=(), block=512):
    rows, features = other.shape
    block = min(block, rows)
    steps = rows // block

    def kernel(info, other_ref, out):
        out[...] = other_ref[...]

    return call(
        kernel,
        move.info,
        [(other, pl.BlockSpec((block, features), lambda i, info: (i, 0)))],
        [
            (
                full.shape,
                UPPER,
                pl.BlockSpec((block, features), lambda i, info: ((1 - info[0]) * steps + i, 0)),
            )
        ],
        grid=(steps,),
        moved=2 * rows * features * 4,
        name="fill",
        after=after,
        aliased=[full],
    )[0]


def make_body(dp_size):
    def body(
        tokens,
        latents,
        condition,
        modulator,
        offsets,
        local_qkv,
        local_out,
        global_qkv,
        global_out,
        latent_gain,
        up_weight,
        down_weight,
        group_image,
        latent_keep,
        token_cotangent,
        latent_cotangent,
    ):
        move = Moves(dp_size)
        mp, dp = move.mp, move.dp
        groups = condition.shape[0]
        own = groups // 2
        features = tokens.shape[1]
        group_len = tokens.shape[0] // groups
        lat_count = latents.shape[0] // groups
        shard, width = modulator.shape
        half = local_out.shape[1]
        units = up_weight.shape[1]
        middle = width // 2
        sizes = (group_len, lat_count, features, half)

        def mine(value):
            size = value.shape[0] // 2
            return lax.dynamic_slice_in_dim(value, mp * size, size, 0)

        def others(value):
            size = value.shape[0] // 2
            return lax.dynamic_slice_in_dim(value, (1 - mp) * size, size, 0)

        scaled = jax.nn.silu(condition).astype(LOWER)
        gain_row = lax.dynamic_update_slice(
            jnp.zeros((1, features), LOWER), latent_gain.astype(LOWER)[None], (0, dp * shard)
        )
        bias_row = lax.dynamic_update_slice(
            jnp.zeros((1, width), UPPER),
            offsets.astype(LOWER).astype(UPPER)[None],
            (0, dp * (width // dp_size)),
        )
        vectors = move.spread(
            move.line(
                jnp.concatenate(
                    [scaled, gain_row, jnp.zeros((SLOT - 1 - groups, features), LOWER)], 0
                )
            )
        )
        found = modulation_terms(move, vectors, modulator, bias_row, middle)
        nb = len(vectors)
        picked, gain = found[nb : 2 * nb], found[2 * nb]

        total = move.finish(
            move.fold(move.meet([term.reshape(-1, term.shape[2]) for term in found[:nb]]))
        )
        total, came = mine(total), move.swap(others(total))
        mod_one, mod_two = [
            move.in_order(total[:, part], came[:, part], 1)[:, None]
            for part in (slice(0, middle // 2), slice(middle // 2, middle))
        ]

        wide_shard = jnp.concatenate([up_weight, down_weight], 1).astype(LOWER)
        if move.staged:
            wide_w = lax.all_gather(wide_shard, ("dp", "mp"), axis=0)
        else:
            wide_w = lax.all_gather(
                lax.all_gather(wide_shard, "dp", axis=0, tiled=True), "mp", axis=0
            )
        shards = jnp.concatenate(
            [
                local_qkv.reshape(shard, 3 * half),
                local_out,
                global_qkv.reshape(shard, 3 * half),
                global_out,
            ],
            1,
        ).astype(LOWER)
        if move.staged:
            turned = [shards] + [move.turn(shards, step) for step in (1, 2, 3)]
            first_line, lat_line = [
                jnp.stack([part[:, start : start + 4 * half] for part in turned])
                for start in (0, 4 * half)
            ]
        else:
            first_line, lat_line = shards[:, : 4 * half], shards[:, 4 * half :]
        first_w = move.spread(first_line)
        first_other = [move.swap(piece) for piece in first_w]
        latent_w = move.spread(wait_for(lat_line, first_w[-1]))

        after, lat_one, triple, stats, mixed, attended = attention_forward(
            move, 0, own, tokens, latents, mod_one, first_w, first_other, sizes
        )


        chip_count = groups * lat_count
        images = jnp.repeat(group_image, lat_count)
        own_slice = lambda value: lax.dynamic_slice_in_dim(value, dp * chip_count, chip_count)
        masks = (
            own_slice(images)[:, None],
            images[None],
            latent_keep[None],
            own_slice(latent_keep)[:, None],
        )
        lat_came = move.swap(lat_one)
        lat_triple, lat_in, lat_weight = latent_project(
            move, lat_one, lat_came, gain, latent_w, half
        )
        key_values_line = move.line(lat_triple)
        key_values = move.spread(key_values_line, chips=True)

        part = own // 2
        ff = token_feed_forward(
            move, 0, part, after, token_cotangent, mod_two, wide_w, sizes, after=[key_values_line]
        )
        lat_mixed, lat_stats, branch_own, branch_other = latent_forward(
            move, lat_triple, key_values, lat_weight, masks, half, features, after=[ff[6]]
        )
        lat_result, grad_lat_two, lat_inputs, lat_narrow, lat_hidden, lat_upward, lat_vec = (
            latent_feed_forward(
                move,
                lat_one,
                branch_own,
                move.swap(branch_other),
                latent_cotangent,
                mod_two,
                wide_w,
                sizes,
            )
        )

        sent, grad_query, out_grad = latent_backward(
            move,
            lat_triple,
            key_values,
            lat_weight,
            masks,
            lat_mixed,
            lat_stats,
            grad_lat_two,
            move.swap(grad_lat_two),
            half,
            features,
        )
        came_line = move.line(sent)
        came = move.spread(came_line, chips=True)
        ff = token_feed_forward(
            move, part, own - part, after, token_cotangent, mod_two, wide_w, sizes, ff, [sent]
        )
        token_result, grad_tok, ff_inputs, ff_narrow, ff_hidden, ff_upward, ff_vec, token_output = ff
        factors = (
            [ff_inputs, ff_narrow],
            [ff_upward, ff_hidden],
            [lat_inputs, lat_narrow],
            [lat_upward, lat_hidden],
        )
        (wide_other,) = wide_gradients(move, 1, *factors, after=[came_line])
        lat_grad_own, lat_grad_other, gain_rows, *lat_parts = latent_sources(
            move,
            lat_triple,
            key_values,
            came,
            lat_weight,
            masks,
            grad_query,
            lat_in,
            out_grad,
            lat_one,
            lat_came,
            gain,
            half,
            features,
            2 * units,
            after=[wide_other],
        )
        (early_parts,) = wide_gradients(
            move, 0, *factors, came=[move.swap(wide_other)], before=lat_parts
        )
        early_line = move.square_to_line(early_parts)
        grad_lat_one, grad_att, gate_vec = attention_entry(
            move,
            lat_grad_own,
            move.swap(lat_grad_other),
            lat_one,
            grad_lat_two,
            gain,
            mod_one,
            grad_tok,
            attended,
            sizes,
            after=[early_parts],
        )

        token_output = fill(move, token_output, move.swap(token_result), [wide_other])

        grad_tokens, grad_latents, first_in, first_triples, vec_one, grad_output = attention_backward(
            move,
            0,
            own,
            tokens,
            latents,
            mod_one,
            grad_tok,
            grad_lat_one,
            grad_att,
            (triple, stats),
            first_w,
            first_other,
            sizes,
            after=[token_output],
        )
        vec_two = ff_vec + lat_vec
        vectors = jnp.concatenate(
            [vec_one[:, 0], vec_one[:, 1], gate_vec[:, 0]]
            + [vec_two[:, i] for i in range(3)]
            + [gain_rows],
            0,
        ).astype(LOWER)
        vectors_line = move.line(vectors)
        first_factors = (first_in, first_triples, grad_att, mixed, half)
        (first_grads_other,) = attention_gradients(move, 1, *first_factors, after=[vectors])
        first_parts = attention_gradients(
            move, 0, *first_factors, [move.swap(first_grads_other)], [vectors_line]
        )
        first_terms = move.meet(first_parts)
        early_sum = move.line_to_own(early_line)
        mod_grad, grad_terms = modulation_gradients(
            move,
            picked,
            move.spread(vectors_line, chips=True),
            modulator,
            dp_size,
            after=[first_parts[0], early_line],
        )
        grad_output = fill(move, grad_output, move.swap(grad_tokens))
        first_sum = move.finish(
            move.fold(wait_for(first_terms, grad_output, mod_grad))
        )
        mod_grad = mod_grad + move.swap(mod_grad)
        grad_scaled = lax.all_to_all(grad_terms, "dp", 0, 0, tiled=True)
        grad_scaled = grad_scaled.transpose(1, 0, 2).reshape(own, features)
        grad_scaled = move.in_order(grad_scaled, move.swap(grad_scaled))
        grad_condition = jax.vjp(jax.nn.silu, condition)[1](grad_scaled)[0]
        bias_all = mod_grad[shard]
        gain_grad = lax.dynamic_slice_in_dim(mod_grad[shard + 1, :features], dp * shard, shard)
        piece = width // dp_size
        latent_output = move.in_order(lat_result, move.swap(lat_result))
        return (
            token_output,
            latent_output,
            grad_output,
            move.in_order(grad_latents, move.swap(grad_latents)),
            grad_condition,
            mod_grad[:shard],
            lax.dynamic_slice_in_dim(bias_all, dp * piece, piece),
            first_sum[:, : 3 * half].reshape(shard, 3, half),
            first_sum[:, 3 * half :],
            early_sum[:, : 3 * half].reshape(shard, 3, half),
            early_sum[:, 3 * half : 4 * half],
            gain_grad,
            early_sum[:, 4 * half : 4 * half + units],
            early_sum[:, 4 * half + units :],
        )

    return body


def solution(mesh):
    rows, heads = P("dp", None), P("dp", None, "mp")
    columns, vector = P("dp", "mp"), P("dp")
    return jax.shard_map(
        make_body(mesh.shape["dp"]),
        mesh=mesh,
        in_specs=(
            rows, rows, rows, rows, vector, heads, columns, heads, columns, vector,
            columns, columns, P(), P(), rows, rows,
        ),
        out_specs=(
            rows, rows, rows, rows, rows, rows, vector, heads, columns, heads, columns,
            vector, columns, columns,
        ),
        check_vma=False,
    )
```

time: 2090 us -> 487 us (0.23)
  waiting for transfers between devices: 1350 us -> 102 us
  blocking collectives: 325 us -> 13.3 us
  matrix products: 217 us -> 0 us
  Pallas kernels: 0 us -> 217 us
  starting transfers between devices: 1.18 us -> 83.4 us
  other arithmetic: 94.4 us -> 23 us
  local copies, waits for them, and re-layouts: 74.3 us -> 24.8 us
    reduce_scatter x9 -> x0, waiting for transfers between devices: 1140 us -> none  [the longest x1 227 us: body(): lax.psum_scatter(mod_grad, 'dp', scatter_dimension=0, tiled=True)]
    dot_general x33 -> x0, matrix products: 217 us -> none  [the longest x1 16.4 us: body(): jnp.einsum('gnd,df->gnf', grad_narrow, w_down, preferred_element_type=UPPER)]
    pallas_call x0 -> x18, Pallas kernels: none -> 217 us  [call(): pl.pallas_call(inner, input_output_aliases={1 + number: number for number...]
    all_gather x5 -> x1, waiting for transfers between devices: 179 us -> 0.01 us  [body(): wide_w = lax.all_gather(wide_shard, ('dp', 'mp'), axis=0)]
    all_gather x4 -> x0, blocking collectives: 169 us -> none  [the longest x1 44.6 us: body(): lax.all_gather(global_out.astype(LOWER), 'dp', axis=0, tiled=True)]
    unnamed x2 -> x0, blocking collectives: 155 us -> none
    ppermute x0 -> x62, waiting for transfers between devices: none -> 102 us  [the longest x24 58.3 us: flip(): return lax.ppermute(value, 'dp', [(d, d ^ bits) for d in range(16)])]
    ppermute x0 -> x62, starting transfers between devices: none -> 74 us  [the longest x21 42.8 us: turn(): lax.ppermute(value, 'dp', [(d, (d + 4 * step) % 16) for d in range(16)])]
  transfers between devices with their start and end apart: 19 -> 65, of which waited for: 14 -> 23; matrix products, arithmetic and copies ran while one was open for 9% -> 7% of each run, Pallas kernels for 0% -> 37%
where the time goes in v2:
time: 487 us; the launch traced here: 478 us
  Pallas kernels  217 us (45%)
  waiting for transfers between devices  102 us (21%)
  starting transfers between devices  83.4 us (17%)
  local copies, waits for them, and re-layouts  24.8 us (5%)
  other arithmetic  23 us (5%)
  between operations  15.4 us (3%)
  blocking collectives  13.3 us (3%)
    pallas_call x18, Pallas kernels, call(): pl.pallas_call(inner, input_output_aliases={1 + number: number for number...  217 us
    ppermute x24, waiting for transfers between devices, flip(): return lax.ppermute(value, 'dp', [(d, d ^ bits) for d in range(16)])  58.3 us
    ppermute x21, starting transfers between devices, turn(): lax.ppermute(value, 'dp', [(d, (d + 4 * step) % 16) for d in range(16)])  42.8 us
    ppermute x21, waiting for transfers between devices, turn(): lax.ppermute(value, 'dp', [(d, (d + 4 * step) % 16) for d in range(16)])  38.6 us
    ppermute x24, starting transfers between devices, flip(): return lax.ppermute(value, 'dp', [(d, d ^ bits) for d in range(16)])  28.8 us
    all_to_all x1, blocking collectives, body(): grad_scaled = lax.all_to_all(grad_terms, 'dp', 0, 0, tiled=True)  13.3 us
    unnamed x96, local copies, waits for them, and re-layouts  9.96 us
  transfers between devices with their start and end apart: 65, of which 23 were waited for; matrix products, arithmetic and copies ran while one was open for 7% of the time, Pallas kernels for 37%

profile of v2, /device:TPU:0, one launch (start us, length us, event | category | flops | bytes accessed | tf_op | source)
XLA Modules:
  0.0 478.1 jit_solution(5631577572995288855)
XLA Ops:
  10.8 3.1 collective-permute-start
  13.9 2.6 collective-permute-start.1
  21.9 1.6 collective-permute-start.3
  23.5 1.5 collective-permute-start.4
  27.3 1.9 collective-permute-done.3.refs_1_
  29.1 3.3 collective-permute-start.15
  33.7 3.8 modulation_terms.1
  38.0 1.5 collective-permute-start.7
  41.0 8.6 %collective-permute-done.14 = bf16[48,3072]{1,0:T(8,128)(2,1)S(1)} collective-permute-done((bf16[48,3072]{1,0:T(8,128)(2,1)S(1)}, bf16[48,3072]{1,0:T(8,128)(2,1)S(1)}, u32[]{:S(2)}, u32[]{:S(2)}) %collective-permute-start.14) | collective-permute-done | bytes 294944 | tf_op jit(solution)/shard_map/ppermute | solution.py:81
  49.8 2.6 collective-permute-start.18
  53.9 5.2 %collective-permute-start.10 = (f32[8,2304]{1,0:T(8,128)S(1)}, f32[8,2304]{1,0:T(8,128)S(1)}, u32[]{:S(2)}, u32[]{:S(2)}) collective-permute-start(f32[8,2304]{1,0:T(8,128)S(1)} %get-tuple-element.205), channel_id=1, source_target_pairs={{0,16},{2,18},{4,20},{6,22},{8,24},{10,26},{12,28},{14,30},{16,0},... | collective-permute-start | bytes 221192 | tf_op jit(solution)/shard_map/ppermute | solution.py:81
  59.1 3.4 collective-permute-start.11
  62.6 5.3 %collective-permute-done.10 = f32[8,2304]{1,0:T(8,128)S(1)} collective-permute-done((f32[8,2304]{1,0:T(8,128)S(1)}, f32[8,2304]{1,0:T(8,128)S(1)}, u32[]{:S(2)}, u32[]{:S(2)}) %collective-permute-start.10) | collective-permute-done | bytes 73760 | tf_op jit(solution)/shard_map/ppermute | solution.py:81
  70.5 4.9 %collective-permute-done.18.refs_6_.refs_12_ = bf16[4,48,1536]{2,1,0:T(8,128)(2,1)S(1)} collective-permute-done((bf16[4,48,1536]{2,1,0:T(8,128)(2,1)S(1)}, bf16[4,48,1536]{2,1,0:T(8,128)(2,1)S(1)}, u32[]{:S(2)}, u32[]{:S(2)}) %collective-permute-start.18) | collective-permute-done | bytes 589856 | tf_op jit(solution)/shard_map/ppermute | solution.py:78
  75.4 10.5 %collective-permute-done.16.refs_4_.refs_10_ = bf16[4,48,1536]{2,1,0:T(8,128)(2,1)S(1)} collective-permute-done((bf16[4,48,1536]{2,1,0:T(8,128)(2,1)S(1)}, bf16[4,48,1536]{2,1,0:T(8,128)(2,1)S(1)}, u32[]{:S(2)}, u32[]{:S(2)}) %collective-permute-start.16) | collective-permute-done | bytes 589856 | tf_op jit(solution)/shard_map/ppermute | solution.py:78
  87.1 1.5 collective-permute-start.24
  89.2 1.5 collective-permute-start.26
  92.3 24.3 %attention_forward.1 = (f32[1024,768]{1,0:T(8,128)}, f32[32,768]{1,0:T(8,128)}, bf16[1088,2304]{1,0:T(8,128)(2,1)}, f32[4,12,272]{2,1,0:T(8,128)}, bf16[1088,768]{1,0:T(8,128)(2,1)}, /*index=5*/bf16[1088,768]{1,0:T(8,128)(2,1)}) custom-call(s32[34]{0:T(128)} %stack.215.info_ref, f32[2048,768]{1,0:T(8,128)} %refs_1_.3, f32[64,768]{1,0:T(8,128)} %refs_2_.3, ...), custom_call_target="tpu_custom_call" | custom-call | flops 10267656192 | bytes 16000000 | tf_op jit(solution)/shard_map/attention_forward/pallas_call | solution.py:164
  118.4 12.1 %collective-permute-done.26.refs_6_ = bf16[4,48,1536]{2,1,0:T(8,128)(2,1)S(1)} collective-permute-done((bf16[4,48,1536]{2,1,0:T(8,128)(2,1)S(1)}, bf16[4,48,1536]{2,1,0:T(8,128)(2,1)S(1)}, u32[]{:S(2)}, u32[]{:S(2)}) %collective-permute-start.26) | collective-permute-done | bytes 589856 | tf_op jit(solution)/shard_map/ppermute | solution.py:78
  131.4 4.9 %latent_project.1 = (bf16[64,1152]{1,0:T(8,128)(2,1)}, bf16[64,768]{1,0:T(8,128)(2,1)}, bf16[768,1536]{1,0:T(8,128)(2,1)}) custom-call(s32[34]{0:T(128)} %stack.215.info_ref, f32[32,768]{1,0:T(8,128)} %get-tuple-element.90.refs_0_.refs_9_.refs_3_, f32[32,768]{1,0:T(8,128)} %copy-done.16, f32[1,768]{1,0:T(1,128)} %get-tuple-element.91.refs_2_.refs_11_.refs_5_, ...), custom_call_target="tpu_custom_call" | custom-call | flops 500000000 | bytes 6000000 | tf_op jit(solution)/shard_map/latent_project/pallas_call | solution.py:164
  136.3 4.2 collective-permute-start.27
  140.5 2.6 collective-permute-start.29
  145.0 5.3 %collective-permute-done.28 = bf16[64,1152]{1,0:T(8,128)(2,1)S(1)} collective-permute-done((bf16[64,1152]{1,0:T(8,128)(2,1)}, bf16[64,1152]{1,0:T(8,128)(2,1)S(1)}, u32[]{:S(2)}, u32[]{:S(2)}) %collective-permute-start.28) | collective-permute-done | bytes 147488 | tf_op jit(solution)/shard_map/ppermute | solution.py:81
  152.1 1.5 collective-permute-start.31
  154.9 21.4 %token_feed_forward.2 = (f32[1024,768]{1,0:T(8,128)}, f32[1024,768]{1,0:T(8,128)}, bf16[768,1024]{1,0:T(8,128)(2,1)}, bf16[768,1024]{1,0:T(8,128)(2,1)}, bf16[10...) custom-call(s32[34]{0:T(128)} %stack.215.info_ref, ...), custom_call_target="tpu_custom_call" | custom-call | flops 9663676416 | bytes 16000000 | tf_op jit(solution)/shard_map/token_feed_forward/pallas_call | solution.py:164
  176.3 3.3 collective-permute-done.31.refs_8_.refs_11_.refs_18_
  180.6 7.7 %latent_forward.1 = (bf16[64,384]{1,0:T(8,128)(2,1)}, f32[64,128]{1,0:T(8,128)}, f32[32,768]{1,0:T(8,128)}, f32[32,768]{1,0:T(8,128)}) custom-call(s32[34]{0:T(128)} %stack.215.info_ref, f32[4,3,768]{2,1,0:T(4,128)} %get-tuple-element.101.refs_0_.refs_6_, bf16[64,1152]{1,0:T(8,128)(2,1)} %get-tuple-element.93.refs_1_.refs_0_, ...), custom_call_target="tpu_custom_call" | custom-call | flops 1000000000 | bytes 6000000 | tf_op jit(solution)/shard_map/latent_forward/pallas_call | solution.py:164
  188.5 1.5 collective-permute-done.33.refs_2_
  190.6 11.5 %latent_feed_forward.1 = (f32[32,768]{1,0:T(8,128)}, f32[32,768]{1,0:T(8,128)}, bf16[32,768]{1,0:T(8,128)(2,1)}, bf16[32,768]{1,0:T(8,128)(2,1)}, bf16[32,3072]{...) custom-call(s32[34]{0:T(128)} %stack.215.info_ref, ...), custom_call_target="tpu_custom_call" | custom-call | flops 2415919104 | bytes 12000000 | tf_op jit(solution)/shard_map/latent_feed_forward/pallas_call | solution.py:164
  204.3 8.1 %latent_backward.1 = (bf16[64,512]{1,0:T(8,128)(2,1)}, bf16[64,384]{1,0:T(8,128)(2,1)}, f32[768,384]{1,0:T(8,128)}) custom-call(s32[34]{0:T(128)} %stack.215.info_ref, bf16[64,1152]{1,0:T(8,128)(2,1)} %get-tuple-element.93.refs_1_.refs_0_, bf16[768,1536]{1,0:T(8,128)(2,1)} %get-tuple-element.103.refs_2_.refs_1_, s32[64,1]{1,0:T(8,128)} %copy.82.refs_3_.refs_2_, ...), custom_call_target="tpu_custom_call" | custom-call | flops 1500000000 | bytes 6000000 | tf_op jit(solution)/shard_map/latent_backward/pallas_call | solution.py:164
  212.4 3.8 collective-permute-start.35
  216.2 2.3 collective-permute-start.36
  218.6 21.7 %token_feed_forward.3 = (f32[1024,768]{1,0:T(8,128)}, f32[1024,768]{1,0:T(8,128)}, bf16[768,1024]{1,0:T(8,128)(2,1)}, bf16[768,1024]{1,0:T(8,128)(2,1)}, bf16[10...) custom-call(s32[34]{0:T(128)} %stack.215.info_ref, ...), custom_call_target="tpu_custom_call", output_to_operand_aliasing={{0}: (1, {}), {1}: (2, {}), {2}: (3, {}), {3}: (4, {}), {4}... | custom-call | flops 9663676416 | bytes 16000000 | tf_op jit(solution)/shard_map/token_feed_forward/pallas_call | solution.py:164
  241.1 12.3 %wide_gradients.2.refs_1_.refs_0_ = bf16[768,3072]{1,0:T(8,128)(2,1)} custom-call(s32[34]{0:T(128)} %stack.215.info_ref, bf16[4,64,512]{2,1,0:T(8,128)(2,1)} %pad_maximum_fusion.5.refs_0_.refs_12_, bf16[768,1024]{1,0:T(8,128)(2,1)} %get-tuple-element.111.refs_1_, bf16[768,1024]{1,0:T(8,128)(2,1)} %get-tuple-element.112.refs_2_, ...), custom_call_target="tpu_custom_call" | custom-call | flops 4831838208 | bytes 11010048 | tf_op jit(solution)/shard_map/wide_gradients/pallas_call | solution.py:164
  258.9 4.3 collective-permute-done.40.refs_13_
  263.3 5.9 %collective-permute-done.41.refs_14_ = bf16[4,64,512]{2,1,0:T(8,128)(2,1)} collective-permute-done((bf16[4,64,512]{2,1,0:T(8,128)(2,1)S(1)}, bf16[4,64,512]{2,1,0:T(8,128)(2,1)}, u32[]{:S(2)}, u32[]{:S(2)}) %collective-permute-start.41) | collective-permute-done | bytes 262176 | tf_op jit(solution)/shard_map/ppermute | solution.py:78
  269.1 9.3 %latent_sources.1 = (f32[32,768]{1,0:T(8,128)}, f32[32,768]{1,0:T(8,128)}, f32[8,768]{1,0:T(8,128)}, bf16[768,4608]{1,0:T(8,128)(2,1)}) custom-call(s32[34]{0:T(128)} %stack.215.info_ref, bf16[768,3072]{1,0:T(8,128)(2,1)} %wide_gradients.2.refs_1_.refs_0_, bf16[64,1152]{1,0:T(8,128)(2,1)} %get-tuple-element.93.refs_1_.refs_0_, ...), custom_call_target="tpu_custom_call" | custom-call | flops 2000000000 | bytes 8000000 | tf_op jit(solution)/shard_map/latent_sources/pallas_call | solution.py:164
  278.4 12.7 %wide_gradients.3.refs_0_ = bf16[768,4608]{1,0:T(8,128)(2,1)} custom-call(s32[34]{0:T(128)} %stack.215.info_ref, bf16[768,4608]{1,0:T(8,128)(2,1)} %get-tuple-element.125.refs_0_, bf16[768,1024]{1,0:T(8,128)(2,1)} %get-tuple-element.111.refs_1_, bf16[768,1024]{1,0:T(8,128)(2,1)} %get-tuple-element.112.refs_2_, ...), custom_call_target="tpu_custom_call", output_to_operand_aliasing={{}: (1, {})} | custom-call | flops 4831838208 | bytes 11010048 | tf_op jit(solution)/shard_map/wide_gradients/pallas_call | solution.py:164
  291.2 5.7 %all-to-all-start = ((bf16[4,192,4608]{2,1,0:T(8,128)(2,1)}), bf16[4,192,4608]{2,1,0:T(8,128)(2,1)}, u32[]{:S(2)}, u32[]{:S(2)}) async-start(bf16[4,192,4608]{2,1,0:T(8,128)(2,1)} %bitcast.136), calls=%async_computation | async-start | bytes 14155776 | tf_op jit(solution)/shard_map/all_to_all | solution.py:124
  297.1 3.9 fill.2.refs_0_
  301.6 5.6 %attention_entry.1 = (f32[32,768]{1,0:T(8,128)}, bf16[1088,768]{1,0:T(8,128)(2,1)}, f32[4,1,768]{2,1,0:T(1,128)}) custom-call(s32[34]{0:T(128)} %stack.215.info_ref, bf16[768,4608]{1,0:T(8,128)(2,1)} %wide_gradients.3.refs_0_, f32[32,768]{1,0:T(8,128)} %get-tuple-element.126.refs_1_, f32[32,768]{1,0:T(8,128)} %copy-done.24, ...), custom_call_target="tpu_custom_call" | custom-call | flops 8355840 | bytes 10000000 | tf_op jit(solution)/shard_map/attention_entry/pallas_call | solution.py:164
  307.2 43.0 %attention_backward.1 = (f32[1024,768]{1,0:T(8,128)}, f32[32,768]{1,0:T(8,128)}, bf16[1088,768]{1,0:T(8,128)(2,1)}, bf16[1088,2304]{1,0:T(8,128)(2,1)}, f32[4,2,768]{2,1,0:T(2,128)}, /*index=5*/f32[2048,768]{1,0:T(8,128)}) custom-call(s32[34]{0:T(128)} %stack.215.info_ref, f32[2048,768]{1,0:T(8,128)} %fill.2.refs_0_, f32[2048,768]{1,0:T(8,128)} %refs_1_.3, ...), custom_call_target="tpu_custom_call" | custom-call | flops 12834570240 | bytes 20000000 | tf_op jit(solution)/shard_map/attention_backward/pallas_call | solution.py:164
  351.0 2.5 concatenate.149.refs_0_
  353.5 8.8 %attention_gradients.2 = bf16[768,1536]{1,0:T(8,128)(2,1)} custom-call(s32[34]{0:T(128)} %stack.215.info_ref, bf16[32,768]{1,0:T(8,128)(2,1)} %concatenate.149.refs_0_, bf16[1088,768]{1,0:T(8,128)(2,1)} %get-tuple-element.141.refs_1_, bf16[1088,2304]{1,0:T(8,128)(2,1)} %get-tuple-element.142.refs_2_, bf16[1088,768]{1,0:T(8,128)(2,1)} %get-tuple-element.130.refs_6_.refs_3_, ...), custom_call_target="tpu_custom_call" | custom-call | flops 2566914048 | bytes 5013504 | tf_op jit(solution)/shard_map/attention_gradients/pallas_call | solution.py:164
  362.8 1.8 collective-permute-start.47
  365.3 1.8 collective-permute-start.49
  367.1 1.7 collective-permute-done.47
  368.9 1.6 collective-permute-done.48
  370.5 2.1 collective-permute-start.51
  372.5 1.5 collective-permute-start.52
  375.6 9.4 %attention_gradients.3 = (bf16[192,1536]{1,0:T(8,128)(2,1)}, bf16[192,1536]{1,0:T(8,128)(2,1)}, bf16[192,1536]{1,0:T(8,128)(2,1)}, bf16[192,1536]{1,0:T(8,128)(2,1)}) custom-call(s32[34]{0:T(128)} %stack.215.info_ref, bf16[4,32,768]{2,1,0:T(8,128)(2,1)} %copy-done.9, bf16[1088,768]{1,0:T(8,128)(2,1)} %get-tuple-element.141.refs_1_, ...), custom_call_target="tpu_custom_call" | custom-call | flops 2566914048 | bytes 5013504 | tf_op jit(solution)/shard_map/attention_gradients/pallas_call | solution.py:164
  385.0 5.2 %add_convert_fusion = bf16[1,192,4608]{2,1,0:T(8,128)(2,1)} fusion(bf16[4,192,4608]{2,1,0:T(8,128)(2,1)} %all-to-all-done), kind=kLoop, calls=%fused_computation | loop fusion | flops 7077888 | bytes 8847360 | tf_op jit(solution)/shard_map/convert.1
  391.0 4.5 modulation_gradients.1
  396.3 13.3 %all_to_all.15 = f32[16,1,192]{2,1,0:T(1,128)S(1)} all-to-all(f32[16,1,192]{2,1,0:T(1,128)S(1)} %reshape.347), channel_id=1, replica_groups=mesh['dp'=16,'mp'=2] {'dp'}, dimensions={0} | all-to-all | bytes 24576 | tf_op jit(solution)/shard_map/all_to_all | solution.py:1395
  409.6 3.6 all-to-all-start.2
  414.4 2.3 collective-permute-start.58
  420.1 4.0 fill.3
  424.2 5.6 %collective-permute-done.56 = bf16[192,1536]{1,0:T(8,128)(2,1)} collective-permute-done((bf16[192,1536]{1,0:T(8,128)(2,1)}, bf16[192,1536]{1,0:T(8,128)(2,1)}, u32[]{:S(2)}, u32[]{:S(2)}) %collective-permute-start.56) | collective-permute-done | bytes 589856 | tf_op jit(solution)/shard_map/ppermute | solution.py:78
  429.9 8.8 %collective-permute-done.57 = bf16[192,1536]{1,0:T(8,128)(2,1)} collective-permute-done((bf16[192,1536]{1,0:T(8,128)(2,1)}, bf16[192,1536]{1,0:T(8,128)(2,1)}, u32[]{:S(2)}, u32[]{:S(2)}) %collective-permute-start.57) | collective-permute-done | bytes 589856 | tf_op jit(solution)/shard_map/ppermute | solution.py:78
  440.2 1.6 add_convert_fusion.3
  441.8 1.7 collective-permute-start.59
  443.5 2.4 collective-permute-start.60
  447.9 2.4 collective-permute-done.59
  450.4 11.8 %collective-permute-done.60 = bf16[48,1536]{1,0:T(8,128)(2,1)S(1)} collective-permute-done((bf16[48,1536]{1,0:T(8,128)(2,1)S(1)}, bf16[48,1536]{1,0:T(8,128)(2,1)S(1)}, u32[]{:S(2)}, u32[]{:S(2)}) %collective-permute-start.60) | collective-permute-done | bytes 147488 | tf_op jit(solution)/shard_map/ppermute | solution.py:81
  (264 shorter events, 62.9 us)
Async XLA Ops:
  7.2 147.7 %all-gather.2.cloned.1.call-start = ((), (), s32[]{:S(2)}) async-start(), calls=%async_computation.3 | async-start | bytes 9732096 | tf_op jit(solution)/shard_map/all_gather | solution.py:1220
  10.8 11.1 %collective-permute-start = (bf16[16,768]{1,0:T(8,128)(2,1)S(1)}, bf16[16,768]{1,0:T(8,128)(2,1)S(1)}, u32[]{:S(2)}, u32[]{:S(2)}) collective-permute-start(bf16[16,768]{1,0:T(8,128)(2,1)S(1)} %get-tuple-element.225), channel_id=1, source_target_pairs={{0,8},{2,10},{4,12},{6,14},{8,16},{10,18},{12,20},{14,22},{16,24},... | collective-permute-start | bytes 73736 | tf_op jit(solution)/shard_map/ppermute | solution.py:81
  13.9 7.9 %collective-permute-start.1 = (bf16[16,768]{1,0:T(8,128)(2,1)S(1)}, bf16[16,768]{1,0:T(8,128)(2,1)S(1)}, u32[]{:S(2)}, u32[]{:S(2)}) collective-permute-start(bf16[16,768]{1,0:T(8,128)(2,1)S(1)} %get-tuple-element.225), channel_id=1, source_target_pairs={{0,16},{2,18},{4,20},{6,22},{8,24},{10,26},{12,28},{14,30},{16,0},... | collective-permute-start | bytes 73736 | tf_op jit(solution)/shard_map/ppermute | solution.py:81
  16.5 5.4 %collective-permute-start.2 = (bf16[16,768]{1,0:T(8,128)(2,1)S(1)}, bf16[16,768]{1,0:T(8,128)(2,1)S(1)}, u32[]{:S(2)}, u32[]{:S(2)}) collective-permute-start(bf16[16,768]{1,0:T(8,128)(2,1)S(1)} %get-tuple-element.225), channel_id=1, source_target_pairs={{0,24},{2,26},{4,28},{6,30},{8,0},{10,2},{12,4},{14,6},{16,8},{18,... | collective-permute-start | bytes 73736 | tf_op jit(solution)/shard_map/ppermute | solution.py:81
  20.7 18.9 %collective-permute-start.13 = (bf16[48,3072]{1,0:T(8,128)(2,1)S(1)}, bf16[48,3072]{1,0:T(8,128)(2,1)S(1)}, u32[]{:S(2)}, u32[]{:S(2)}) collective-permute-start(bf16[48,3072]{1,0:T(8,128)(2,1)S(1)} %pad_maximum_fusion.3), channel_id=1, source_target_pairs={{0,8},{2,10},{4,12},{6,14},{8,16},{10,18},{12,20},{14,22},{16,24},... | collective-permute-start | bytes 884744 | tf_op jit(solution)/shard_map/ppermute | solution.py:81
  21.5 28.1 %collective-permute-start.14 = (bf16[48,3072]{1,0:T(8,128)(2,1)S(1)}, bf16[48,3072]{1,0:T(8,128)(2,1)S(1)}, u32[]{:S(2)}, u32[]{:S(2)}) collective-permute-start(bf16[48,3072]{1,0:T(8,128)(2,1)S(1)} %pad_maximum_fusion.3), channel_id=1, source_target_pairs={{0,16},{2,18},{4,20},{6,22},{8,24},{10,26},{12,28},{14,30},{16,0},... | collective-permute-start | bytes 884744 | tf_op jit(solution)/shard_map/ppermute | solution.py:81
  21.9 7.2 %collective-permute-start.3 = (bf16[4,16,768]{2,1,0:T(8,128)(2,1)S(1)}, bf16[4,16,768]{2,1,0:T(8,128)(2,1)S(1)}, u32[]{:S(2)}, u32[]{:S(2)}) collective-permute-start(bf16[4,16,768]{2,1,0:T(8,128)(2,1)S(1)} %pad_maximum_fusion.7.refs_0_), channel_id=1, source_target_pairs={{0,2},{2,0},{4,6},{6,4},{8,10},{10,8},{12,14},{14,12},{16,18},{18,... | collective-permute-start | bytes 294920 | tf_op jit(solution)/shard_map/ppermute | solution.py:78
  23.5 8.9 %collective-permute-start.4 = (bf16[4,16,768]{2,1,0:T(8,128)(2,1)S(1)}, bf16[4,16,768]{2,1,0:T(8,128)(2,1)S(1)}, u32[]{:S(2)}, u32[]{:S(2)}) collective-permute-start(bf16[4,16,768]{2,1,0:T(8,128)(2,1)S(1)} %pad_maximum_fusion.7.refs_0_), channel_id=1, source_target_pairs={{0,4},{2,6},{4,0},{6,2},{8,12},{10,14},{12,8},{14,10},{16,20},{18,... | collective-permute-start | bytes 294920 | tf_op jit(solution)/shard_map/ppermute | solution.py:78
  25.0 7.4 %collective-permute-start.5 = (bf16[4,16,768]{2,1,0:T(8,128)(2,1)S(1)}, bf16[4,16,768]{2,1,0:T(8,128)(2,1)S(1)}, u32[]{:S(2)}, u32[]{:S(2)}) collective-permute-start(bf16[4,16,768]{2,1,0:T(8,128)(2,1)S(1)} %pad_maximum_fusion.7.refs_0_), channel_id=1, source_target_pairs={{0,6},{2,4},{4,2},{6,0},{8,14},{10,12},{12,10},{14,8},{16,22},{18,... | collective-permute-start | bytes 294920 | tf_op jit(solution)/shard_map/ppermute | solution.py:78
  29.1 20.5 %collective-permute-start.15 = (bf16[48,3072]{1,0:T(8,128)(2,1)S(1)}, bf16[48,3072]{1,0:T(8,128)(2,1)S(1)}, u32[]{:S(2)}, u32[]{:S(2)}) collective-permute-start(bf16[48,3072]{1,0:T(8,128)(2,1)S(1)} %pad_maximum_fusion.3), channel_id=1, source_target_pairs={{0,24},{2,26},{4,28},{6,30},{8,0},{10,2},{12,4},{14,6},{16,8},{18,... | collective-permute-start | bytes 884744 | tf_op jit(solution)/shard_map/ppermute | solution.py:81
  37.5 15.4 %collective-permute-start.6 = (f32[32,2304]{1,0:T(8,128)}, f32[32,2304]{1,0:T(8,128)S(1)}, u32[]{:S(2)}, u32[]{:S(2)}) collective-permute-start(f32[32,2304]{1,0:T(8,128)} %bitcast.166), channel_id=1, source_target_pairs={{0,2},{2,0},{4,6},{6,4},{8,10},{10,8},{12,14},{14,12},{16,18},{18,... | collective-permute-start | bytes 884744 | tf_op jit(solution)/shard_map/ppermute | solution.py:78
  38.0 14.9 %collective-permute-start.7 = (f32[32,2304]{1,0:T(8,128)}, f32[32,2304]{1,0:T(8,128)S(1)}, u32[]{:S(2)}, u32[]{:S(2)}) collective-permute-start(f32[32,2304]{1,0:T(8,128)} %bitcast.165), channel_id=1, source_target_pairs={{0,4},{2,6},{4,0},{6,2},{8,12},{10,14},{12,8},{14,10},{16,20},{18,... | collective-permute-start | bytes 884744 | tf_op jit(solution)/shard_map/ppermute | solution.py:78
  39.6 13.4 %collective-permute-start.8 = (f32[32,2304]{1,0:T(8,128)}, f32[32,2304]{1,0:T(8,128)S(1)}, u32[]{:S(2)}, u32[]{:S(2)}) collective-permute-start(f32[32,2304]{1,0:T(8,128)} %bitcast.164), channel_id=1, source_target_pairs={{0,6},{2,4},{4,2},{6,0},{8,14},{10,12},{12,10},{14,8},{16,22},{18,... | collective-permute-start | bytes 884744 | tf_op jit(solution)/shard_map/ppermute | solution.py:78
  49.8 25.7 %collective-permute-start.18 = (bf16[4,48,1536]{2,1,0:T(8,128)(2,1)S(1)}, bf16[4,48,1536]{2,1,0:T(8,128)(2,1)S(1)}, u32[]{:S(2)}, u32[]{:S(2)}) collective-permute-start(bf16[4,48,1536]{2,1,0:T(8,128)(2,1)S(1)} %pad_maximum_fusion.refs_3_.refs_9_), channel_id=1, source_target_pairs={{0,6},{2,4},{4,2},{6,0},{8,14},{10,12},{12,10},{14,8},{16,22},{18,... | collective-permute-start | bytes 1769480 | tf_op jit(solution)/shard_map/ppermute | solution.py:78
  52.4 33.6 %collective-permute-start.16 = (bf16[4,48,1536]{2,1,0:T(8,128)(2,1)S(1)}, bf16[4,48,1536]{2,1,0:T(8,128)(2,1)S(1)}, u32[]{:S(2)}, u32[]{:S(2)}) collective-permute-start(bf16[4,48,1536]{2,1,0:T(8,128)(2,1)S(1)} %pad_maximum_fusion.refs_3_.refs_9_), channel_id=1, source_target_pairs={{0,2},{2,0},{4,6},{6,4},{8,10},{10,8},{12,14},{14,12},{16,18},{18,... | collective-permute-start | bytes 1769480 | tf_op jit(solution)/shard_map/ppermute | solution.py:78
  53.9 13.9 %collective-permute-start.10 = (f32[8,2304]{1,0:T(8,128)S(1)}, f32[8,2304]{1,0:T(8,128)S(1)}, u32[]{:S(2)}, u32[]{:S(2)}) collective-permute-start(f32[8,2304]{1,0:T(8,128)S(1)} %get-tuple-element.205), channel_id=1, source_target_pairs={{0,16},{2,18},{4,20},{6,22},{8,24},{10,26},{12,28},{14,30},{16,0},... | collective-permute-start | bytes 221192 | tf_op jit(solution)/shard_map/ppermute | solution.py:81
  59.1 9.7 %collective-permute-start.11 = (f32[8,2304]{1,0:T(8,128)S(1)}, f32[8,2304]{1,0:T(8,128)S(1)}, u32[]{:S(2)}, u32[]{:S(2)}) collective-permute-start(f32[8,2304]{1,0:T(8,128)S(1)} %get-tuple-element.204), channel_id=1, source_target_pairs={{0,24},{2,26},{4,28},{6,30},{8,0},{10,2},{12,4},{14,6},{16,8},{18,... | collective-permute-start | bytes 221192 | tf_op jit(solution)/shard_map/ppermute | solution.py:81
  62.5 6.8 %collective-permute-start.9 = (f32[8,2304]{1,0:T(8,128)S(1)}, f32[8,2304]{1,0:T(8,128)S(1)}, u32[]{:S(2)}, u32[]{:S(2)}) collective-permute-start(f32[8,2304]{1,0:T(8,128)S(1)} %get-tuple-element.203), channel_id=1, source_target_pairs={{0,8},{2,10},{4,12},{6,14},{8,16},{10,18},{12,20},{14,22},{16,24},... | collective-permute-start | bytes 221192 | tf_op jit(solution)/shard_map/ppermute | solution.py:81
  67.9 18.1 %collective-permute-start.17 = (bf16[4,48,1536]{2,1,0:T(8,128)(2,1)S(1)}, bf16[4,48,1536]{2,1,0:T(8,128)(2,1)S(1)}, u32[]{:S(2)}, u32[]{:S(2)}) collective-permute-start(bf16[4,48,1536]{2,1,0:T(8,128)(2,1)S(1)} %pad_maximum_fusion.refs_3_.refs_9_), channel_id=1, source_target_pairs={{0,4},{2,6},{4,0},{6,2},{8,12},{10,14},{12,8},{14,10},{16,20},{18,... | collective-permute-start | bytes 1769480 | tf_op jit(solution)/shard_map/ppermute | solution.py:78
  68.8 19.8 %collective-permute-start.19 = (bf16[4,48,1536]{2,1,0:T(8,128)(2,1)S(1)}, bf16[4,48,1536]{2,1,0:T(8,128)(2,1)S(1)}, u32[]{:S(2)}, u32[]{:S(2)}) collective-permute-start(bf16[4,48,1536]{2,1,0:T(8,128)(2,1)S(1)} %pad_maximum_fusion.refs_3_.refs_9_), channel_id=1, source_target_pairs={{0,1},{1,0},{2,3},{3,2},{4,5},{5,4},{6,7},{7,6},{8,9},{9,8},{10,11... | collective-permute-start | bytes 1769480 | tf_op jit(solution)/shard_map/ppermute | solution.py:68
  70.3 16.1 %collective-permute-start.12 = (f32[4,2304]{1,0:T(4,128)S(1)}, f32[4,2304]{1,0:T(4,128)S(1)}, u32[]{:S(2)}, u32[]{:S(2)}) collective-permute-start(f32[4,2304]{1,0:T(4,128)S(1)} %constant_dynamic-slice_fusion.2), channel_id=1, source_target_pairs={{0,1},{1,0},{2,3},{3,2},{4,5},{5,4},{6,7},{7,6},{8,9},{9,8},{10,11... | collective-permute-start | bytes 110600 | tf_op jit(solution)/shard_map/ppermute | solution.py:68
  75.4 13.7 %collective-permute-start.22 = (bf16[4,48,1536]{2,1,0:T(8,128)(2,1)S(1)}, bf16[4,48,1536]{2,1,0:T(8,128)(2,1)S(1)}, u32[]{:S(2)}, u32[]{:S(2)}) collective-permute-start(bf16[4,48,1536]{2,1,0:T(8,128)(2,1)S(1)} %collective-permute-done.18.refs_6_.refs_12_), channel_id=1, source_target_pairs={{0,1},{1,0},{2,3},{3,2},{4,5},{5,4},{6,7},{7,6},{8,9},{9,8},{10,11... | collective-permute-start | bytes 1769480 | tf_op jit(solution)/shard_map/ppermute | solution.py:68
  85.9 4.7 collective-permute-start.20
  86.0 4.7 collective-permute-start.21
  87.1 30.3 %collective-permute-start.24 = (bf16[4,48,1536]{2,1,0:T(8,128)(2,1)S(1)}, bf16[4,48,1536]{2,1,0:T(8,128)(2,1)S(1)}, u32[]{:S(2)}, u32[]{:S(2)}) collective-permute-start(bf16[4,48,1536]{2,1,0:T(8,128)(2,1)S(1)} %pad_maximum_fusion.1.refs_3_), channel_id=1, source_target_pairs={{0,2},{2,0},{4,6},{6,4},{8,10},{10,8},{12,14},{14,12},{16,18},{18,... | collective-permute-start | bytes 1769480 | tf_op jit(solution)/shard_map/ppermute | solution.py:78
  88.6 29.8 %collective-permute-start.25 = (bf16[4,48,1536]{2,1,0:T(8,128)(2,1)S(1)}, bf16[4,48,1536]{2,1,0:T(8,128)(2,1)S(1)}, u32[]{:S(2)}, u32[]{:S(2)}) collective-permute-start(bf16[4,48,1536]{2,1,0:T(8,128)(2,1)S(1)} %pad_maximum_fusion.1.refs_3_), channel_id=1, source_target_pairs={{0,4},{2,6},{4,0},{6,2},{8,12},{10,14},{12,8},{14,10},{16,20},{18,... | collective-permute-start | bytes 1769480 | tf_op jit(solution)/shard_map/ppermute | solution.py:78
  89.2 41.3 %collective-permute-start.26 = (bf16[4,48,1536]{2,1,0:T(8,128)(2,1)S(1)}, bf16[4,48,1536]{2,1,0:T(8,128)(2,1)S(1)}, u32[]{:S(2)}, u32[]{:S(2)}) collective-permute-start(bf16[4,48,1536]{2,1,0:T(8,128)(2,1)S(1)} %pad_maximum_fusion.1.refs_3_), channel_id=1, source_target_pairs={{0,6},{2,4},{4,2},{6,0},{8,14},{10,12},{12,10},{14,8},{16,22},{18,... | collective-permute-start | bytes 1769480 | tf_op jit(solution)/shard_map/ppermute | solution.py:78
  116.6 13.9 %collective-permute-start.23 = (f32[32,768]{1,0:T(8,128)}, f32[32,768]{1,0:T(8,128)S(1)}, u32[]{:S(2)}, u32[]{:S(2)}) collective-permute-start(f32[32,768]{1,0:T(8,128)} %get-tuple-element.90.refs_0_.refs_9_.refs_3_), channel_id=1, source_target_pairs={{0,1},{1,0},{2,3},{3,2},{4,5},{5,4},{6,7},{7,6},{8,9},{9,8},{10,11... | collective-permute-start | bytes 294920 | tf_op jit(solution)/shard_map/ppermute | solution.py:68
  136.3 8.7 %collective-permute-start.27 = (bf16[64,1152]{1,0:T(8,128)(2,1)}, bf16[64,1152]{1,0:T(8,128)(2,1)S(1)}, u32[]{:S(2)}, u32[]{:S(2)}) collective-permute-start(bf16[64,1152]{1,0:T(8,128)(2,1)} %get-tuple-element.93.refs_1_.refs_0_), channel_id=1, source_target_pairs={{0,8},{2,10},{4,12},{6,14},{8,16},{10,18},{12,20},{14,22},{16,24},... | collective-permute-start | bytes 442376 | tf_op jit(solution)/shard_map/ppermute | solution.py:81
  140.5 9.9 %collective-permute-start.28 = (bf16[64,1152]{1,0:T(8,128)(2,1)}, bf16[64,1152]{1,0:T(8,128)(2,1)S(1)}, u32[]{:S(2)}, u32[]{:S(2)}) collective-permute-start(bf16[64,1152]{1,0:T(8,128)(2,1)} %get-tuple-element.93.refs_1_.refs_0_), channel_id=1, source_target_pairs={{0,16},{2,18},{4,20},{6,22},{8,24},{10,26},{12,28},{14,30},{16,0},... | collective-permute-start | bytes 442376 | tf_op jit(solution)/shard_map/ppermute | solution.py:81
  140.5 9.9 %collective-permute-start.29 = (bf16[64,1152]{1,0:T(8,128)(2,1)}, bf16[64,1152]{1,0:T(8,128)(2,1)S(1)}, u32[]{:S(2)}, u32[]{:S(2)}) collective-permute-start(bf16[64,1152]{1,0:T(8,128)(2,1)} %get-tuple-element.93.refs_1_.refs_0_), channel_id=1, source_target_pairs={{0,24},{2,26},{4,28},{6,30},{8,0},{10,2},{12,4},{14,6},{16,8},{18,... | collective-permute-start | bytes 442376 | tf_op jit(solution)/shard_map/ppermute | solution.py:81
  151.4 24.9 %collective-permute-start.30 = (bf16[4,64,1152]{2,1,0:T(8,128)(2,1)S(1)}, bf16[4,64,1152]{2,1,0:T(8,128)(2,1)S(1)}, u32[]{:S(2)}, u32[]{:S(2)}) collective-permute-start(bf16[4,64,1152]{2,1,0:T(8,128)(2,1)S(1)} %pad_maximum_fusion.2.refs_0_.refs_6_.refs_9_.refs_16_), channel_id=1, source_target_pairs={{0,2},{2,0},{4,6},{6,4},{8,10},{10,8},{12,14},{14,12},{16,18},{18,... | collective-permute-start | bytes 1769480 | tf_op jit(solution)/shard_map/ppermute | solution.py:78
  152.1 27.5 %collective-permute-start.31 = (bf16[4,64,1152]{2,1,0:T(8,128)(2,1)S(1)}, bf16[4,64,1152]{2,1,0:T(8,128)(2,1)S(1)}, u32[]{:S(2)}, u32[]{:S(2)}) collective-permute-start(bf16[4,64,1152]{2,1,0:T(8,128)(2,1)S(1)} %pad_maximum_fusion.2.refs_0_.refs_6_.refs_9_.refs_16_), channel_id=1, source_target_pairs={{0,4},{2,6},{4,0},{6,2},{8,12},{10,14},{12,8},{14,10},{16,20},{18,... | collective-permute-start | bytes 1769480 | tf_op jit(solution)/shard_map/ppermute | solution.py:78
  153.6 26.0 %collective-permute-start.32 = (bf16[4,64,1152]{2,1,0:T(8,128)(2,1)S(1)}, bf16[4,64,1152]{2,1,0:T(8,128)(2,1)S(1)}, u32[]{:S(2)}, u32[]{:S(2)}) collective-permute-start(bf16[4,64,1152]{2,1,0:T(8,128)(2,1)S(1)} %pad_maximum_fusion.2.refs_0_.refs_6_.refs_9_.refs_16_), channel_id=1, source_target_pairs={{0,6},{2,4},{4,2},{6,0},{8,14},{10,12},{12,10},{14,8},{16,22},{18,... | collective-permute-start | bytes 1769480 | tf_op jit(solution)/shard_map/ppermute | solution.py:78
  188.4 1.6 collective-permute-start.33
  202.1 1.6 collective-permute-start.34
  212.4 27.9 %collective-permute-start.35 = (bf16[64,512]{1,0:T(8,128)(2,1)}, bf16[64,512]{1,0:T(8,128)(2,1)S(1)}, u32[]{:S(2)}, u32[]{:S(2)}) collective-permute-start(bf16[64,512]{1,0:T(8,128)(2,1)} %get-tuple-element.109.refs_8_), channel_id=1, source_target_pairs={{0,8},{2,10},{4,12},{6,14},{8,16},{10,18},{12,20},{14,22},{16,24},... | collective-permute-start | bytes 196616 | tf_op jit(solution)/shard_map/ppermute | solution.py:81
  216.2 24.2 %collective-permute-start.36 = (bf16[64,512]{1,0:T(8,128)(2,1)}, bf16[64,512]{1,0:T(8,128)(2,1)S(1)}, u32[]{:S(2)}, u32[]{:S(2)}) collective-permute-start(bf16[64,512]{1,0:T(8,128)(2,1)} %get-tuple-element.109.refs_8_), channel_id=1, source_target_pairs={{0,16},{2,18},{4,20},{6,22},{8,24},{10,26},{12,28},{14,30},{16,0},... | collective-permute-start | bytes 196616 | tf_op jit(solution)/shard_map/ppermute | solution.py:81
  218.5 21.9 %collective-permute-start.37 = (bf16[64,512]{1,0:T(8,128)(2,1)}, bf16[64,512]{1,0:T(8,128)(2,1)S(1)}, u32[]{:S(2)}, u32[]{:S(2)}) collective-permute-start(bf16[64,512]{1,0:T(8,128)(2,1)} %get-tuple-element.109.refs_8_), channel_id=1, source_target_pairs={{0,24},{2,26},{4,28},{6,30},{8,0},{10,2},{12,4},{14,6},{16,8},{18,... | collective-permute-start | bytes 196616 | tf_op jit(solution)/shard_map/ppermute | solution.py:81
  253.4 25.0 %collective-permute-start.43 = (bf16[768,3072]{1,0:T(8,128)(2,1)}, bf16[768,3072]{1,0:T(8,128)(2,1)}, u32[]{:S(2)}, u32[]{:S(2)}) collective-permute-start(bf16[768,3072]{1,0:T(8,128)(2,1)} %wide_gradients.2.refs_1_.refs_0_), channel_id=1, source_target_pairs={{0,1},{1,0},{2,3},{3,2},{4,5},{5,4},{6,7},{7,6},{8,9},{9,8},{10,11... | collective-permute-start | bytes 14155784 | tf_op jit(solution)/shard_map/ppermute | solution.py:68
  253.5 43.6 %collective-permute-start.38 = (f32[1024,768]{1,0:T(8,128)S(1)}, f32[1024,768]{1,0:T(8,128)}, u32[]{:S(2)}, u32[]{:S(2)}) collective-permute-start(f32[1024,768]{1,0:T(8,128)S(1)} %copy-done.1), channel_id=1, source_target_pairs={{0,1},{1,0},{2,3},{3,2},{4,5},{5,4},{6,7},{7,6},{8,9},{9,8},{10,11... | collective-permute-start | bytes 9437192 | tf_op jit(solution)/shard_map/ppermute | solution.py:68
  254.0 9.3 %collective-permute-start.40 = (bf16[4,64,512]{2,1,0:T(8,128)(2,1)S(1)}, bf16[4,64,512]{2,1,0:T(8,128)(2,1)}, u32[]{:S(2)}, u32[]{:S(2)}) collective-permute-start(bf16[4,64,512]{2,1,0:T(8,128)(2,1)S(1)} %copy-done.2), channel_id=1, source_target_pairs={{0,2},{2,0},{4,6},{6,4},{8,10},{10,8},{12,14},{14,12},{16,18},{18,... | collective-permute-start | bytes 786440 | tf_op jit(solution)/shard_map/ppermute | solution.py:78
  255.4 13.7 %collective-permute-start.41 = (bf16[4,64,512]{2,1,0:T(8,128)(2,1)S(1)}, bf16[4,64,512]{2,1,0:T(8,128)(2,1)}, u32[]{:S(2)}, u32[]{:S(2)}) collective-permute-start(bf16[4,64,512]{2,1,0:T(8,128)(2,1)S(1)} %copy-done.2), channel_id=1, source_target_pairs={{0,4},{2,6},{4,0},{6,2},{8,12},{10,14},{12,8},{14,10},{16,20},{18,... | collective-permute-start | bytes 786440 | tf_op jit(solution)/shard_map/ppermute | solution.py:78
  256.1 13.0 %collective-permute-start.42 = (bf16[4,64,512]{2,1,0:T(8,128)(2,1)S(1)}, bf16[4,64,512]{2,1,0:T(8,128)(2,1)}, u32[]{:S(2)}, u32[]{:S(2)}) collective-permute-start(bf16[4,64,512]{2,1,0:T(8,128)(2,1)S(1)} %copy-done.2), channel_id=1, source_target_pairs={{0,6},{2,4},{4,2},{6,0},{8,14},{10,12},{12,10},{14,8},{16,22},{18,... | collective-permute-start | bytes 786440 | tf_op jit(solution)/shard_map/ppermute | solution.py:78
  291.2 93.8 %all-to-all-start = ((bf16[4,192,4608]{2,1,0:T(8,128)(2,1)}), bf16[4,192,4608]{2,1,0:T(8,128)(2,1)}, u32[]{:S(2)}, u32[]{:S(2)}) async-start(bf16[4,192,4608]{2,1,0:T(8,128)(2,1)} %bitcast.136), calls=%async_computation | async-start | bytes 14155776 | tf_op jit(solution)/shard_map/all_to_all | solution.py:124
  297.0 4.0 collective-permute-start.44
  362.3 11.8 %collective-permute-start.50 = (bf16[768,1536]{1,0:T(8,128)(2,1)}, bf16[768,1536]{1,0:T(8,128)(2,1)S(1)}, u32[]{:S(2)}, u32[]{:S(2)}) collective-permute-start(bf16[768,1536]{1,0:T(8,128)(2,1)} %attention_gradients.2), channel_id=1, source_target_pairs={{0,1},{1,0},{2,3},{3,2},{4,5},{5,4},{6,7},{7,6},{8,9},{9,8},{10,11... | collective-permute-start | bytes 7077896 | tf_op jit(solution)/shard_map/ppermute | solution.py:68
  362.8 6.1 %collective-permute-start.47 = (bf16[32,768]{1,0:T(8,128)(2,1)S(1)}, bf16[32,768]{1,0:T(8,128)(2,1)S(1)}, u32[]{:S(2)}, u32[]{:S(2)}) collective-permute-start(bf16[32,768]{1,0:T(8,128)(2,1)S(1)} %copy-done.19), channel_id=1, source_target_pairs={{0,8},{2,10},{4,12},{6,14},{8,16},{10,18},{12,20},{14,22},{16,24},... | collective-permute-start | bytes 147464 | tf_op jit(solution)/shard_map/ppermute | solution.py:81
  364.6 5.8 %collective-permute-start.48 = (bf16[32,768]{1,0:T(8,128)(2,1)S(1)}, bf16[32,768]{1,0:T(8,128)(2,1)S(1)}, u32[]{:S(2)}, u32[]{:S(2)}) collective-permute-start(bf16[32,768]{1,0:T(8,128)(2,1)S(1)} %copy-done.19), channel_id=1, source_target_pairs={{0,16},{2,18},{4,20},{6,22},{8,24},{10,26},{12,28},{14,30},{16,0},... | collective-permute-start | bytes 147464 | tf_op jit(solution)/shard_map/ppermute | solution.py:81
  365.3 5.1 %collective-permute-start.49 = (bf16[32,768]{1,0:T(8,128)(2,1)S(1)}, bf16[32,768]{1,0:T(8,128)(2,1)S(1)}, u32[]{:S(2)}, u32[]{:S(2)}) collective-permute-start(bf16[32,768]{1,0:T(8,128)(2,1)S(1)} %copy-done.19), channel_id=1, source_target_pairs={{0,24},{2,26},{4,28},{6,30},{8,0},{10,2},{12,4},{14,6},{16,8},{18,... | collective-permute-start | bytes 147464 | tf_op jit(solution)/shard_map/ppermute | solution.py:81
  367.1 53.0 %collective-permute-start.45 = (f32[1024,768]{1,0:T(8,128)}, f32[1024,768]{1,0:T(8,128)}, u32[]{:S(2)}, u32[]{:S(2)}) collective-permute-start(f32[1024,768]{1,0:T(8,128)} %get-tuple-element.134), channel_id=1, source_target_pairs={{0,1},{1,0},{2,3},{3,2},{4,5},{5,4},{6,7},{7,6},{8,9},{9,8},{10,11... | collective-permute-start | bytes 9437192 | tf_op jit(solution)/shard_map/ppermute | solution.py:68
  370.5 19.7 %collective-permute-start.51 = (bf16[4,32,768]{2,1,0:T(8,128)(2,1)S(1)}, bf16[4,32,768]{2,1,0:T(8,128)(2,1)S(1)}, u32[]{:S(2)}, u32[]{:S(2)}) collective-permute-start(bf16[4,32,768]{2,1,0:T(8,128)(2,1)S(1)} %pad_maximum_fusion.6.refs_0_.refs_6_), channel_id=1, source_target_pairs={{0,2},{2,0},{4,6},{6,4},{8,10},{10,8},{12,14},{14,12},{16,18},{18,... | collective-permute-start | bytes 589832 | tf_op jit(solution)/shard_map/ppermute | solution.py:78
  372.5 17.7 %collective-permute-start.52 = (bf16[4,32,768]{2,1,0:T(8,128)(2,1)S(1)}, bf16[4,32,768]{2,1,0:T(8,128)(2,1)S(1)}, u32[]{:S(2)}, u32[]{:S(2)}) collective-permute-start(bf16[4,32,768]{2,1,0:T(8,128)(2,1)S(1)} %pad_maximum_fusion.6.refs_0_.refs_6_), channel_id=1, source_target_pairs={{0,4},{2,6},{4,0},{6,2},{8,12},{10,14},{12,8},{14,10},{16,20},{18,... | collective-permute-start | bytes 589832 | tf_op jit(solution)/shard_map/ppermute | solution.py:78
  374.0 16.2 %collective-permute-start.53 = (bf16[4,32,768]{2,1,0:T(8,128)(2,1)S(1)}, bf16[4,32,768]{2,1,0:T(8,128)(2,1)S(1)}, u32[]{:S(2)}, u32[]{:S(2)}) collective-permute-start(bf16[4,32,768]{2,1,0:T(8,128)(2,1)S(1)} %pad_maximum_fusion.6.refs_0_.refs_6_), channel_id=1, source_target_pairs={{0,6},{2,4},{4,2},{6,0},{8,14},{10,12},{12,10},{14,8},{16,22},{18,... | collective-permute-start | bytes 589832 | tf_op jit(solution)/shard_map/ppermute | solution.py:78
  409.6 58.7 %all-to-all-start.2 = ((bf16[4,48,4608]{2,1,0:T(8,128)(2,1)}), bf16[4,48,4608]{2,1,0:T(8,128)(2,1)S(1)}, u32[]{:S(2)}, u32[]{:S(2)}) async-start(bf16[4,48,4608]{2,1,0:T(8,128)(2,1)} %bitcast.82.refs_1_), calls=%async_computation.2 | async-start | bytes 3538944 | tf_op jit(solution)/shard_map/all_to_all | solution.py:134
  413.2 16.6 %collective-permute-start.56 = (bf16[192,1536]{1,0:T(8,128)(2,1)}, bf16[192,1536]{1,0:T(8,128)(2,1)}, u32[]{:S(2)}, u32[]{:S(2)}) collective-permute-start(bf16[192,1536]{1,0:T(8,128)(2,1)} %get-tuple-element.151), channel_id=1, source_target_pairs={{0,2},{2,0},{4,6},{6,4},{8,10},{10,8},{12,14},{14,12},{16,18},{18,... | collective-permute-start | bytes 1769480 | tf_op jit(solution)/shard_map/ppermute | solution.py:78
  413.9 24.8 %collective-permute-start.57 = (bf16[192,1536]{1,0:T(8,128)(2,1)}, bf16[192,1536]{1,0:T(8,128)(2,1)}, u32[]{:S(2)}, u32[]{:S(2)}) collective-permute-start(bf16[192,1536]{1,0:T(8,128)(2,1)} %get-tuple-element.152), channel_id=1, source_target_pairs={{0,4},{2,6},{4,0},{6,2},{8,12},{10,14},{12,8},{14,10},{16,20},{18,... | collective-permute-start | bytes 1769480 | tf_op jit(solution)/shard_map/ppermute | solution.py:78
  414.4 24.3 %collective-permute-start.58 = (bf16[192,1536]{1,0:T(8,128)(2,1)}, bf16[192,1536]{1,0:T(8,128)(2,1)}, u32[]{:S(2)}, u32[]{:S(2)}) collective-permute-start(bf16[192,1536]{1,0:T(8,128)(2,1)} %get-tuple-element.153), channel_id=1, source_target_pairs={{0,6},{2,4},{4,2},{6,0},{8,14},{10,12},{12,10},{14,8},{16,22},{18,... | collective-permute-start | bytes 1769480 | tf_op jit(solution)/shard_map/ppermute | solution.py:78
  418.1 1.3 collective-permute-start.46
  424.1 40.7 %collective-permute-start.55 = (f32[56,4608]{1,0:T(8,128)S(1)}, f32[56,4608]{1,0:T(8,128)}, u32[]{:S(2)}, u32[]{:S(2)}) collective-permute-start(f32[56,4608]{1,0:T(8,128)S(1)} %copy-done.10), channel_id=1, source_target_pairs={{0,1},{1,0},{2,3},{3,2},{4,5},{5,4},{6,7},{7,6},{8,9},{9,8},{10,11... | collective-permute-start | bytes 3096584 | tf_op jit(solution)/shard_map/ppermute | solution.py:68
  440.1 7.2 %collective-permute-start.54 = (f32[4,768]{1,0:T(4,128)S(1)}, f32[4,768]{1,0:T(4,128)S(1)}, u32[]{:S(2)}, u32[]{:S(2)}) collective-permute-start(f32[4,768]{1,0:T(4,128)S(1)} %reshape.342), channel_id=1, source_target_pairs={{0,1},{1,0},{2,3},{3,2},{4,5},{5,4},{6,7},{7,6},{8,9},{9,8},{10,11... | collective-permute-start | bytes 36872 | tf_op jit(solution)/shard_map/ppermute | solution.py:68
  441.8 8.6 %collective-permute-start.59 = (bf16[48,1536]{1,0:T(8,128)(2,1)S(1)}, bf16[48,1536]{1,0:T(8,128)(2,1)S(1)}, u32[]{:S(2)}, u32[]{:S(2)}) collective-permute-start(bf16[48,1536]{1,0:T(8,128)(2,1)S(1)} %get-tuple-element.200), channel_id=1, source_target_pairs={{0,8},{2,10},{4,12},{6,14},{8,16},{10,18},{12,20},{14,22},{16,24},... | collective-permute-start | bytes 442376 | tf_op jit(solution)/shard_map/ppermute | solution.py:81
  443.5 18.7 %collective-permute-start.60 = (bf16[48,1536]{1,0:T(8,128)(2,1)S(1)}, bf16[48,1536]{1,0:T(8,128)(2,1)S(1)}, u32[]{:S(2)}, u32[]{:S(2)}) collective-permute-start(bf16[48,1536]{1,0:T(8,128)(2,1)S(1)} %get-tuple-element.202), channel_id=1, source_target_pairs={{0,16},{2,18},{4,20},{6,22},{8,24},{10,26},{12,28},{14,30},{16,0},... | collective-permute-start | bytes 442376 | tf_op jit(solution)/shard_map/ppermute | solution.py:81
  445.8 16.4 %collective-permute-start.61 = (bf16[48,1536]{1,0:T(8,128)(2,1)S(1)}, bf16[48,1536]{1,0:T(8,128)(2,1)S(1)}, u32[]{:S(2)}, u32[]{:S(2)}) collective-permute-start(bf16[48,1536]{1,0:T(8,128)(2,1)S(1)} %get-tuple-element.201), channel_id=1, source_target_pairs={{0,24},{2,26},{4,28},{6,30},{8,0},{10,2},{12,4},{14,6},{16,8},{18,... | collective-permute-start | bytes 442376 | tf_op jit(solution)/shard_map/ppermute | solution.py:81
  (48 other events, 469.3 us)
Sparse Core Ops, SparseCore 0:
  10.9 119.6 all-gather.1

commit v3 on v2

--- a/solution.py
+++ b/solution.py
@@ -121,11 +121,16 @@
             return value
         rows, columns = value.shape
         groups = [[4 * z + here for here in range(4)] for z in range(4)]
-        value = lax.all_to_all(
+        return lax.all_to_all(
             value.reshape(4, rows // 4, columns), "dp", 0, 0, axis_index_groups=groups, tiled=True
         )
+
+    def square_sums(self, value):
+        if not self.staged:
+            return value
+        _, rows, columns = value.shape
         total = sum(value[number].astype(UPPER) for number in range(4)).astype(value.dtype)
-        return total.reshape(4, rows // 16, columns)
+        return total.reshape(4, rows // 4, columns)
 
     def line_to_own(self, value):
         if not self.staged:
@@ -691,59 +696,39 @@
     )
 
 
-def wide_gradients(move, side, lefts, rights, lat_lefts, lat_rights, came=(), before=(), after=(), tile=768):
-    features, total = lefts[0].shape
-    units = rights[0].shape[1] // 2
+def wide_gradients(move, at, left, right, lat_left, lat_right, before=(), after=(), tile=768):
+    features, total = left.shape
+    units = right.shape[1] // 2
     tiles = units // tile
-    nb, nk = move.blocks
-    extra = len(came)
-
-    def kernel(info, *refs):
-        outs = refs[8 + extra :]
-        step = pl.program_id(1)
-        for which in range(2):
-            left, right, lat_left, lat_right = [refs[2 * number + which] for number in range(4)]
-
-            @pl.when(pl.program_id(0) == which)
-            def _():
-                acc = mm_tn(lat_left[...], lat_right[...]) + mm(left[...], right[...])
-                if side == 1:
-                    outs[0][...] = acc.astype(LOWER)
-                else:
-                    outs[-1][...] = (acc + refs[8][...].astype(UPPER)).astype(LOWER)
-
-        if side == 0:
-            place_square(move.staged, outs[-1], outs[0], 0, tile)
-
-    def columns(rows, which):
-        def at(w, s, info):
-            core = info[0] if side == 0 else 1 - info[0]
-            held = (tiles - 1) if which == 0 else 0
-            return (0, core * tiles + jnp.where(w == which, s, held))
-
-        return pl.BlockSpec((rows, tile), at)
-
-    here = lambda w, s, info: (0, w * tiles + s)
-    offset = 0 if side == 1 else before[0].shape[1] // tile - 2 * tiles
-    out_at = lambda w, s, info: (0, offset + w * tiles + s)
-    shapes = [part.shape for part in before] if side == 0 else [(features, 2 * units)]
+
+    def kernel(info, left_ref, right_ref, lat_l, lat_r, out):
+        acc = mm_tn(lat_l[...], lat_r[...]) + mm(left_ref[...], right_ref[...])
+        out[...] = acc.astype(LOWER)
+
+    columns = lambda rows: pl.BlockSpec((rows, tile), lambda s, info: (0, s))
     return call(
         kernel,
         move.info,
-        [(part, whole(part.shape)) for part in lefts]
-        + [(part, columns(part.shape[0], which)) for which, part in enumerate(rights)]
-        + [(part, whole(part.shape)) for part in lat_lefts]
-        + [(part, columns(part.shape[0], which)) for which, part in enumerate(lat_rights)]
-        + [(part, pl.BlockSpec((features, tile), here)) for part in came],
-        [(shape, LOWER, pl.BlockSpec((shape[0], tile), out_at)) for shape in shapes],
-        [pltpu.VMEM((features, tile), LOWER)] if side == 0 else [],
-        grid=(2, tiles),
+        [
+            (left, whole(left.shape)),
+            (right, columns(total)),
+            (lat_left, whole(lat_left.shape)),
+            (lat_right, columns(lat_right.shape[0])),
+        ],
+        [
+            (
+                (2 * features, 2 * units),
+                LOWER,
+                pl.BlockSpec((features, tile), lambda s, info: (s // tiles, at * tiles + s % tiles)),
+            )
+        ],
+        grid=(2 * tiles,),
         flops=total * features * units * 4,
         moved=total * units * 4 + features * units * 4,
         name="wide_gradients",
         aliased=before,
         after=after,
-    )
+    )[0]
 
 
 def modulation_terms(move, vectors, modulator, bias, middle):
@@ -1035,7 +1020,7 @@
     )
 
 
-def latent_sources(move, key_value, gathered, came, weights, masks, grad_query, lat_in, out_grad, lat_own, lat_other, gain, half, features, room, after=()):
+def latent_sources(move, key_value, gathered, came, weights, masks, grad_query, lat_in, out_grad, lat_own, lat_other, gain, half, features, after=()):
     count = key_value.shape[0]
     np_ = len(came)
     total = np_ * came[0].shape[0] * count
@@ -1104,7 +1089,7 @@
         + [(piece, ANY) for piece in came + gathered],
         [(part, UPPER, whole(part))] * 2
         + [((8, features), UPPER, whole((8, features)))]
-        + [((features, columns + room), LOWER, whole((features, columns)))],
+        + [((features, columns), LOWER, whole((features, columns)))],
         [
             pltpu.VMEM((total, 2 * half + 128), LOWER),
             pltpu.VMEM((count, features), UPPER),
@@ -1303,14 +1288,21 @@
             move, part, own - part, after, token_cotangent, mod_two, wide_w, sizes, ff, [sent]
         )
         token_result, grad_tok, ff_inputs, ff_narrow, ff_hidden, ff_upward, ff_vec, token_output = ff
-        factors = (
-            [ff_inputs, ff_narrow],
-            [ff_upward, ff_hidden],
-            [lat_inputs, lat_narrow],
-            [lat_upward, lat_hidden],
-        )
-        (wide_other,) = wide_gradients(move, 1, *factors, after=[came_line])
-        lat_grad_own, lat_grad_other, gain_rows, *lat_parts = latent_sources(
+        wide_parts = wide_gradients(
+            move, 0, ff_inputs, ff_upward, lat_inputs, lat_upward, after=[came_line]
+        )
+        wide_parts = wide_gradients(
+            move, 1, ff_narrow, ff_hidden, lat_narrow, lat_hidden, [wide_parts], came[1:]
+        )
+        if move.staged:
+            wide_sum = lax.psum_scatter(wide_parts, ("mp", "dp"), scatter_dimension=0, tiled=True)
+        else:
+            wide_sum = lax.psum_scatter(wide_parts, "mp", scatter_dimension=0, tiled=True)
+            wide_sum = lax.psum_scatter(
+                wide_sum.astype(UPPER), "dp", scatter_dimension=0, tiled=True
+            )
+        wide_sum = wide_sum.astype(UPPER)
+        lat_grad_own, lat_grad_other, gain_rows, early_parts = latent_sources(
             move,
             lat_triple,
             key_values,
@@ -1325,11 +1317,7 @@
             gain,
             half,
             features,
-            2 * units,
-            after=[wide_other],
-        )
-        (early_parts,) = wide_gradients(
-            move, 0, *factors, came=[move.swap(wide_other)], before=lat_parts
+            after=[wide_parts],
         )
         early_line = move.square_to_line(early_parts)
         grad_lat_one, grad_att, gate_vec = attention_entry(
@@ -1343,10 +1331,9 @@
             grad_tok,
             attended,
             sizes,
-            after=[early_parts],
-        )
-
-        token_output = fill(move, token_output, move.swap(token_result), [wide_other])
+        )
+
+        token_output = fill(move, token_output, move.swap(token_result), [wide_parts])
 
         grad_tokens, grad_latents, first_in, first_triples, vec_one, grad_output = attention_backward(
             move,
@@ -1373,24 +1360,26 @@
         ).astype(LOWER)
         vectors_line = move.line(vectors)
         first_factors = (first_in, first_triples, grad_att, mixed, half)
-        (first_grads_other,) = attention_gradients(move, 1, *first_factors, after=[vectors])
+        early_line = move.square_sums(wait_for(early_line, vectors))
+        (first_grads_other,) = attention_gradients(
+            move, 1, *first_factors, after=[vectors, early_line]
+        )
         first_parts = attention_gradients(
             move, 0, *first_factors, [move.swap(first_grads_other)], [vectors_line]
         )
         first_terms = move.meet(first_parts)
-        early_sum = move.line_to_own(early_line)
+        early_sum = move.line_to_own(wait_for(early_line, first_parts[0]))
         mod_grad, grad_terms = modulation_gradients(
             move,
             picked,
             move.spread(vectors_line, chips=True),
             modulator,
             dp_size,
-            after=[first_parts[0], early_line],
-        )
-        grad_output = fill(move, grad_output, move.swap(grad_tokens))
-        first_sum = move.finish(
-            move.fold(wait_for(first_terms, grad_output, mod_grad))
-        )
+            after=[first_parts[0]],
+        )
+        first_sums = move.fold(wait_for(first_terms, mod_grad))
+        first_sum = move.finish(first_sums)
+        grad_output = fill(move, grad_output, move.swap(grad_tokens), [first_sums[-1]])
         mod_grad = mod_grad + move.swap(mod_grad)
         grad_scaled = lax.all_to_all(grad_terms, "dp", 0, 0, tiled=True)
         grad_scaled = grad_scaled.transpose(1, 0, 2).reshape(own, features)
@@ -1413,8 +1402,8 @@
             early_sum[:, : 3 * half].reshape(shard, 3, half),
             early_sum[:, 3 * half : 4 * half],
             gain_grad,
-            early_sum[:, 4 * half : 4 * half + units],
-            early_sum[:, 4 * half + units :],
+            wide_sum[:, :units],
+            wide_sum[:, units:],
         )
 
     return body

time: 487 us -> 488 us (level)
  blocking collectives: 13.3 us -> 0 us
  waiting for transfers between devices: 102 us -> 115 us
    all_to_all x1 -> x0, blocking collectives: 13.3 us -> none  [body(): grad_scaled = lax.all_to_all(grad_terms, 'dp', 0, 0, tiled=True)]
    all_to_all x0 -> x1, waiting for transfers between devices: none -> 6.42 us  [body(): grad_scaled = lax.all_to_all(grad_terms, 'dp', 0, 0, tiled=True)]
    ppermute x24, waiting for transfers between devices: 58.3 us -> 63.9 us  [flip(): return lax.ppermute(value, 'dp', [(d, d ^ bits) for d in range(16)])]
  transfers between devices with their start and end apart: 65 -> 66, of which waited for: 23 -> 21; matrix products, arithmetic and copies ran while one was open for 7% -> 7% of each run, Pallas kernels for 37% -> 37%
where the time goes in v3:
time: 488 us; the launch traced here: 478 us
  Pallas kernels  214 us (44%)
  waiting for transfers between devices  115 us (24%)
  starting transfers between devices  86.9 us (18%)
  local copies, waits for them, and re-layouts  27.3 us (6%)
  other arithmetic  19.7 us (4%)
  between operations  15.2 us (3%)
    pallas_call x18, Pallas kernels, call(): pl.pallas_call(inner, input_output_aliases={1 + number: number for number...  214 us
    ppermute x24, waiting for transfers between devices, flip(): return lax.ppermute(value, 'dp', [(d, d ^ bits) for d in range(16)])  63.9 us
    ppermute x21, starting transfers between devices, turn(): lax.ppermute(value, 'dp', [(d, (d + 4 * step) % 16) for d in range(16)])  43 us
    ppermute x21, waiting for transfers between devices, turn(): lax.ppermute(value, 'dp', [(d, (d + 4 * step) % 16) for d in range(16)])  40.7 us
    ppermute x24, starting transfers between devices, flip(): return lax.ppermute(value, 'dp', [(d, d ^ bits) for d in range(16)])  29.5 us
    unnamed x96, local copies, waits for them, and re-layouts  10.8 us
  transfers between devices with their start and end apart: 66, of which 21 were waited for; matrix products, arithmetic and copies ran while one was open for 7% of the time, Pallas kernels for 37%

profile of v3, /device:TPU:0, one launch (start us, length us, event | category | flops | bytes accessed | tf_op | source)
XLA Modules:
  0.0 478.3 jit_solution(3861308967631985456)
XLA Ops:
  10.8 3.1 collective-permute-start
  14.0 2.6 collective-permute-start.1
  22.0 1.6 collective-permute-start.3
  23.5 1.5 collective-permute-start.4
  27.3 1.8 collective-permute-done.3.refs_1_
  29.2 3.3 collective-permute-start.15
  33.7 3.8 modulation_terms.1
  38.0 1.5 collective-permute-start.7
  41.0 8.6 %collective-permute-done.14 = bf16[48,3072]{1,0:T(8,128)(2,1)S(1)} collective-permute-done((bf16[48,3072]{1,0:T(8,128)(2,1)S(1)}, bf16[48,3072]{1,0:T(8,128)(2,1)S(1)}, u32[]{:S(2)}, u32[]{:S(2)}) %collective-permute-start.14) | collective-permute-done | bytes 294944 | tf_op jit(solution)/shard_map/ppermute | solution.py:81
  49.8 2.6 collective-permute-start.18
  54.0 5.2 %collective-permute-start.10 = (f32[8,2304]{1,0:T(8,128)S(1)}, f32[8,2304]{1,0:T(8,128)S(1)}, u32[]{:S(2)}, u32[]{:S(2)}) collective-permute-start(f32[8,2304]{1,0:T(8,128)S(1)} %get-tuple-element.209), channel_id=1, source_target_pairs={{0,16},{2,18},{4,20},{6,22},{8,24},{10,26},{12,28},{14,30},{16,0},... | collective-permute-start | bytes 221192 | tf_op jit(solution)/shard_map/ppermute | solution.py:81
  59.2 3.4 collective-permute-start.11
  62.6 5.0 %collective-permute-done.10 = f32[8,2304]{1,0:T(8,128)S(1)} collective-permute-done((f32[8,2304]{1,0:T(8,128)S(1)}, f32[8,2304]{1,0:T(8,128)S(1)}, u32[]{:S(2)}, u32[]{:S(2)}) %collective-permute-start.10) | collective-permute-done | bytes 73760 | tf_op jit(solution)/shard_map/ppermute | solution.py:81
  70.5 4.9 %collective-permute-done.18.refs_6_.refs_12_ = bf16[4,48,1536]{2,1,0:T(8,128)(2,1)S(1)} collective-permute-done((bf16[4,48,1536]{2,1,0:T(8,128)(2,1)S(1)}, bf16[4,48,1536]{2,1,0:T(8,128)(2,1)S(1)}, u32[]{:S(2)}, u32[]{:S(2)}) %collective-permute-start.18) | collective-permute-done | bytes 589856 | tf_op jit(solution)/shard_map/ppermute | solution.py:78
  75.5 10.5 %collective-permute-done.16.refs_4_.refs_10_ = bf16[4,48,1536]{2,1,0:T(8,128)(2,1)S(1)} collective-permute-done((bf16[4,48,1536]{2,1,0:T(8,128)(2,1)S(1)}, bf16[4,48,1536]{2,1,0:T(8,128)(2,1)S(1)}, u32[]{:S(2)}, u32[]{:S(2)}) %collective-permute-start.16) | collective-permute-done | bytes 589856 | tf_op jit(solution)/shard_map/ppermute | solution.py:78
  87.2 1.5 collective-permute-start.24
  89.2 1.5 collective-permute-start.26
  92.3 24.3 %attention_forward.1 = (f32[1024,768]{1,0:T(8,128)}, f32[32,768]{1,0:T(8,128)}, bf16[1088,2304]{1,0:T(8,128)(2,1)}, f32[4,12,272]{2,1,0:T(8,128)}, bf16[1088,768]{1,0:T(8,128)(2,1)}, /*index=5*/bf16[1088,768]{1,0:T(8,128)(2,1)}) custom-call(s32[34]{0:T(128)} %stack.215.info_ref, f32[2048,768]{1,0:T(8,128)} %refs_1_.3, f32[64,768]{1,0:T(8,128)} %refs_2_.3, ...), custom_call_target="tpu_custom_call" | custom-call | flops 10267656192 | bytes 16000000 | tf_op jit(solution)/shard_map/attention_forward/pallas_call | solution.py:169
  118.4 12.1 %collective-permute-done.26.refs_6_ = bf16[4,48,1536]{2,1,0:T(8,128)(2,1)S(1)} collective-permute-done((bf16[4,48,1536]{2,1,0:T(8,128)(2,1)S(1)}, bf16[4,48,1536]{2,1,0:T(8,128)(2,1)S(1)}, u32[]{:S(2)}, u32[]{:S(2)}) %collective-permute-start.26) | collective-permute-done | bytes 589856 | tf_op jit(solution)/shard_map/ppermute | solution.py:78
  131.4 4.9 %latent_project.1 = (bf16[64,1152]{1,0:T(8,128)(2,1)}, bf16[64,768]{1,0:T(8,128)(2,1)}, bf16[768,1536]{1,0:T(8,128)(2,1)}) custom-call(s32[34]{0:T(128)} %stack.215.info_ref, f32[32,768]{1,0:T(8,128)} %get-tuple-element.92.refs_0_.refs_9_.refs_2_, f32[32,768]{1,0:T(8,128)} %copy-done.17, f32[1,768]{1,0:T(1,128)} %get-tuple-element.93.refs_2_.refs_11_.refs_4_, ...), custom_call_target="tpu_custom_call" | custom-call | flops 500000000 | bytes 6000000 | tf_op jit(solution)/shard_map/latent_project/pallas_call | solution.py:169
  136.3 4.2 collective-permute-start.27
  140.5 2.6 collective-permute-start.29
  145.0 5.3 %collective-permute-done.28 = bf16[64,1152]{1,0:T(8,128)(2,1)S(1)} collective-permute-done((bf16[64,1152]{1,0:T(8,128)(2,1)}, bf16[64,1152]{1,0:T(8,128)(2,1)S(1)}, u32[]{:S(2)}, u32[]{:S(2)}) %collective-permute-start.28) | collective-permute-done | bytes 147488 | tf_op jit(solution)/shard_map/ppermute | solution.py:81
  152.1 1.5 collective-permute-start.31
  154.9 21.3 %token_feed_forward.2 = (f32[1024,768]{1,0:T(8,128)}, f32[1024,768]{1,0:T(8,128)}, bf16[768,1024]{1,0:T(8,128)(2,1)}, bf16[768,1024]{1,0:T(8,128)(2,1)}, bf16[10...) custom-call(s32[34]{0:T(128)} %stack.215.info_ref, ...), custom_call_target="tpu_custom_call" | custom-call | flops 9663676416 | bytes 16000000 | tf_op jit(solution)/shard_map/token_feed_forward/pallas_call | solution.py:169
  176.2 3.4 collective-permute-done.31.refs_8_.refs_11_.refs_18_
  180.6 7.7 %latent_forward.1 = (bf16[64,384]{1,0:T(8,128)(2,1)}, f32[64,128]{1,0:T(8,128)}, f32[32,768]{1,0:T(8,128)}, f32[32,768]{1,0:T(8,128)}) custom-call(s32[34]{0:T(128)} %stack.215.info_ref, f32[4,3,768]{2,1,0:T(4,128)} %get-tuple-element.103.refs_0_.refs_6_, bf16[64,1152]{1,0:T(8,128)(2,1)} %get-tuple-element.95.refs_1_.refs_0_, ...), custom_call_target="tpu_custom_call" | custom-call | flops 1000000000 | bytes 6000000 | tf_op jit(solution)/shard_map/latent_forward/pallas_call | solution.py:169
  188.4 1.5 collective-permute-done.33.refs_2_
  190.6 11.5 %latent_feed_forward.1 = (f32[32,768]{1,0:T(8,128)}, f32[32,768]{1,0:T(8,128)}, bf16[32,768]{1,0:T(8,128)(2,1)}, bf16[32,768]{1,0:T(8,128)(2,1)}, bf16[32,3072]{...) custom-call(s32[34]{0:T(128)} %stack.215.info_ref, ...), custom_call_target="tpu_custom_call" | custom-call | flops 2415919104 | bytes 12000000 | tf_op jit(solution)/shard_map/latent_feed_forward/pallas_call | solution.py:169
  204.3 8.1 %latent_backward.1 = (bf16[64,512]{1,0:T(8,128)(2,1)}, bf16[64,384]{1,0:T(8,128)(2,1)}, f32[768,384]{1,0:T(8,128)}) custom-call(s32[34]{0:T(128)} %stack.215.info_ref, bf16[64,1152]{1,0:T(8,128)(2,1)} %get-tuple-element.95.refs_1_.refs_0_, bf16[768,1536]{1,0:T(8,128)(2,1)} %get-tuple-element.105.refs_2_.refs_1_, s32[64,1]{1,0:T(8,128)} %copy.82.refs_3_.refs_2_, ...), custom_call_target="tpu_custom_call" | custom-call | flops 1500000000 | bytes 6000000 | tf_op jit(solution)/shard_map/latent_backward/pallas_call | solution.py:169
  212.4 3.8 collective-permute-start.35
  216.1 2.3 collective-permute-start.36
  218.6 21.6 %token_feed_forward.3 = (f32[1024,768]{1,0:T(8,128)}, f32[1024,768]{1,0:T(8,128)}, bf16[768,1024]{1,0:T(8,128)(2,1)}, bf16[768,1024]{1,0:T(8,128)(2,1)}, bf16[10...) custom-call(s32[34]{0:T(128)} %stack.215.info_ref, ...), custom_call_target="tpu_custom_call", output_to_operand_aliasing={{0}: (1, {}), {1}: (2, {}), {2}: (3, {}), {3}: (4, {}), {4}... | custom-call | flops 9663676416 | bytes 16000000 | tf_op jit(solution)/shard_map/token_feed_forward/pallas_call | solution.py:169
  243.9 10.7 %wide_gradients.2.refs_0_ = bf16[1536,3072]{1,0:T(8,128)(2,1)} custom-call(s32[34]{0:T(128)} %stack.215.info_ref, bf16[4,64,512]{2,1,0:T(8,128)(2,1)} %copy-done.10, bf16[768,1024]{1,0:T(8,128)(2,1)} %get-tuple-element.113.refs_1_, bf16[1024,3072]{1,0:T(8,128)(2,1)} %get-tuple-element.114.refs_2_, bf16[32,768]{1,0:T(8,128)(2,1)} %get-tuple-element.115.refs_3_, ...), custom_call_target="tpu_custom_call" | custom-call | flops 4831838208 | bytes 11010048 | tf_op jit(solution)/shard_map/wide_gradients/pallas_call | solution.py:169
  255.7 10.9 %wide_gradients.3.refs_1_.refs_0_ = bf16[1536,3072]{1,0:T(8,128)(2,1)} custom-call(s32[34]{0:T(128)} %stack.215.info_ref, bf16[1536,3072]{1,0:T(8,128)(2,1)} %wide_gradients.2.refs_0_, bf16[4,64,512]{2,1,0:T(8,128)(2,1)} %copy-done.7, bf16[4,64,512]{2,1,0:T(8,128)(2,1)} %copy-done.8, bf16[4,64,512]{2,1,0:T(8,128)(2,1)} %copy-done.9, ...), custom_call_target="tpu_custom_call", output_to_operand_aliasing={{}: (1, {})} | custom-call | flops 4831838208 | bytes 11010048 | tf_op jit(solution)/shard_map/wide_gradients/pallas_call | solution.py:169
  268.2 9.4 %latent_sources.1 = (f32[32,768]{1,0:T(8,128)}, f32[32,768]{1,0:T(8,128)}, f32[8,768]{1,0:T(8,128)}, bf16[768,1536]{1,0:T(8,128)(2,1)}) custom-call(s32[34]{0:T(128)} %stack.215.info_ref, bf16[1536,3072]{1,0:T(8,128)(2,1)} %wide_gradients.3.refs_1_.refs_0_, bf16[64,1152]{1,0:T(8,128)(2,1)} %get-tuple-element.95.refs_1_.refs_0_, ...), custom_call_target="tpu_custom_call" | custom-call | flops 2000000000 | bytes 8000000 | tf_op jit(solution)/shard_map/latent_sources/pallas_call | solution.py:169
  277.7 3.8 all-to-all-start
  283.7 5.9 %attention_entry.1 = (f32[32,768]{1,0:T(8,128)}, bf16[1088,768]{1,0:T(8,128)(2,1)}, f32[4,1,768]{2,1,0:T(1,128)}) custom-call(s32[34]{0:T(128)} %stack.215.info_ref, f32[32,768]{1,0:T(8,128)} %get-tuple-element.127.refs_0_, f32[32,768]{1,0:T(8,128)} %copy-done.33, f32[32,768]{1,0:T(8,128)} %get-tuple-element.92.refs_0_.refs_9_.refs_2_, ...), custom_call_target="tpu_custom_call" | custom-call | flops 8355840 | bytes 10000000 | tf_op jit(solution)/shard_map/attention_entry/pallas_call | solution.py:169
  290.3 4.0 fill.2.refs_0_
  294.3 43.4 %attention_backward.1 = (f32[1024,768]{1,0:T(8,128)}, f32[32,768]{1,0:T(8,128)}, bf16[1088,768]{1,0:T(8,128)(2,1)}, bf16[1088,2304]{1,0:T(8,128)(2,1)}, f32[4,2,768]{2,1,0:T(2,128)}, /*index=5*/f32[2048,768]{1,0:T(8,128)}) custom-call(s32[34]{0:T(128)} %stack.215.info_ref, f32[2048,768]{1,0:T(8,128)} %fill.2.refs_0_, f32[2048,768]{1,0:T(8,128)} %refs_1_.3, ...), custom_call_target="tpu_custom_call" | custom-call | flops 12834570240 | bytes 20000000 | tf_op jit(solution)/shard_map/attention_backward/pallas_call | solution.py:169
  338.5 2.5 concatenate.147.refs_0_
  342.1 9.0 %attention_gradients.2 = bf16[768,1536]{1,0:T(8,128)(2,1)} custom-call(s32[34]{0:T(128)} %stack.215.info_ref, bf16[32,768]{1,0:T(8,128)(2,1)} %concatenate.147.refs_0_, bf16[4,48,1536]{2,1,0:T(8,128)(2,1)} %bitcast.82.refs_1_, bf16[1088,768]{1,0:T(8,128)(2,1)} %get-tuple-element.140.refs_2_.refs_1_, bf16[1088,2304]{1,0:T(8,128)(2,1)} %get-tuple-element.141.refs_3_.refs_2_, ...), custom_call_target="tpu_custom_call" | custom-call | flops 2566914048 | bytes 5013504 | tf_op jit(solution)/shard_map/attention_gradients/pallas_call | solution.py:169
  351.5 1.7 collective-permute-start.44
  353.8 2.0 collective-permute-start.46
  355.9 2.1 collective-permute-done.44
  358.0 1.6 collective-permute-done.45
  359.7 1.8 collective-permute-start.51
  361.4 1.5 collective-permute-start.52
  362.9 9.5 %attention_gradients.3 = (bf16[192,1536]{1,0:T(8,128)(2,1)}, bf16[192,1536]{1,0:T(8,128)(2,1)}, bf16[192,1536]{1,0:T(8,128)(2,1)}, bf16[192,1536]{1,0:T(8,128)(2,1)}) custom-call(s32[34]{0:T(128)} %stack.215.info_ref, bf16[4,32,768]{2,1,0:T(8,128)(2,1)} %copy-done.6, bf16[1088,768]{1,0:T(8,128)(2,1)} %get-tuple-element.140.refs_2_.refs_1_, ...), custom_call_target="tpu_custom_call" | custom-call | flops 2566914048 | bytes 5013504 | tf_op jit(solution)/shard_map/attention_gradients/pallas_call | solution.py:169
  373.8 2.1 collective-permute-start.50
  376.7 29.9 %collective-permute-done.53.refs_8_ = bf16[4,32,768]{2,1,0:T(8,128)(2,1)S(1)} collective-permute-done((bf16[4,32,768]{2,1,0:T(8,128)(2,1)}, bf16[4,32,768]{2,1,0:T(8,128)(2,1)S(1)}, u32[]{:S(2)}, u32[]{:S(2)}) %collective-permute-start.53) | collective-permute-done | bytes 196640 | tf_op jit(solution)/shard_map/ppermute | solution.py:78
  407.4 4.5 modulation_gradients.1
  413.4 4.0 all-to-all-start.1
  418.2 6.4 %all-to-all-done.1 = f32[16,1,192]{2,1,0:T(1,128)S(1)} async-done(((f32[16,1,192]{2,1,0:T(1,128)}), f32[16,1,192]{2,1,0:T(1,128)S(1)}, u32[]{:S(2)}, u32[]{:S(2)}) %all-to-all-start.1) | async-done | bytes 12320 | tf_op jit(solution)/shard_map/all_to_all | solution.py:1384
  424.7 4.1 all-to-all-start.2
  430.3 1.7 add_convert_fusion.2
  432.1 2.0 collective-permute-start.58
  434.1 2.4 collective-permute-start.59
  438.6 8.5 %collective-permute-done.58 = bf16[48,1536]{1,0:T(8,128)(2,1)S(1)} collective-permute-done((bf16[48,1536]{1,0:T(8,128)(2,1)S(1)}, bf16[48,1536]{1,0:T(8,128)(2,1)S(1)}, u32[]{:S(2)}, u32[]{:S(2)}) %collective-permute-start.58) | collective-permute-done | bytes 147488 | tf_op jit(solution)/shard_map/ppermute | solution.py:81
  447.0 7.7 %collective-permute-done.59 = bf16[48,1536]{1,0:T(8,128)(2,1)S(1)} collective-permute-done((bf16[48,1536]{1,0:T(8,128)(2,1)S(1)}, bf16[48,1536]{1,0:T(8,128)(2,1)S(1)}, u32[]{:S(2)}, u32[]{:S(2)}) %collective-permute-start.59) | collective-permute-done | bytes 147488 | tf_op jit(solution)/shard_map/ppermute | solution.py:81
  457.3 1.8 copy-done.1
  459.1 3.8 fill.3
  465.5 1.6 add.381
  469.4 1.8 fusion.19
  (266 shorter events, 62.6 us)
Async XLA Ops:
  7.2 147.7 %all-gather.2.cloned.1.call-start = ((), (), s32[]{:S(2)}) async-start(), calls=%async_computation.4 | async-start | bytes 9732096 | tf_op jit(solution)/shard_map/all_gather | solution.py:1205
  9.1 460.3 %reduce-scatter.2.cloned.1.call-start = ((), (), s32[]{:S(2)}) async-start(), calls=%async_computation.5 | async-start | bytes 9732096 | tf_op jit(solution)/shard_map/reduce_scatter | solution.py:1298
  10.8 11.1 %collective-permute-start = (bf16[16,768]{1,0:T(8,128)(2,1)S(1)}, bf16[16,768]{1,0:T(8,128)(2,1)S(1)}, u32[]{:S(2)}, u32[]{:S(2)}) collective-permute-start(bf16[16,768]{1,0:T(8,128)(2,1)S(1)} %get-tuple-element.229), channel_id=1, source_target_pairs={{0,8},{2,10},{4,12},{6,14},{8,16},{10,18},{12,20},{14,22},{16,24},... | collective-permute-start | bytes 73736 | tf_op jit(solution)/shard_map/ppermute | solution.py:81
  14.0 7.9 %collective-permute-start.1 = (bf16[16,768]{1,0:T(8,128)(2,1)S(1)}, bf16[16,768]{1,0:T(8,128)(2,1)S(1)}, u32[]{:S(2)}, u32[]{:S(2)}) collective-permute-start(bf16[16,768]{1,0:T(8,128)(2,1)S(1)} %get-tuple-element.229), channel_id=1, source_target_pairs={{0,16},{2,18},{4,20},{6,22},{8,24},{10,26},{12,28},{14,30},{16,0},... | collective-permute-start | bytes 73736 | tf_op jit(solution)/shard_map/ppermute | solution.py:81
  16.6 5.4 %collective-permute-start.2 = (bf16[16,768]{1,0:T(8,128)(2,1)S(1)}, bf16[16,768]{1,0:T(8,128)(2,1)S(1)}, u32[]{:S(2)}, u32[]{:S(2)}) collective-permute-start(bf16[16,768]{1,0:T(8,128)(2,1)S(1)} %get-tuple-element.229), channel_id=1, source_target_pairs={{0,24},{2,26},{4,28},{6,30},{8,0},{10,2},{12,4},{14,6},{16,8},{18,... | collective-permute-start | bytes 73736 | tf_op jit(solution)/shard_map/ppermute | solution.py:81
  20.7 18.8 %collective-permute-start.13 = (bf16[48,3072]{1,0:T(8,128)(2,1)S(1)}, bf16[48,3072]{1,0:T(8,128)(2,1)S(1)}, u32[]{:S(2)}, u32[]{:S(2)}) collective-permute-start(bf16[48,3072]{1,0:T(8,128)(2,1)S(1)} %pad_maximum_fusion.3), channel_id=1, source_target_pairs={{0,8},{2,10},{4,12},{6,14},{8,16},{10,18},{12,20},{14,22},{16,24},... | collective-permute-start | bytes 884744 | tf_op jit(solution)/shard_map/ppermute | solution.py:81
  21.5 28.1 %collective-permute-start.14 = (bf16[48,3072]{1,0:T(8,128)(2,1)S(1)}, bf16[48,3072]{1,0:T(8,128)(2,1)S(1)}, u32[]{:S(2)}, u32[]{:S(2)}) collective-permute-start(bf16[48,3072]{1,0:T(8,128)(2,1)S(1)} %pad_maximum_fusion.3), channel_id=1, source_target_pairs={{0,16},{2,18},{4,20},{6,22},{8,24},{10,26},{12,28},{14,30},{16,0},... | collective-permute-start | bytes 884744 | tf_op jit(solution)/shard_map/ppermute | solution.py:81
  22.0 7.2 %collective-permute-start.3 = (bf16[4,16,768]{2,1,0:T(8,128)(2,1)S(1)}, bf16[4,16,768]{2,1,0:T(8,128)(2,1)S(1)}, u32[]{:S(2)}, u32[]{:S(2)}) collective-permute-start(bf16[4,16,768]{2,1,0:T(8,128)(2,1)S(1)} %pad_maximum_fusion.7.refs_0_), channel_id=1, source_target_pairs={{0,2},{2,0},{4,6},{6,4},{8,10},{10,8},{12,14},{14,12},{16,18},{18,... | collective-permute-start | bytes 294920 | tf_op jit(solution)/shard_map/ppermute | solution.py:78
  23.5 8.9 %collective-permute-start.4 = (bf16[4,16,768]{2,1,0:T(8,128)(2,1)S(1)}, bf16[4,16,768]{2,1,0:T(8,128)(2,1)S(1)}, u32[]{:S(2)}, u32[]{:S(2)}) collective-permute-start(bf16[4,16,768]{2,1,0:T(8,128)(2,1)S(1)} %pad_maximum_fusion.7.refs_0_), channel_id=1, source_target_pairs={{0,4},{2,6},{4,0},{6,2},{8,12},{10,14},{12,8},{14,10},{16,20},{18,... | collective-permute-start | bytes 294920 | tf_op jit(solution)/shard_map/ppermute | solution.py:78
  25.1 7.4 %collective-permute-start.5 = (bf16[4,16,768]{2,1,0:T(8,128)(2,1)S(1)}, bf16[4,16,768]{2,1,0:T(8,128)(2,1)S(1)}, u32[]{:S(2)}, u32[]{:S(2)}) collective-permute-start(bf16[4,16,768]{2,1,0:T(8,128)(2,1)S(1)} %pad_maximum_fusion.7.refs_0_), channel_id=1, source_target_pairs={{0,6},{2,4},{4,2},{6,0},{8,14},{10,12},{12,10},{14,8},{16,22},{18,... | collective-permute-start | bytes 294920 | tf_op jit(solution)/shard_map/ppermute | solution.py:78
  29.2 20.5 %collective-permute-start.15 = (bf16[48,3072]{1,0:T(8,128)(2,1)S(1)}, bf16[48,3072]{1,0:T(8,128)(2,1)S(1)}, u32[]{:S(2)}, u32[]{:S(2)}) collective-permute-start(bf16[48,3072]{1,0:T(8,128)(2,1)S(1)} %pad_maximum_fusion.3), channel_id=1, source_target_pairs={{0,24},{2,26},{4,28},{6,30},{8,0},{10,2},{12,4},{14,6},{16,8},{18,... | collective-permute-start | bytes 884744 | tf_op jit(solution)/shard_map/ppermute | solution.py:81
  37.5 15.5 %collective-permute-start.6 = (f32[32,2304]{1,0:T(8,128)}, f32[32,2304]{1,0:T(8,128)S(1)}, u32[]{:S(2)}, u32[]{:S(2)}) collective-permute-start(f32[32,2304]{1,0:T(8,128)} %bitcast.166), channel_id=1, source_target_pairs={{0,2},{2,0},{4,6},{6,4},{8,10},{10,8},{12,14},{14,12},{16,18},{18,... | collective-permute-start | bytes 884744 | tf_op jit(solution)/shard_map/ppermute | solution.py:78
  38.0 14.9 %collective-permute-start.7 = (f32[32,2304]{1,0:T(8,128)}, f32[32,2304]{1,0:T(8,128)S(1)}, u32[]{:S(2)}, u32[]{:S(2)}) collective-permute-start(f32[32,2304]{1,0:T(8,128)} %bitcast.165), channel_id=1, source_target_pairs={{0,4},{2,6},{4,0},{6,2},{8,12},{10,14},{12,8},{14,10},{16,20},{18,... | collective-permute-start | bytes 884744 | tf_op jit(solution)/shard_map/ppermute | solution.py:78
  39.6 13.4 %collective-permute-start.8 = (f32[32,2304]{1,0:T(8,128)}, f32[32,2304]{1,0:T(8,128)S(1)}, u32[]{:S(2)}, u32[]{:S(2)}) collective-permute-start(f32[32,2304]{1,0:T(8,128)} %bitcast.164), channel_id=1, source_target_pairs={{0,6},{2,4},{4,2},{6,0},{8,14},{10,12},{12,10},{14,8},{16,22},{18,... | collective-permute-start | bytes 884744 | tf_op jit(solution)/shard_map/ppermute | solution.py:78
  49.8 25.7 %collective-permute-start.18 = (bf16[4,48,1536]{2,1,0:T(8,128)(2,1)S(1)}, bf16[4,48,1536]{2,1,0:T(8,128)(2,1)S(1)}, u32[]{:S(2)}, u32[]{:S(2)}) collective-permute-start(bf16[4,48,1536]{2,1,0:T(8,128)(2,1)S(1)} %pad_maximum_fusion.refs_3_.refs_9_), channel_id=1, source_target_pairs={{0,6},{2,4},{4,2},{6,0},{8,14},{10,12},{12,10},{14,8},{16,22},{18,... | collective-permute-start | bytes 1769480 | tf_op jit(solution)/shard_map/ppermute | solution.py:78
  52.4 33.6 %collective-permute-start.16 = (bf16[4,48,1536]{2,1,0:T(8,128)(2,1)S(1)}, bf16[4,48,1536]{2,1,0:T(8,128)(2,1)S(1)}, u32[]{:S(2)}, u32[]{:S(2)}) collective-permute-start(bf16[4,48,1536]{2,1,0:T(8,128)(2,1)S(1)} %pad_maximum_fusion.refs_3_.refs_9_), channel_id=1, source_target_pairs={{0,2},{2,0},{4,6},{6,4},{8,10},{10,8},{12,14},{14,12},{16,18},{18,... | collective-permute-start | bytes 1769480 | tf_op jit(solution)/shard_map/ppermute | solution.py:78
  54.0 13.7 %collective-permute-start.10 = (f32[8,2304]{1,0:T(8,128)S(1)}, f32[8,2304]{1,0:T(8,128)S(1)}, u32[]{:S(2)}, u32[]{:S(2)}) collective-permute-start(f32[8,2304]{1,0:T(8,128)S(1)} %get-tuple-element.209), channel_id=1, source_target_pairs={{0,16},{2,18},{4,20},{6,22},{8,24},{10,26},{12,28},{14,30},{16,0},... | collective-permute-start | bytes 221192 | tf_op jit(solution)/shard_map/ppermute | solution.py:81
  59.2 9.6 %collective-permute-start.11 = (f32[8,2304]{1,0:T(8,128)S(1)}, f32[8,2304]{1,0:T(8,128)S(1)}, u32[]{:S(2)}, u32[]{:S(2)}) collective-permute-start(f32[8,2304]{1,0:T(8,128)S(1)} %get-tuple-element.208), channel_id=1, source_target_pairs={{0,24},{2,26},{4,28},{6,30},{8,0},{10,2},{12,4},{14,6},{16,8},{18,... | collective-permute-start | bytes 221192 | tf_op jit(solution)/shard_map/ppermute | solution.py:81
  62.6 6.8 %collective-permute-start.9 = (f32[8,2304]{1,0:T(8,128)S(1)}, f32[8,2304]{1,0:T(8,128)S(1)}, u32[]{:S(2)}, u32[]{:S(2)}) collective-permute-start(f32[8,2304]{1,0:T(8,128)S(1)} %get-tuple-element.207), channel_id=1, source_target_pairs={{0,8},{2,10},{4,12},{6,14},{8,16},{10,18},{12,20},{14,22},{16,24},... | collective-permute-start | bytes 221192 | tf_op jit(solution)/shard_map/ppermute | solution.py:81
  67.7 18.3 %collective-permute-start.17 = (bf16[4,48,1536]{2,1,0:T(8,128)(2,1)S(1)}, bf16[4,48,1536]{2,1,0:T(8,128)(2,1)S(1)}, u32[]{:S(2)}, u32[]{:S(2)}) collective-permute-start(bf16[4,48,1536]{2,1,0:T(8,128)(2,1)S(1)} %pad_maximum_fusion.refs_3_.refs_9_), channel_id=1, source_target_pairs={{0,4},{2,6},{4,0},{6,2},{8,12},{10,14},{12,8},{14,10},{16,20},{18,... | collective-permute-start | bytes 1769480 | tf_op jit(solution)/shard_map/ppermute | solution.py:78
  68.8 19.8 %collective-permute-start.19 = (bf16[4,48,1536]{2,1,0:T(8,128)(2,1)S(1)}, bf16[4,48,1536]{2,1,0:T(8,128)(2,1)S(1)}, u32[]{:S(2)}, u32[]{:S(2)}) collective-permute-start(bf16[4,48,1536]{2,1,0:T(8,128)(2,1)S(1)} %pad_maximum_fusion.refs_3_.refs_9_), channel_id=1, source_target_pairs={{0,1},{1,0},{2,3},{3,2},{4,5},{5,4},{6,7},{7,6},{8,9},{9,8},{10,11... | collective-permute-start | bytes 1769480 | tf_op jit(solution)/shard_map/ppermute | solution.py:68
  70.3 16.2 %collective-permute-start.12 = (f32[4,2304]{1,0:T(4,128)S(1)}, f32[4,2304]{1,0:T(4,128)S(1)}, u32[]{:S(2)}, u32[]{:S(2)}) collective-permute-start(f32[4,2304]{1,0:T(4,128)S(1)} %constant_dynamic-slice_fusion.2), channel_id=1, source_target_pairs={{0,1},{1,0},{2,3},{3,2},{4,5},{5,4},{6,7},{7,6},{8,9},{9,8},{10,11... | collective-permute-start | bytes 110600 | tf_op jit(solution)/shard_map/ppermute | solution.py:68
  75.4 13.7 %collective-permute-start.22 = (bf16[4,48,1536]{2,1,0:T(8,128)(2,1)S(1)}, bf16[4,48,1536]{2,1,0:T(8,128)(2,1)S(1)}, u32[]{:S(2)}, u32[]{:S(2)}) collective-permute-start(bf16[4,48,1536]{2,1,0:T(8,128)(2,1)S(1)} %collective-permute-done.18.refs_6_.refs_12_), channel_id=1, source_target_pairs={{0,1},{1,0},{2,3},{3,2},{4,5},{5,4},{6,7},{7,6},{8,9},{9,8},{10,11... | collective-permute-start | bytes 1769480 | tf_op jit(solution)/shard_map/ppermute | solution.py:68
  86.0 4.7 collective-permute-start.20
  86.0 4.7 collective-permute-start.21
  87.2 30.4 %collective-permute-start.24 = (bf16[4,48,1536]{2,1,0:T(8,128)(2,1)S(1)}, bf16[4,48,1536]{2,1,0:T(8,128)(2,1)S(1)}, u32[]{:S(2)}, u32[]{:S(2)}) collective-permute-start(bf16[4,48,1536]{2,1,0:T(8,128)(2,1)S(1)} %pad_maximum_fusion.1.refs_3_), channel_id=1, source_target_pairs={{0,2},{2,0},{4,6},{6,4},{8,10},{10,8},{12,14},{14,12},{16,18},{18,... | collective-permute-start | bytes 1769480 | tf_op jit(solution)/shard_map/ppermute | solution.py:78
  88.7 29.8 %collective-permute-start.25 = (bf16[4,48,1536]{2,1,0:T(8,128)(2,1)S(1)}, bf16[4,48,1536]{2,1,0:T(8,128)(2,1)S(1)}, u32[]{:S(2)}, u32[]{:S(2)}) collective-permute-start(bf16[4,48,1536]{2,1,0:T(8,128)(2,1)S(1)} %pad_maximum_fusion.1.refs_3_), channel_id=1, source_target_pairs={{0,4},{2,6},{4,0},{6,2},{8,12},{10,14},{12,8},{14,10},{16,20},{18,... | collective-permute-start | bytes 1769480 | tf_op jit(solution)/shard_map/ppermute | solution.py:78
  89.2 41.3 %collective-permute-start.26 = (bf16[4,48,1536]{2,1,0:T(8,128)(2,1)S(1)}, bf16[4,48,1536]{2,1,0:T(8,128)(2,1)S(1)}, u32[]{:S(2)}, u32[]{:S(2)}) collective-permute-start(bf16[4,48,1536]{2,1,0:T(8,128)(2,1)S(1)} %pad_maximum_fusion.1.refs_3_), channel_id=1, source_target_pairs={{0,6},{2,4},{4,2},{6,0},{8,14},{10,12},{12,10},{14,8},{16,22},{18,... | collective-permute-start | bytes 1769480 | tf_op jit(solution)/shard_map/ppermute | solution.py:78
  116.7 13.9 %collective-permute-start.23 = (f32[32,768]{1,0:T(8,128)}, f32[32,768]{1,0:T(8,128)S(1)}, u32[]{:S(2)}, u32[]{:S(2)}) collective-permute-start(f32[32,768]{1,0:T(8,128)} %get-tuple-element.92.refs_0_.refs_9_.refs_2_), channel_id=1, source_target_pairs={{0,1},{1,0},{2,3},{3,2},{4,5},{5,4},{6,7},{7,6},{8,9},{9,8},{10,11... | collective-permute-start | bytes 294920 | tf_op jit(solution)/shard_map/ppermute | solution.py:68
  136.3 8.7 %collective-permute-start.27 = (bf16[64,1152]{1,0:T(8,128)(2,1)}, bf16[64,1152]{1,0:T(8,128)(2,1)S(1)}, u32[]{:S(2)}, u32[]{:S(2)}) collective-permute-start(bf16[64,1152]{1,0:T(8,128)(2,1)} %get-tuple-element.95.refs_1_.refs_0_), channel_id=1, source_target_pairs={{0,8},{2,10},{4,12},{6,14},{8,16},{10,18},{12,20},{14,22},{16,24},... | collective-permute-start | bytes 442376 | tf_op jit(solution)/shard_map/ppermute | solution.py:81
  140.5 9.9 %collective-permute-start.28 = (bf16[64,1152]{1,0:T(8,128)(2,1)}, bf16[64,1152]{1,0:T(8,128)(2,1)S(1)}, u32[]{:S(2)}, u32[]{:S(2)}) collective-permute-start(bf16[64,1152]{1,0:T(8,128)(2,1)} %get-tuple-element.95.refs_1_.refs_0_), channel_id=1, source_target_pairs={{0,16},{2,18},{4,20},{6,22},{8,24},{10,26},{12,28},{14,30},{16,0},... | collective-permute-start | bytes 442376 | tf_op jit(solution)/shard_map/ppermute | solution.py:81
  140.5 9.9 %collective-permute-start.29 = (bf16[64,1152]{1,0:T(8,128)(2,1)}, bf16[64,1152]{1,0:T(8,128)(2,1)S(1)}, u32[]{:S(2)}, u32[]{:S(2)}) collective-permute-start(bf16[64,1152]{1,0:T(8,128)(2,1)} %get-tuple-element.95.refs_1_.refs_0_), channel_id=1, source_target_pairs={{0,24},{2,26},{4,28},{6,30},{8,0},{10,2},{12,4},{14,6},{16,8},{18,... | collective-permute-start | bytes 442376 | tf_op jit(solution)/shard_map/ppermute | solution.py:81
  151.3 24.9 %collective-permute-start.30 = (bf16[4,64,1152]{2,1,0:T(8,128)(2,1)S(1)}, bf16[4,64,1152]{2,1,0:T(8,128)(2,1)S(1)}, u32[]{:S(2)}, u32[]{:S(2)}) collective-permute-start(bf16[4,64,1152]{2,1,0:T(8,128)(2,1)S(1)} %pad_maximum_fusion.2.refs_0_.refs_6_.refs_9_.refs_16_), channel_id=1, source_target_pairs={{0,2},{2,0},{4,6},{6,4},{8,10},{10,8},{12,14},{14,12},{16,18},{18,... | collective-permute-start | bytes 1769480 | tf_op jit(solution)/shard_map/ppermute | solution.py:78
  152.1 27.5 %collective-permute-start.31 = (bf16[4,64,1152]{2,1,0:T(8,128)(2,1)S(1)}, bf16[4,64,1152]{2,1,0:T(8,128)(2,1)S(1)}, u32[]{:S(2)}, u32[]{:S(2)}) collective-permute-start(bf16[4,64,1152]{2,1,0:T(8,128)(2,1)S(1)} %pad_maximum_fusion.2.refs_0_.refs_6_.refs_9_.refs_16_), channel_id=1, source_target_pairs={{0,4},{2,6},{4,0},{6,2},{8,12},{10,14},{12,8},{14,10},{16,20},{18,... | collective-permute-start | bytes 1769480 | tf_op jit(solution)/shard_map/ppermute | solution.py:78
  153.6 26.0 %collective-permute-start.32 = (bf16[4,64,1152]{2,1,0:T(8,128)(2,1)S(1)}, bf16[4,64,1152]{2,1,0:T(8,128)(2,1)S(1)}, u32[]{:S(2)}, u32[]{:S(2)}) collective-permute-start(bf16[4,64,1152]{2,1,0:T(8,128)(2,1)S(1)} %pad_maximum_fusion.2.refs_0_.refs_6_.refs_9_.refs_16_), channel_id=1, source_target_pairs={{0,6},{2,4},{4,2},{6,0},{8,14},{10,12},{12,10},{14,8},{16,22},{18,... | collective-permute-start | bytes 1769480 | tf_op jit(solution)/shard_map/ppermute | solution.py:78
  188.4 1.6 collective-permute-start.33
  212.4 27.9 %collective-permute-start.35 = (bf16[64,512]{1,0:T(8,128)(2,1)}, bf16[64,512]{1,0:T(8,128)(2,1)S(1)}, u32[]{:S(2)}, u32[]{:S(2)}) collective-permute-start(bf16[64,512]{1,0:T(8,128)(2,1)} %get-tuple-element.111.refs_8_), channel_id=1, source_target_pairs={{0,8},{2,10},{4,12},{6,14},{8,16},{10,18},{12,20},{14,22},{16,24},... | collective-permute-start | bytes 196616 | tf_op jit(solution)/shard_map/ppermute | solution.py:81
  216.1 24.1 %collective-permute-start.36 = (bf16[64,512]{1,0:T(8,128)(2,1)}, bf16[64,512]{1,0:T(8,128)(2,1)S(1)}, u32[]{:S(2)}, u32[]{:S(2)}) collective-permute-start(bf16[64,512]{1,0:T(8,128)(2,1)} %get-tuple-element.111.refs_8_), channel_id=1, source_target_pairs={{0,16},{2,18},{4,20},{6,22},{8,24},{10,26},{12,28},{14,30},{16,0},... | collective-permute-start | bytes 196616 | tf_op jit(solution)/shard_map/ppermute | solution.py:81
  218.5 21.8 %collective-permute-start.37 = (bf16[64,512]{1,0:T(8,128)(2,1)}, bf16[64,512]{1,0:T(8,128)(2,1)S(1)}, u32[]{:S(2)}, u32[]{:S(2)}) collective-permute-start(bf16[64,512]{1,0:T(8,128)(2,1)} %get-tuple-element.111.refs_8_), channel_id=1, source_target_pairs={{0,24},{2,26},{4,28},{6,30},{8,0},{10,2},{12,4},{14,6},{16,8},{18,... | collective-permute-start | bytes 196616 | tf_op jit(solution)/shard_map/ppermute | solution.py:81
  240.3 14.2 %collective-permute-start.38 = (bf16[4,64,512]{2,1,0:T(8,128)(2,1)S(1)}, bf16[4,64,512]{2,1,0:T(8,128)(2,1)S(1)}, u32[]{:S(2)}, u32[]{:S(2)}) collective-permute-start(bf16[4,64,512]{2,1,0:T(8,128)(2,1)S(1)} %pad_maximum_fusion.5.refs_0_.refs_12_), channel_id=1, source_target_pairs={{0,2},{2,0},{4,6},{6,4},{8,10},{10,8},{12,14},{14,12},{16,18},{18,... | collective-permute-start | bytes 786440 | tf_op jit(solution)/shard_map/ppermute | solution.py:78
  241.7 13.2 %collective-permute-start.39 = (bf16[4,64,512]{2,1,0:T(8,128)(2,1)S(1)}, bf16[4,64,512]{2,1,0:T(8,128)(2,1)S(1)}, u32[]{:S(2)}, u32[]{:S(2)}) collective-permute-start(bf16[4,64,512]{2,1,0:T(8,128)(2,1)S(1)} %pad_maximum_fusion.5.refs_0_.refs_12_), channel_id=1, source_target_pairs={{0,4},{2,6},{4,0},{6,2},{8,12},{10,14},{12,8},{14,10},{16,20},{18,... | collective-permute-start | bytes 786440 | tf_op jit(solution)/shard_map/ppermute | solution.py:78
  242.5 12.4 %collective-permute-start.40 = (bf16[4,64,512]{2,1,0:T(8,128)(2,1)S(1)}, bf16[4,64,512]{2,1,0:T(8,128)(2,1)S(1)}, u32[]{:S(2)}, u32[]{:S(2)}) collective-permute-start(bf16[4,64,512]{2,1,0:T(8,128)(2,1)S(1)} %pad_maximum_fusion.5.refs_0_.refs_12_), channel_id=1, source_target_pairs={{0,6},{2,4},{4,2},{6,0},{8,14},{10,12},{12,10},{14,8},{16,22},{18,... | collective-permute-start | bytes 786440 | tf_op jit(solution)/shard_map/ppermute | solution.py:78
  266.7 23.7 %collective-permute-start.41 = (f32[1024,768]{1,0:T(8,128)}, f32[1024,768]{1,0:T(8,128)}, u32[]{:S(2)}, u32[]{:S(2)}) collective-permute-start(f32[1024,768]{1,0:T(8,128)} %get-tuple-element.121), channel_id=1, source_target_pairs={{0,1},{1,0},{2,3},{3,2},{4,5},{5,4},{6,7},{7,6},{8,9},{9,8},{10,11... | collective-permute-start | bytes 9437192 | tf_op jit(solution)/shard_map/ppermute | solution.py:68
  277.7 63.2 %all-to-all-start = ((bf16[4,192,1536]{2,1,0:T(8,128)(2,1)}), bf16[4,192,1536]{2,1,0:T(8,128)(2,1)S(1)}, u32[]{:S(2)}, u32[]{:S(2)}) async-start(bf16[4,192,1536]{2,1,0:T(8,128)(2,1)} %bitcast.136), calls=%async_computation | async-start | bytes 4718592 | tf_op jit(solution)/shard_map/all_to_all | solution.py:124
  351.0 11.9 %collective-permute-start.47 = (bf16[768,1536]{1,0:T(8,128)(2,1)}, bf16[768,1536]{1,0:T(8,128)(2,1)}, u32[]{:S(2)}, u32[]{:S(2)}) collective-permute-start(bf16[768,1536]{1,0:T(8,128)(2,1)} %attention_gradients.2), channel_id=1, source_target_pairs={{0,1},{1,0},{2,3},{3,2},{4,5},{5,4},{6,7},{7,6},{8,9},{9,8},{10,11... | collective-permute-start | bytes 7077896 | tf_op jit(solution)/shard_map/ppermute | solution.py:68
  351.4 105.9 %collective-permute-start.54 = (f32[1024,768]{1,0:T(8,128)}, f32[1024,768]{1,0:T(8,128)S(1)}, u32[]{:S(2)}, u32[]{:S(2)}) collective-permute-start(f32[1024,768]{1,0:T(8,128)} %get-tuple-element.158), channel_id=1, source_target_pairs={{0,1},{1,0},{2,3},{3,2},{4,5},{5,4},{6,7},{7,6},{8,9},{9,8},{10,11... | collective-permute-start | bytes 9437192 | tf_op jit(solution)/shard_map/ppermute | solution.py:68
  351.5 6.4 %collective-permute-start.44 = (bf16[32,768]{1,0:T(8,128)(2,1)S(1)}, bf16[32,768]{1,0:T(8,128)(2,1)S(1)}, u32[]{:S(2)}, u32[]{:S(2)}) collective-permute-start(bf16[32,768]{1,0:T(8,128)(2,1)S(1)} %copy-done.20), channel_id=1, source_target_pairs={{0,8},{2,10},{4,12},{6,14},{8,16},{10,18},{12,20},{14,22},{16,24},... | collective-permute-start | bytes 147464 | tf_op jit(solution)/shard_map/ppermute | solution.py:81
  353.2 6.4 %collective-permute-start.45 = (bf16[32,768]{1,0:T(8,128)(2,1)S(1)}, bf16[32,768]{1,0:T(8,128)(2,1)S(1)}, u32[]{:S(2)}, u32[]{:S(2)}) collective-permute-start(bf16[32,768]{1,0:T(8,128)(2,1)S(1)} %copy-done.20), channel_id=1, source_target_pairs={{0,16},{2,18},{4,20},{6,22},{8,24},{10,26},{12,28},{14,30},{16,0},... | collective-permute-start | bytes 147464 | tf_op jit(solution)/shard_map/ppermute | solution.py:81
  353.8 5.8 %collective-permute-start.46 = (bf16[32,768]{1,0:T(8,128)(2,1)S(1)}, bf16[32,768]{1,0:T(8,128)(2,1)S(1)}, u32[]{:S(2)}, u32[]{:S(2)}) collective-permute-start(bf16[32,768]{1,0:T(8,128)(2,1)S(1)} %copy-done.20), channel_id=1, source_target_pairs={{0,24},{2,26},{4,28},{6,30},{8,0},{10,2},{12,4},{14,6},{16,8},{18,... | collective-permute-start | bytes 147464 | tf_op jit(solution)/shard_map/ppermute | solution.py:81
  358.0 15.0 %collective-permute-start.42 = (f32[32,768]{1,0:T(8,128)S(1)}, f32[32,768]{1,0:T(8,128)S(1)}, u32[]{:S(2)}, u32[]{:S(2)}) collective-permute-start(f32[32,768]{1,0:T(8,128)S(1)} %copy-done.31), channel_id=1, source_target_pairs={{0,1},{1,0},{2,3},{3,2},{4,5},{5,4},{6,7},{7,6},{8,9},{9,8},{10,11... | collective-permute-start | bytes 294920 | tf_op jit(solution)/shard_map/ppermute | solution.py:68
  359.7 14.2 %collective-permute-start.51 = (bf16[4,32,768]{2,1,0:T(8,128)(2,1)S(1)}, bf16[4,32,768]{2,1,0:T(8,128)(2,1)S(1)}, u32[]{:S(2)}, u32[]{:S(2)}) collective-permute-start(bf16[4,32,768]{2,1,0:T(8,128)(2,1)S(1)} %pad_maximum_fusion.6.refs_0_.refs_5_), channel_id=1, source_target_pairs={{0,2},{2,0},{4,6},{6,4},{8,10},{10,8},{12,14},{14,12},{16,18},{18,... | collective-permute-start | bytes 589832 | tf_op jit(solution)/shard_map/ppermute | solution.py:78
  361.4 14.5 %collective-permute-start.52 = (bf16[4,32,768]{2,1,0:T(8,128)(2,1)S(1)}, bf16[4,32,768]{2,1,0:T(8,128)(2,1)S(1)}, u32[]{:S(2)}, u32[]{:S(2)}) collective-permute-start(bf16[4,32,768]{2,1,0:T(8,128)(2,1)S(1)} %pad_maximum_fusion.6.refs_0_.refs_5_), channel_id=1, source_target_pairs={{0,4},{2,6},{4,0},{6,2},{8,12},{10,14},{12,8},{14,10},{16,20},{18,... | collective-permute-start | bytes 589832 | tf_op jit(solution)/shard_map/ppermute | solution.py:78
  372.4 57.8 %collective-permute-start.48 = (bf16[192,1536]{1,0:T(8,128)(2,1)}, bf16[192,1536]{1,0:T(8,128)(2,1)}, u32[]{:S(2)}, u32[]{:S(2)}) collective-permute-start(bf16[192,1536]{1,0:T(8,128)(2,1)} %get-tuple-element.146), channel_id=1, source_target_pairs={{0,2},{2,0},{4,6},{6,4},{8,10},{10,8},{12,14},{14,12},{16,18},{18,... | collective-permute-start | bytes 1769480 | tf_op jit(solution)/shard_map/ppermute | solution.py:78
  373.0 57.3 %collective-permute-start.49 = (bf16[192,1536]{1,0:T(8,128)(2,1)}, bf16[192,1536]{1,0:T(8,128)(2,1)}, u32[]{:S(2)}, u32[]{:S(2)}) collective-permute-start(bf16[192,1536]{1,0:T(8,128)(2,1)} %get-tuple-element.147), channel_id=1, source_target_pairs={{0,4},{2,6},{4,0},{6,2},{8,12},{10,14},{12,8},{14,10},{16,20},{18,... | collective-permute-start | bytes 1769480 | tf_op jit(solution)/shard_map/ppermute | solution.py:78
  373.8 56.5 %collective-permute-start.50 = (bf16[192,1536]{1,0:T(8,128)(2,1)}, bf16[192,1536]{1,0:T(8,128)(2,1)}, u32[]{:S(2)}, u32[]{:S(2)}) collective-permute-start(bf16[192,1536]{1,0:T(8,128)(2,1)} %get-tuple-element.148), channel_id=1, source_target_pairs={{0,6},{2,4},{4,2},{6,0},{8,14},{10,12},{12,10},{14,8},{16,22},{18,... | collective-permute-start | bytes 1769480 | tf_op jit(solution)/shard_map/ppermute | solution.py:78
  375.9 30.7 %collective-permute-start.53 = (bf16[4,32,768]{2,1,0:T(8,128)(2,1)}, bf16[4,32,768]{2,1,0:T(8,128)(2,1)S(1)}, u32[]{:S(2)}, u32[]{:S(2)}) collective-permute-start(bf16[4,32,768]{2,1,0:T(8,128)(2,1)} %copy-done.6), channel_id=1, source_target_pairs={{0,6},{2,4},{4,2},{6,0},{8,14},{10,12},{12,10},{14,8},{16,22},{18,... | collective-permute-start | bytes 589832 | tf_op jit(solution)/shard_map/ppermute | solution.py:78
  406.6 10.7 %collective-permute-start.55 = (f32[32,768]{1,0:T(8,128)S(1)}, f32[32,768]{1,0:T(8,128)S(1)}, u32[]{:S(2)}, u32[]{:S(2)}) collective-permute-start(f32[32,768]{1,0:T(8,128)S(1)} %copy-done.32), channel_id=1, source_target_pairs={{0,1},{1,0},{2,3},{3,2},{4,5},{5,4},{6,7},{7,6},{8,9},{9,8},{10,11... | collective-permute-start | bytes 294920 | tf_op jit(solution)/shard_map/ppermute | solution.py:68
  413.4 11.3 %all-to-all-start.1 = ((f32[16,1,192]{2,1,0:T(1,128)}), f32[16,1,192]{2,1,0:T(1,128)S(1)}, u32[]{:S(2)}, u32[]{:S(2)}) async-start(f32[16,1,192]{2,1,0:T(1,128)} %reshape.347), calls=%async_computation.1 | async-start | bytes 32768 | tf_op jit(solution)/shard_map/all_to_all | solution.py:1384
  418.0 47.5 %collective-permute-start.57 = (f32[56,4608]{1,0:T(8,128)}, f32[56,4608]{1,0:T(8,128)}, u32[]{:S(2)}, u32[]{:S(2)}) collective-permute-start(f32[56,4608]{1,0:T(8,128)} %get-tuple-element.153), channel_id=1, source_target_pairs={{0,1},{1,0},{2,3},{3,2},{4,5},{5,4},{6,7},{7,6},{8,9},{9,8},{10,11... | collective-permute-start | bytes 3096584 | tf_op jit(solution)/shard_map/ppermute | solution.py:68
  424.7 38.3 %all-to-all-start.2 = ((bf16[4,48,1536]{2,1,0:T(8,128)(2,1)}), bf16[4,48,1536]{2,1,0:T(8,128)(2,1)}, u32[]{:S(2)}, u32[]{:S(2)}) async-start(bf16[4,48,1536]{2,1,0:T(8,128)(2,1)} %bitcast.82.refs_1_), calls=%async_computation.2 | async-start | bytes 1179648 | tf_op jit(solution)/shard_map/all_to_all | solution.py:139
  430.2 6.2 %collective-permute-start.56 = (f32[4,768]{1,0:T(4,128)S(1)}, f32[4,768]{1,0:T(4,128)S(1)}, u32[]{:S(2)}, u32[]{:S(2)}) collective-permute-start(f32[4,768]{1,0:T(4,128)S(1)} %reshape.342), channel_id=1, source_target_pairs={{0,1},{1,0},{2,3},{3,2},{4,5},{5,4},{6,7},{7,6},{8,9},{9,8},{10,11... | collective-permute-start | bytes 36872 | tf_op jit(solution)/shard_map/ppermute | solution.py:68
  432.1 15.0 %collective-permute-start.58 = (bf16[48,1536]{1,0:T(8,128)(2,1)S(1)}, bf16[48,1536]{1,0:T(8,128)(2,1)S(1)}, u32[]{:S(2)}, u32[]{:S(2)}) collective-permute-start(bf16[48,1536]{1,0:T(8,128)(2,1)S(1)} %get-tuple-element.204), channel_id=1, source_target_pairs={{0,8},{2,10},{4,12},{6,14},{8,16},{10,18},{12,20},{14,22},{16,24},... | collective-permute-start | bytes 442376 | tf_op jit(solution)/shard_map/ppermute | solution.py:81
  434.1 20.6 %collective-permute-start.59 = (bf16[48,1536]{1,0:T(8,128)(2,1)S(1)}, bf16[48,1536]{1,0:T(8,128)(2,1)S(1)}, u32[]{:S(2)}, u32[]{:S(2)}) collective-permute-start(bf16[48,1536]{1,0:T(8,128)(2,1)S(1)} %get-tuple-element.205), channel_id=1, source_target_pairs={{0,16},{2,18},{4,20},{6,22},{8,24},{10,26},{12,28},{14,30},{16,0},... | collective-permute-start | bytes 442376 | tf_op jit(solution)/shard_map/ppermute | solution.py:81
  436.5 18.2 %collective-permute-start.60 = (bf16[48,1536]{1,0:T(8,128)(2,1)S(1)}, bf16[48,1536]{1,0:T(8,128)(2,1)S(1)}, u32[]{:S(2)}, u32[]{:S(2)}) collective-permute-start(bf16[48,1536]{1,0:T(8,128)(2,1)S(1)} %get-tuple-element.206.refs_1_), channel_id=1, source_target_pairs={{0,24},{2,26},{4,28},{6,30},{8,0},{10,2},{12,4},{14,6},{16,8},{18,... | collective-permute-start | bytes 442376 | tf_op jit(solution)/shard_map/ppermute | solution.py:81
  (49 other events, 479.1 us)
Sparse Core Ops, SparseCore 0:
  10.9 119.6 all-gather.1
  266.8 149.2 reduce-scatter.1
